TPU v7x, 256 devices: a whole 4x4x8 slice. The times are simulated.
256 devices in a mesh: row: 64 (over z, y, core), col: 4 (over x).
Axes of the slice: x: 4, y: 4, z: 8, core: 2. Of those that a mesh axis runs over, the one named last changes fastest.
Arguments:
- source: bfloat16 [16384, 256], P('row'), may hold values from -6 to 6
- target: bfloat16 [16384, 256], P('col'), may hold values from -6 to 6
Outputs:
- row_potential: float32 [16384], P('row')
- column_potential: float32 [16384], P('col')
All inputs are finite; a program needn't handle non-finite values.
Results may differ from a plain program's by a relative error of at most 0.0003.
Values sent between devices are 32-bit elements; how exact they have to be, the bound alone decides.
No kernel may reach another device: no remote copies, remote signals or barrier semaphores. Data moves between devices by JAX's collectives and lax.ppermute only.
A program may use at most 64 MiB of HBM per device.

v0:
```python
import math

import jax
import jax.numpy as jnp
from jax import lax
from jax.sharding import PartitionSpec as P

ITERS = 4


epsilon = 0.1


def local(source, target):
    rows_here = source.shape[0]
    cols_here = target.shape[0]
    width = source.shape[1]
    total_rows = rows_here * lax.axis_size("row")
    total_cols = cols_here * lax.axis_size("col")
    scale = 1.0 / math.sqrt(width)

    def cost_tile():
        return -jnp.einsum("rw,cw->rc", source, target, preferred_element_type=jnp.float32) * scale

    column_potential = jnp.zeros((cols_here,), jnp.float32)
    row_potential = jnp.zeros((rows_here,), jnp.float32)
    for step in range(ITERS):
        cost = cost_tile()
        scores = (column_potential[None, :] - cost) / epsilon
        local_peak = jnp.max(scores, axis=1)
        peak = lax.pmax(local_peak, "col")
        total = lax.psum(jnp.sum(jnp.exp(scores - peak[:, None]), axis=1), "col")
        row_potential = epsilon * math.log(total_cols) - epsilon * (peak + jnp.log(total))
        cost = cost_tile()
        scores = (row_potential[:, None] - cost) / epsilon
        local_peak = jnp.max(scores, axis=0)
        peak = lax.pmax(local_peak, "row")
        total = lax.psum(jnp.sum(jnp.exp(scores - peak[None, :]), axis=0), "row")
        column_potential = epsilon * math.log(total_rows) - epsilon * (peak + jnp.log(total))
    return (row_potential, column_potential)


def solution(mesh):
    return jax.shard_map(
        local,
        mesh=mesh,
        in_specs=(P("row", None), P("col", None)),
        out_specs=(P("row"), P("col")),
        check_vma=False,
    )
```

profile of v0, /device:TPU:1, one launch (start us, length us, event | category | flops | bytes accessed | tf_op | source)
XLA Modules:
  0.0 2090.4 jit_solution(2755994335630552689)
XLA Ops:
  0.6 0.0 copy-start
  0.6 1.6 copy-done
  2.2 3.6 fusion.1
  5.8 9.3 pmax.56
  15.1 3.1 exponential_reduce_fusion.7
  18.2 6.0 psum.56
  24.2 2.8 fusion.2
  27.0 248.9 %pmax.57 = f32[4096]{0:T(1024)S(1)} all-reduce(f32[4096]{0:T(1024)S(1)} %fusion.2), channel_id=1, replica_groups=mesh['row'=64,'col'=4] {'row'}, use_global_device_ids=true, to_apply=%region_5.0 | all-reduce | flops 4096 | bytes 32768 | tf_op jit(solution)/shard_map/pmax | solution.py:37
  275.9 3.1 exponential_reduce_fusion.6
  279.0 246.1 %psum.57 = f32[4096]{0:T(1024)S(1)} all-reduce(f32[4096]{0:T(1024)S(1)} %exponential_reduce_fusion.6), channel_id=1, replica_groups=mesh['row'=64,'col'=4] {'row'}, use_global_device_ids=true, to_apply=%region_7.0 | all-reduce | flops 4096 | bytes 32768 | tf_op jit(solution)/shard_map/psum | solution.py:38
  525.1 2.7 fusion.3
  527.8 7.7 pmax.58
  535.6 3.1 exponential_reduce_fusion.5
  538.7 6.0 psum.58
  544.7 2.8 fusion.4
  547.5 249.9 %pmax.59 = f32[4096]{0:T(1024)S(1)} all-reduce(f32[4096]{0:T(1024)S(1)} %fusion.4), channel_id=1, replica_groups=mesh['row'=64,'col'=4] {'row'}, use_global_device_ids=true, to_apply=%region_13.0 | all-reduce | flops 4096 | bytes 32768 | tf_op jit(solution)/shard_map/pmax | solution.py:37
  797.4 3.1 exponential_reduce_fusion.4
  800.5 246.1 %psum.59 = f32[4096]{0:T(1024)S(1)} all-reduce(f32[4096]{0:T(1024)S(1)} %exponential_reduce_fusion.4), channel_id=1, replica_groups=mesh['row'=64,'col'=4] {'row'}, use_global_device_ids=true, to_apply=%region_15.0 | all-reduce | flops 4096 | bytes 32768 | tf_op jit(solution)/shard_map/psum | solution.py:38
  1046.6 2.7 fusion.5
  1049.3 7.7 pmax.60
  1057.0 3.1 exponential_reduce_fusion.3
  1060.2 6.0 psum.60
  1066.2 2.8 fusion.6
  1069.0 249.9 %pmax.61 = f32[4096]{0:T(1024)S(1)} all-reduce(f32[4096]{0:T(1024)S(1)} %fusion.6), channel_id=1, replica_groups=mesh['row'=64,'col'=4] {'row'}, use_global_device_ids=true, to_apply=%region_21.0 | all-reduce | flops 4096 | bytes 32768 | tf_op jit(solution)/shard_map/pmax | solution.py:37
  1318.9 3.1 exponential_reduce_fusion.2
  1322.0 246.3 %psum.61 = f32[4096]{0:T(1024)S(1)} all-reduce(f32[4096]{0:T(1024)S(1)} %exponential_reduce_fusion.2), channel_id=1, replica_groups=mesh['row'=64,'col'=4] {'row'}, use_global_device_ids=true, to_apply=%region_23.0 | all-reduce | flops 4096 | bytes 32768 | tf_op jit(solution)/shard_map/psum | solution.py:38
  1568.3 2.7 fusion.7
  1571.0 7.7 pmax.62
  1578.7 3.1 exponential_reduce_fusion.1
  1581.8 6.0 psum.62
  1587.8 0.0 copy-start.1
  1587.8 2.8 fusion.8
  1590.6 249.9 %pmax.63 = f32[4096]{0:T(1024)S(1)} all-reduce(f32[4096]{0:T(1024)S(1)} %fusion.8), channel_id=1, replica_groups=mesh['row'=64,'col'=4] {'row'}, use_global_device_ids=true, to_apply=%region_29.0 | all-reduce | flops 4096 | bytes 32768 | tf_op jit(solution)/shard_map/pmax | solution.py:37
  1840.5 3.1 exponential_reduce_fusion
  1843.6 0.0 copy-done.1
  1843.6 246.1 %psum.63 = f32[4096]{0:T(1024)S(1)} all-reduce(f32[4096]{0:T(1024)S(1)} %exponential_reduce_fusion), channel_id=1, replica_groups=mesh['row'=64,'col'=4] {'row'}, use_global_device_ids=true, to_apply=%region_31.0 | all-reduce | flops 4096 | bytes 32768 | tf_op jit(solution)/shard_map/psum | solution.py:38
  2089.8 0.6 multiply_subtract_fusion
  (7 shorter events, 0.1 us)
Async XLA Ops:
  0.6 1.6 copy-start
  1587.8 255.8 %copy-start.1 = (f32[256]{0:T(256)}, f32[256]{0:T(256)S(1)}, u32[]{:S(2)}) copy-start(f32[256]{0:T(256)S(1)} %multiply_subtract_fusion.4) | copy-start | bytes 3076
where the time goes:
time: 2100 us; the launch traced here: 2090 us
  blocking collectives  2040 us (97%)
  other arithmetic  44.7 us (2%)
    pmax x4, blocking collectives, local(): peak = lax.pmax(local_peak, 'row')  999 us
    psum x4, blocking collectives, local(): total = lax.psum(jnp.sum(jnp.exp(scores - peak[None, :]), axis=0), 'row')  985 us

commit v1 on v0

v1 whole, which is shorter than its diff:
```python
import math

import jax
import jax.numpy as jnp
from jax import lax
from jax.experimental import pallas as pl
from jax.experimental.pallas import tpu as pltpu
from jax.sharding import Mesh, PartitionSpec as P

ITERS = 4
EPSILON = 0.1
TILE = 256
LANES = 128

PLANE = ("z", "y")
LINE = ("core", "x")


def combine(parts):
    peak = jnp.max(parts, axis=0, keepdims=True)
    return peak + jnp.log2(jnp.sum(jnp.exp2(parts - peak), axis=0, keepdims=True))


def row_half(scale, bits, source_ref, target_ref, *refs):
    if len(refs) == 4:
        gathered_ref, out_ref, scores, peaks = refs
        potential = bits - combine(gathered_ref[...])
    else:
        out_ref, scores, peaks = refs
        potential = None
    source = source_ref[...]
    rows, cols = source.shape[0], target_ref.shape[0]
    for start in range(0, cols, TILE):
        tile = slice(start, start + TILE)
        part = lax.dot_general(
            source, target_ref[tile, :], (((1,), (1,)), ((), ())), preferred_element_type=jnp.float32
        ) * scale
        if potential is not None:
            part = part + potential[:, tile]
        scores[:, tile] = part
        high = part[:, :LANES]
        for lane in range(LANES, TILE, LANES):
            high = jnp.maximum(high, part[:, lane : lane + LANES])
        peaks[...] = high if start == 0 else jnp.maximum(peaks[...], high)
    for start in range(0, rows, LANES):
        block = slice(start, start + LANES)
        peak = jnp.max(peaks[block, :], axis=1, keepdims=True)
        total = jnp.sum(jnp.exp2(scores[block, :] - peak), axis=1, keepdims=True)
        result = peak + jnp.log2(total)
        turned = jnp.broadcast_to(result, (LANES, LANES)).T
        out_ref[:, block] = jnp.broadcast_to(turned[:1], (out_ref.shape[0], LANES))


def column_half(scale, bits, source_ref, target_ref, gathered_ref, out_ref, row_ref):
    potential = bits - combine(gathered_ref[...])
    row_ref[...] = potential
    rows, cols = source_ref.shape[0], target_ref.shape[0]
    turned = jnp.concatenate(
        [
            jnp.broadcast_to(potential[:, start : start + LANES], (LANES, LANES)).T
            for start in range(0, rows, LANES)
        ],
        axis=0,
    )
    turned = jnp.concatenate([turned] * (TILE // LANES), axis=1)
    source = source_ref[...]
    for start in range(0, cols, TILE):
        tile = slice(start, start + TILE)
        part = lax.dot_general(
            source, target_ref[tile, :], (((1,), (1,)), ((), ())), preferred_element_type=jnp.float32
        ) * scale + turned
        peak = jnp.max(part, axis=0, keepdims=True)
        total = jnp.sum(jnp.exp2(part - peak), axis=0, keepdims=True)
        out_ref[:, tile] = jnp.broadcast_to(peak + jnp.log2(total), (out_ref.shape[0], TILE))


def widen(source_ref, out_ref):
    out_ref[...] = source_ref[...].astype(jnp.float32)


def gather(core_ref, mine_ref, other_ref, target_ref, source_out, target_out):
    core = core_ref[0]
    rows = mine_ref.shape[0]
    half = target_out.shape[0]
    mine = mine_ref[...]
    other = other_ref[...]
    source_out[:rows, :] = jnp.where(core == 0, mine, other).astype(jnp.bfloat16)
    source_out[rows:, :] = jnp.where(core == 0, other, mine).astype(jnp.bfloat16)
    target_out[...] = target_ref[pl.ds(pl.multiple_of(core * half, half), half), :]


def local(source, target):
    width = source.shape[1]
    plane = lax.axis_size(PLANE)
    line = lax.axis_size(LINE)
    rows = source.shape[0] * lax.axis_size("core")
    cols = target.shape[0] // lax.axis_size("core")
    row_bits = math.log2(rows * plane)
    col_bits = math.log2(cols * line)
    scale = math.log2(math.e) / (math.sqrt(width) * EPSILON)
    unit = EPSILON * math.log(2.0)
    limit = pltpu.CompilerParams(vmem_limit_bytes=40 * 2**20)
    core = lax.axis_index("core")
    vmem = pl.BlockSpec(memory_space=pltpu.VMEM)

    mine = pl.pallas_call(
        widen, out_shape=jax.ShapeDtypeStruct(source.shape, jnp.float32), name="widen"
    )(source)
    other = lax.ppermute(mine, "core", [(0, 1), (1, 0)])
    source, target = pl.pallas_call(
        gather,
        in_specs=[pl.BlockSpec(memory_space=pltpu.SMEM), vmem, vmem, vmem],
        out_specs=[vmem, vmem],
        out_shape=[
            jax.ShapeDtypeStruct((rows, width), jnp.bfloat16),
            jax.ShapeDtypeStruct((cols, width), jnp.bfloat16),
        ],
        name="gather",
    )(core.reshape(1), mine, other, target)

    def row_call(*gathered):
        return pl.pallas_call(
            lambda *refs: row_half(scale, row_bits, *refs),
            in_specs=[vmem] * (2 + len(gathered)),
            out_specs=vmem,
            out_shape=jax.ShapeDtypeStruct((line, rows), jnp.float32),
            scratch_shapes=[
                pltpu.VMEM((rows, cols), jnp.float32),
                pltpu.VMEM((rows, LANES), jnp.float32),
            ],
            compiler_params=limit,
            name="row_half",
        )(source, target, *gathered)

    def column_call(gathered):
        return pl.pallas_call(
            lambda *refs: column_half(scale, col_bits, *refs),
            in_specs=[vmem] * 3,
            out_specs=[vmem, vmem],
            out_shape=[
                jax.ShapeDtypeStruct((plane, cols), jnp.float32),
                jax.ShapeDtypeStruct((1, rows), jnp.float32),
            ],
            compiler_params=limit,
            name="column_half",
        )(source, target, gathered)

    columns = None
    for step in range(ITERS):
        parts = row_call() if columns is None else row_call(columns)
        gathered = lax.all_to_all(parts, LINE, 0, 0)
        parts, row_potential = column_call(gathered)
        columns = lax.all_to_all(parts, PLANE, 0, 0)
    column_potential = unit * (row_bits - combine(columns)[0])
    other = lax.ppermute(column_potential, "core", [(0, 1), (1, 0)])
    column_potential = jnp.where(
        core == 0,
        jnp.concatenate([column_potential, other]),
        jnp.concatenate([other, column_potential]),
    )
    own = rows // lax.axis_size("core")
    row_potential = lax.dynamic_slice(row_potential[0], (core * own,), (own,)) * unit
    return (row_potential, column_potential)


def solution(mesh):
    fine = Mesh(mesh.devices.reshape(8, 4, 2, 4), ("z", "y", "core", "x"))
    return jax.shard_map(
        local,
        mesh=fine,
        in_specs=(P(("z", "y", "core"), None), P("x", None)),
        out_specs=(P(("z", "y", "core")), P("x")),
        check_vma=False,
    )
```

time: 2100 us -> 137 us (0.07)
  blocking collectives: 2040 us -> 88.8 us
  other arithmetic: 44.7 us -> 1.47 us
    pmax x8 -> x0, blocking collectives: 1030 us -> none  [the longest x4 999 us: local(): peak = lax.pmax(local_peak, 'row')]
    psum x8 -> x0, blocking collectives: 1010 us -> none  [the longest x4 985 us: local(): total = lax.psum(jnp.sum(jnp.exp(scores - peak[None, :]), axis=0), 'row')]
    all_to_all x0 -> x7, blocking collectives: none -> 88.8 us  [the longest x3 52.4 us: local(): columns = lax.all_to_all(parts, PLANE, 0, 0)]
    reduce_sum x8 -> x1, other arithmetic: 24.9 us -> 0.13 us  [combine(): jnp.sum(jnp.exp2(parts - peak), axis=0, keepdims=True)]
  transfers between devices with their start and end apart: 0 -> 3, of which waited for: 0 -> 3; matrix products, arithmetic and copies ran while one was open for 0% -> 0% of each run, Pallas kernels for 0% -> 0%
where the time goes in v1:
time: 137 us; the launch traced here: 136 us
  blocking collectives  88.8 us (65%)
  Pallas kernels  17.4 us (13%)
  waiting for transfers between devices  13.4 us (10%)
  starting transfers between devices  9.31 us (7%)
  local copies, waits for them, and re-layouts  5.05 us (4%)
  other arithmetic  1.47 us (1%)
    all_to_all x3, blocking collectives, local(): columns = lax.all_to_all(parts, PLANE, 0, 0)  52.4 us
    all_to_all x4, blocking collectives, local(): gathered = lax.all_to_all(parts, LINE, 0, 0)  36.4 us
    all_to_all x1, waiting for transfers between devices, local(): columns = lax.all_to_all(parts, PLANE, 0, 0)  11.8 us
    pallas_call x4, Pallas kernels, column_call(): pl.pallas_call(lambda *refs: column_half(scale, col_bits, *refs), in_spec...  6.82 us
    pallas_call x4, Pallas kernels, row_call(): pl.pallas_call(lambda *refs: row_half(scale, row_bits, *refs), in_specs=[...  6 us
    all_to_all x1, starting transfers between devices, local(): columns = lax.all_to_all(parts, PLANE, 0, 0)  3.87 us
    ppermute x1, starting transfers between devices, local(): other = lax.ppermute(mine, 'core', [(0, 1), (1, 0)])  3.24 us
    unnamed x13, local copies, waits for them, and re-layouts  3.13 us
  transfers between devices with their start and end apart: 3, of which 3 were waited for; matrix products, arithmetic and copies ran while one was open for 0% of the time, Pallas kernels for 0%

profile of v1, /device:TPU:1, one launch (start us, length us, event | category | flops | bytes accessed | tf_op | source)
XLA Modules:
  0.0 136.2 jit_solution(15680492447692140736)
XLA Ops:
  0.6 1.6 %widen.1.mine_ref = f32[256,256]{1,0:T(8,128)} custom-call(bf16[256,256]{1,0:T(8,128)(2,1)} %source_ref.1), custom_call_target="tpu_custom_call" | custom-call | tf_op jit(solution)/shard_map/widen/pallas_call | solution.py:106
  2.3 3.2 %collective-permute-start = (f32[256,256]{1,0:T(8,128)}, f32[256,256]{1,0:T(8,128)S(1)}, u32[]{:S(2)}, u32[]{:S(2)}) collective-permute-start(f32[256,256]{1,0:T(8,128)} %widen.1.mine_ref), channel_id=1, source_target_pairs={{0,4},{4,0},{1,5},{5,1},{2,6},{6,2},{3,7},{7,3},{8,12},{12,8},{9,1... | collective-permute-start | bytes 786440 | tf_op jit(solution)/shard_map/ppermute | solution.py:109
  5.5 1.4 %collective-permute-done.other_ref = f32[256,256]{1,0:T(8,128)S(1)} collective-permute-done((f32[256,256]{1,0:T(8,128)}, f32[256,256]{1,0:T(8,128)S(1)}, u32[]{:S(2)}, u32[]{:S(2)}) %collective-permute-start) | collective-permute-done | bytes 262176 | tf_op jit(solution)/shard_map/ppermute | solution.py:109
  6.9 0.0 copy-start.2
  6.9 0.7 copy-done.2
  7.6 2.9 %gather.1 = (bf16[512,256]{1,0:T(8,128)(2,1)}, bf16[2048,256]{1,0:T(8,128)(2,1)}) custom-call(s32[1]{0:T(128)} %bitcast.core_ref, f32[256,256]{1,0:T(8,128)} %widen.1.mine_ref, f32[256,256]{1,0:T(8,128)} %copy-done.2, bf16[4096,256]{1,0:T(8,128)(2,1)} %target_ref.1), custom_call_target="tpu_custom_call" | custom-call | tf_op jit(solution)/shard_map/gather/pallas_call | solution.py:110
  10.5 0.0 copy-start
  10.5 1.2 copy-done
  11.7 0.0 copy-start.1
  11.7 0.9 copy-done.1
  12.7 1.5 %row_half.4 = f32[8,512]{1,0:T(8,128)S(1)} custom-call(bf16[512,256]{1,0:T(8,128)(2,1)S(1)} %copy-done.1, bf16[2048,256]{1,0:T(8,128)(2,1)S(1)} %copy-done), custom_call_target="tpu_custom_call" | custom-call | tf_op jit(solution)/shard_map/row_half/pallas_call | solution.py:122
  14.2 7.6 %all_to_all.89 = f32[8,1,512]{2,1,0:T(1,128)S(1)} all-to-all(f32[8,1,512]{2,1,0:T(1,128)S(1)} %copy.4), channel_id=1, replica_groups=mesh['z'=8,'y'=4,'core'=2,'x'=4] {'core','x'}, dimensions={0} | all-to-all | bytes 32768 | tf_op jit(solution)/shard_map/all_to_all | solution.py:151
  21.9 1.8 %column_half.4 = (f32[32,2048]{1,0:T(8,128)S(1)}, f32[1,512]{1,0:T(1,128)}) custom-call(bf16[512,256]{1,0:T(8,128)(2,1)S(1)} %copy-done.1, bf16[2048,256]{1,0:T(8,128)(2,1)S(1)} %copy-done, f32[8,512]{1,0:T(8,128)S(1)} %bitcast.50), custom_call_target="tpu_custom_call" | custom-call | tf_op jit(solution)/shard_map/column_half/pallas_call | solution.py:136
  23.7 0.3 copy.5
  24.0 22.6 %all_to_all.90 = f32[32,1,2048]{2,1,0:T(1,128)S(1)} all-to-all(f32[32,1,2048]{2,1,0:T(1,128)S(1)} %copy.5), channel_id=1, replica_groups=mesh['z'=8,'y'=4,'core'=2,'x'=4] {'z','y'}, dimensions={0} | all-to-all | bytes 524288 | tf_op jit(solution)/shard_map/all_to_all | solution.py:153
  46.6 0.1 copy.30
  46.6 1.5 %row_half.5 = f32[8,512]{1,0:T(8,128)S(1)} custom-call(bf16[512,256]{1,0:T(8,128)(2,1)S(1)} %copy-done.1, bf16[2048,256]{1,0:T(8,128)(2,1)S(1)} %copy-done, f32[32,2048]{1,0:T(8,128)S(1)} %bitcast.39), custom_call_target="tpu_custom_call" | custom-call | tf_op jit(solution)/shard_map/row_half/pallas_call | solution.py:122
  48.2 9.6 %all_to_all.91 = f32[8,1,512]{2,1,0:T(1,128)S(1)} all-to-all(f32[8,1,512]{2,1,0:T(1,128)S(1)} %copy.6), channel_id=1, replica_groups=mesh['z'=8,'y'=4,'core'=2,'x'=4] {'core','x'}, dimensions={0} | all-to-all | bytes 32768 | tf_op jit(solution)/shard_map/all_to_all | solution.py:151
  57.8 1.8 %column_half.5 = (f32[32,2048]{1,0:T(8,128)S(1)}, f32[1,512]{1,0:T(1,128)}) custom-call(bf16[512,256]{1,0:T(8,128)(2,1)S(1)} %copy-done.1, bf16[2048,256]{1,0:T(8,128)(2,1)S(1)} %copy-done, f32[8,512]{1,0:T(8,128)S(1)} %bitcast.51), custom_call_target="tpu_custom_call" | custom-call | tf_op jit(solution)/shard_map/column_half/pallas_call | solution.py:136
  59.6 0.3 copy.7
  59.9 14.9 %all_to_all.92 = f32[32,1,2048]{2,1,0:T(1,128)S(1)} all-to-all(f32[32,1,2048]{2,1,0:T(1,128)S(1)} %copy.7), channel_id=1, replica_groups=mesh['z'=8,'y'=4,'core'=2,'x'=4] {'z','y'}, dimensions={0} | all-to-all | bytes 524288 | tf_op jit(solution)/shard_map/all_to_all | solution.py:153
  74.8 0.1 copy.29
  74.9 1.5 %row_half.6 = f32[8,512]{1,0:T(8,128)S(1)} custom-call(bf16[512,256]{1,0:T(8,128)(2,1)S(1)} %copy-done.1, bf16[2048,256]{1,0:T(8,128)(2,1)S(1)} %copy-done, f32[32,2048]{1,0:T(8,128)S(1)} %bitcast.40), custom_call_target="tpu_custom_call" | custom-call | tf_op jit(solution)/shard_map/row_half/pallas_call | solution.py:122
  76.4 9.6 %all_to_all.93 = f32[8,1,512]{2,1,0:T(1,128)S(1)} all-to-all(f32[8,1,512]{2,1,0:T(1,128)S(1)} %copy.8), channel_id=1, replica_groups=mesh['z'=8,'y'=4,'core'=2,'x'=4] {'core','x'}, dimensions={0} | all-to-all | bytes 32768 | tf_op jit(solution)/shard_map/all_to_all | solution.py:151
  86.0 1.8 %column_half.6 = (f32[32,2048]{1,0:T(8,128)S(1)}, f32[1,512]{1,0:T(1,128)}) custom-call(bf16[512,256]{1,0:T(8,128)(2,1)S(1)} %copy-done.1, bf16[2048,256]{1,0:T(8,128)(2,1)S(1)} %copy-done, f32[8,512]{1,0:T(8,128)S(1)} %bitcast.52), custom_call_target="tpu_custom_call" | custom-call | tf_op jit(solution)/shard_map/column_half/pallas_call | solution.py:136
  87.8 0.3 copy.9
  88.1 14.9 %all_to_all.94 = f32[32,1,2048]{2,1,0:T(1,128)S(1)} all-to-all(f32[32,1,2048]{2,1,0:T(1,128)S(1)} %copy.9), channel_id=1, replica_groups=mesh['z'=8,'y'=4,'core'=2,'x'=4] {'z','y'}, dimensions={0} | all-to-all | bytes 524288 | tf_op jit(solution)/shard_map/all_to_all | solution.py:153
  103.0 0.1 copy.28
  103.1 1.5 %row_half.7 = f32[8,512]{1,0:T(8,128)S(1)} custom-call(bf16[512,256]{1,0:T(8,128)(2,1)S(1)} %copy-done.1, bf16[2048,256]{1,0:T(8,128)(2,1)S(1)} %copy-done, f32[32,2048]{1,0:T(8,128)S(1)} %bitcast.41), custom_call_target="tpu_custom_call" | custom-call | tf_op jit(solution)/shard_map/row_half/pallas_call | solution.py:122
  104.7 9.6 %all_to_all.95 = f32[8,1,512]{2,1,0:T(1,128)S(1)} all-to-all(f32[8,1,512]{2,1,0:T(1,128)S(1)} %copy.10), channel_id=1, replica_groups=mesh['z'=8,'y'=4,'core'=2,'x'=4] {'core','x'}, dimensions={0} | all-to-all | bytes 32768 | tf_op jit(solution)/shard_map/all_to_all | solution.py:151
  114.2 1.3 column_half.7
  115.6 1.0 copy.11
  116.5 3.9 %all-to-all-start.7 = ((f32[32,1,2048]{2,1,0:T(1,128)}), f32[32,1,2048]{2,1,0:T(1,128)S(1)}, u32[]{:S(2)}, u32[]{:S(2)}) async-start(f32[32,1,2048]{2,1,0:T(1,128)} %copy.11), calls=%async_computation.7 | async-start | bytes 524288 | tf_op jit(solution)/shard_map/all_to_all | solution.py:153
  120.4 11.8 %all-to-all-done.7 = f32[32,1,2048]{2,1,0:T(1,128)S(1)} async-done(((f32[32,1,2048]{2,1,0:T(1,128)}), f32[32,1,2048]{2,1,0:T(1,128)S(1)}, u32[]{:S(2)}, u32[]{:S(2)}) %all-to-all-start.7) | async-done | bytes 262176 | tf_op jit(solution)/shard_map/all_to_all | solution.py:153
  132.2 0.2 reduce_max.9
  132.4 0.1 fusion.2
  132.5 2.2 %collective-permute-start.1 = (f32[2048]{0:T(1024)S(1)}, f32[2048]{0:T(1024)S(1)}, u32[]{:S(2)}, u32[]{:S(2)}) collective-permute-start(f32[2048]{0:T(1024)S(1)} %subtract_multiply_fusion), channel_id=1, source_target_pairs={{0,4},{4,0},{1,5},{5,1},{2,6},{6,2},{3,7},{7,3},{8,12},{12,8},{9,1... | collective-permute-start | bytes 24584 | tf_op jit(solution)/shard_map/ppermute | solution.py:155
  134.7 0.6 dynamic-slice_multiply_fusion
  135.3 0.3 collective-permute-done.1
  135.5 0.6 maximum_select_fusion
  (9 shorter events, 0.1 us)
Async XLA Ops:
  2.3 4.6 %collective-permute-start = (f32[256,256]{1,0:T(8,128)}, f32[256,256]{1,0:T(8,128)S(1)}, u32[]{:S(2)}, u32[]{:S(2)}) collective-permute-start(f32[256,256]{1,0:T(8,128)} %widen.1.mine_ref), channel_id=1, source_target_pairs={{0,4},{4,0},{1,5},{5,1},{2,6},{6,2},{3,7},{7,3},{8,12},{12,8},{9,1... | collective-permute-start | bytes 786440 | tf_op jit(solution)/shard_map/ppermute | solution.py:109
  6.9 0.7 copy-start.2
  10.5 1.2 copy-start
  11.7 0.9 copy-start.1
  116.5 15.7 %all-to-all-start.7 = ((f32[32,1,2048]{2,1,0:T(1,128)}), f32[32,1,2048]{2,1,0:T(1,128)S(1)}, u32[]{:S(2)}, u32[]{:S(2)}) async-start(f32[32,1,2048]{2,1,0:T(1,128)} %copy.11), calls=%async_computation.7 | async-start | bytes 524288 | tf_op jit(solution)/shard_map/all_to_all | solution.py:153
  132.5 3.0 %collective-permute-start.1 = (f32[2048]{0:T(1024)S(1)}, f32[2048]{0:T(1024)S(1)}, u32[]{:S(2)}, u32[]{:S(2)}) collective-permute-start(f32[2048]{0:T(1024)S(1)} %subtract_multiply_fusion), channel_id=1, source_target_pairs={{0,4},{4,0},{1,5},{5,1},{2,6},{6,2},{3,7},{7,3},{8,12},{12,8},{9,1... | collective-permute-start | bytes 24584 | tf_op jit(solution)/shard_map/ppermute | solution.py:155

commit v2 on v0

v2 whole, which is shorter than its diff:
```python
import math

import jax
import jax.numpy as jnp
from jax import lax
from jax.experimental import pallas as pl
from jax.experimental.pallas import tpu as pltpu
from jax.sharding import Mesh, PartitionSpec as P

ITERS = 4
EPSILON = 0.1
TILE = 256
LANES = 128
SUBLANES = 8
CHUNKS = 4
SAFE = 2.0**-80

PLANE = ("z", "y")
LINE = ("core", "x")


def combine(parts):
    peak = jnp.max(parts, axis=0)
    return peak + jnp.log2(jnp.sum(jnp.exp2(parts - peak[None]), axis=0))


def largest(values):
    return jnp.max(jnp.max(values, axis=1, keepdims=True), axis=0, keepdims=True)


def smallest(values):
    return jnp.min(jnp.min(values, axis=1, keepdims=True), axis=0, keepdims=True)


def stand(values):
    return jnp.concatenate(
        [jnp.broadcast_to(values[k : k + 1], (LANES, LANES)).T for k in range(values.shape[0])], axis=0
    )


def spread(row, count):
    return jnp.concatenate([row] * count, axis=1)


def send(out_ref, values):
    for slot in range(out_ref.shape[0]):
        out_ref[slot] = values


def score(source, target, scale):
    return scale * lax.dot_general(
        source, target, (((1,), (1,)), ((), ())), preferred_element_type=jnp.float32
    )


def first_rows(scale, source_ref, target_ref, out_ref, wide_ref, target, scores, peaks, line, arrived):
    source = source_ref[...]
    rows, cols = source.shape[0], target.shape[0]
    chunk = cols // CHUNKS
    copies = []
    for k in range(CHUNKS):
        part = pl.ds(k * chunk, chunk)
        copies.append(pltpu.make_async_copy(target_ref.at[part], target.at[part], arrived.at[k]))
        copies[-1].start()
    wide_ref[...] = source.astype(jnp.float32)
    for start in range(0, cols, TILE):
        if start % chunk == 0:
            copies[start // chunk].wait()
        tile = slice(start, start + TILE)
        part = score(source, target[tile, :], scale)
        scores[:, tile] = part
        high = part[:, :LANES]
        for lane in range(LANES, TILE, LANES):
            high = jnp.maximum(high, part[:, lane : lane + LANES])
        peaks[...] = high if start == 0 else jnp.maximum(peaks[...], high)
    for k in range(rows // LANES):
        block = slice(k * LANES, (k + 1) * LANES)
        peak = jnp.max(peaks[block, :], axis=1, keepdims=True)
        total = jnp.sum(jnp.exp2(scores[block, :] - peak), axis=1, keepdims=True)
        line[k : k + 1, :] = jnp.broadcast_to(peak + jnp.log2(total), (LANES, LANES)).T[:1]
    send(out_ref, line[...])


def all_scores(scale, core_ref, mine_ref, other_ref, target_ref, scores_ref, source, target, arrived):
    core = core_ref[0]
    rows = mine_ref.shape[0]
    cols = target.shape[0]
    chunk = cols // CHUNKS
    copies = []
    for k in range(CHUNKS):
        copies.append(
            pltpu.make_async_copy(
                target_ref.at[pl.ds(pl.multiple_of(core * cols + k * chunk, chunk), chunk)],
                target.at[pl.ds(k * chunk, chunk)],
                arrived.at[k],
            )
        )
        copies[-1].start()
    mine = mine_ref[...].astype(jnp.float32)
    other = other_ref[...]
    source[:rows, :] = jnp.where(core == 0, mine, other).astype(jnp.bfloat16)
    source[rows:, :] = jnp.where(core == 0, other, mine).astype(jnp.bfloat16)
    for start in range(0, cols, TILE):
        if start % chunk == 0:
            copies[start // chunk].wait()
        tile = slice(start, start + TILE)
        scores_ref[:, tile] = score(source[...], target[tile, :], scale)


def column_sums(rows, width, get):
    total = lax.fori_loop(
        0,
        rows // SUBLANES,
        lambda k, total: total + get(pl.ds(pl.multiple_of(k * SUBLANES, SUBLANES), SUBLANES)),
        jnp.zeros((SUBLANES, width), jnp.float32),
        unroll=8,
    )
    return jnp.sum(total, axis=0, keepdims=True)


def fold(ref, row):
    for k in range(ref.shape[0]):
        ref[k : k + 1, :] = row[:, k * LANES : (k + 1) * LANES]
    return ref[...]


def exact_columns(get, rows, width, keep=None):
    high = lax.fori_loop(
        0,
        rows // SUBLANES,
        lambda k, high: jnp.maximum(high, get(pl.ds(pl.multiple_of(k * SUBLANES, SUBLANES), SUBLANES))),
        jnp.full((SUBLANES, width), -jnp.inf, jnp.float32),
        unroll=8,
    )
    peak = jnp.max(high, axis=0, keepdims=True)
    shift = jnp.broadcast_to(peak, (SUBLANES, width))

    def term(block):
        value = jnp.exp2(get(block) - shift)
        if keep is not None:
            keep[block, :] = value
        return value

    return peak, column_sums(rows, width, term)


def first_columns(bits, scores_ref, gathered_ref, out_ref, plan_ref, row_ref, peak_ref, standing, folded):
    rows, cols = scores_ref.shape
    cores = 2
    each = gathered_ref.shape[0] // cores
    parts = gathered_ref[...]
    potential = bits - jnp.concatenate([combine(parts[k * each : (k + 1) * each]) for k in range(cores)], axis=0)
    row_ref[...] = potential
    standing[...] = stand(potential)
    peak, total = exact_columns(
        lambda block: scores_ref[block, :] + spread(standing[block, :], cols // LANES), rows, cols, plan_ref
    )
    peak = fold(peak_ref, peak)
    send(out_ref, peak + jnp.log2(fold(folded, total)))


def later_rows(
    bits, gathered_ref, plan_ref, row_ref, peak_ref, scores_ref, out_ref, factor, totals, block_scores, arrived
):
    rows, cols = plan_ref.shape
    potential = bits - combine(gathered_ref[...])
    change = potential + peak_ref[...]
    shift = largest(change)
    factor[...] = jnp.exp2(change - shift)
    for k in range(rows // LANES):
        block = slice(k * LANES, (k + 1) * LANES)
        total = jnp.zeros((LANES, LANES), jnp.float32)
        for t in range(cols // LANES):
            total = total + plan_ref[block, t * LANES : (t + 1) * LANES] * factor[t : t + 1, :]
        totals[k : k + 1, :] = jnp.sum(total.T, axis=0, keepdims=True)
    total = totals[...]
    send(out_ref, shift - row_ref[...] + jnp.log2(total))

    @pl.when(jnp.logical_not(smallest(total)[0, 0] >= SAFE))
    def _():
        factor[...] = potential
        for k in range(rows // LANES):
            block = slice(k * LANES, (k + 1) * LANES)
            copy = pltpu.make_async_copy(scores_ref.at[pl.ds(k * LANES, LANES)], block_scores, arrived)
            copy.start()
            copy.wait()
            for t in range(cols // LANES):
                tile = slice(t * LANES, (t + 1) * LANES)
                block_scores[:, tile] = block_scores[:, tile] + factor[t : t + 1, :]
            peak = jnp.max(block_scores[...], axis=1, keepdims=True)
            total = jnp.sum(jnp.exp2(block_scores[...] - peak), axis=1, keepdims=True)
            totals[k : k + 1, :] = jnp.broadcast_to(peak + jnp.log2(total), (LANES, LANES)).T[:1]
        send(out_ref, totals[...])


def later_columns(
    bits,
    gathered_ref,
    plan_ref,
    row_ref,
    peak_ref,
    scores_ref,
    out_ref,
    potential_ref,
    standing,
    folded,
    all_scores_here,
    arrived,
):
    rows, cols = plan_ref.shape
    count = cols // LANES
    potential = bits - combine(gathered_ref[...])
    potential_ref[...] = potential
    change = potential - row_ref[...]
    shift = largest(change)
    standing[...] = stand(jnp.exp2(change - shift))
    total = fold(
        folded,
        column_sums(rows, cols, lambda block: plan_ref[block, :] * spread(standing[block, :], count)),
    )
    send(out_ref, peak_ref[...] + shift + jnp.log2(total))

    @pl.when(jnp.logical_not(smallest(total)[0, 0] >= SAFE))
    def _():
        copy = pltpu.make_async_copy(scores_ref, all_scores_here, arrived)
        copy.start()
        copy.wait()
        standing[...] = stand(potential_ref[...])
        peak, total = exact_columns(
            lambda block: all_scores_here[block, :] + spread(standing[block, :], count), rows, cols
        )
        peak = fold(folded, peak)
        send(out_ref, peak + jnp.log2(fold(folded, total)))


def local(source, target):
    f32 = jnp.float32
    own, width = source.shape
    plane = lax.axis_size(PLANE)
    line = lax.axis_size(LINE)
    cores = lax.axis_size("core")
    rows = own * cores
    cols = target.shape[0] // cores
    row_bits = math.log2(rows * plane)
    col_bits = math.log2(cols * line)
    scale = math.log2(math.e) / (math.sqrt(width) * EPSILON)
    unit = EPSILON * math.log(2.0)
    core = lax.axis_index("core")
    vmem = pl.BlockSpec(memory_space=pltpu.VMEM)
    smem = pl.BlockSpec(memory_space=pltpu.SMEM)
    anywhere = pl.BlockSpec(memory_space=pl.ANY)
    row_shape = (rows // LANES, LANES)
    col_shape = (cols // LANES, LANES)
    limit = pltpu.CompilerParams(vmem_limit_bytes=32 * 2**20)

    parts, mine = pl.pallas_call(
        lambda *refs: first_rows(scale, *refs),
        in_specs=[vmem, anywhere],
        out_specs=[vmem, vmem],
        out_shape=[
            jax.ShapeDtypeStruct((line, own // LANES, LANES), f32),
            jax.ShapeDtypeStruct((own, width), f32),
        ],
        scratch_shapes=[
            pltpu.VMEM(target.shape, target.dtype),
            pltpu.VMEM((own, target.shape[0]), f32),
            pltpu.VMEM((own, LANES), f32),
            pltpu.VMEM((own // LANES, LANES), f32),
            pltpu.SemaphoreType.DMA((CHUNKS,)),
        ],
        compiler_params=limit,
        name="first_rows",
    )(source, target)
    other = lax.ppermute(mine, "core", [(0, 1), (1, 0)])
    gathered = lax.all_to_all(parts, LINE, 0, 0)
    scores = pl.pallas_call(
        lambda *refs: all_scores(scale, *refs),
        in_specs=[smem, vmem, vmem, anywhere],
        out_specs=vmem,
        out_shape=jax.ShapeDtypeStruct((rows, cols), f32),
        scratch_shapes=[
            pltpu.VMEM((rows, width), source.dtype),
            pltpu.VMEM((cols, width), target.dtype),
            pltpu.SemaphoreType.DMA((CHUNKS,)),
        ],
        compiler_params=limit,
        name="all_scores",
    )(core.reshape(1), source, other, target)
    parts, plan, row_base, peaks = pl.pallas_call(
        lambda *refs: first_columns(col_bits, *refs),
        in_specs=[vmem, vmem],
        out_specs=[vmem] * 4,
        out_shape=[
            jax.ShapeDtypeStruct((plane,) + col_shape, f32),
            jax.ShapeDtypeStruct((rows, cols), f32),
            jax.ShapeDtypeStruct(row_shape, f32),
            jax.ShapeDtypeStruct(col_shape, f32),
        ],
        scratch_shapes=[pltpu.VMEM((rows, LANES), f32), pltpu.VMEM(col_shape, f32)],
        compiler_params=limit,
        name="first_columns",
    )(scores, gathered)
    columns = lax.all_to_all(parts, PLANE, 0, 0)

    for step in range(1, ITERS):
        parts = pl.pallas_call(
            lambda *refs: later_rows(row_bits, *refs),
            in_specs=[vmem] * 4 + [anywhere],
            out_specs=vmem,
            out_shape=jax.ShapeDtypeStruct((line,) + row_shape, f32),
            scratch_shapes=[
                pltpu.VMEM(col_shape, f32),
                pltpu.VMEM(row_shape, f32),
                pltpu.VMEM((LANES, cols), f32),
                pltpu.SemaphoreType.DMA,
            ],
            compiler_params=limit,
            name="later_rows",
        )(columns, plan, row_base, peaks, scores)
        gathered = lax.all_to_all(parts, LINE, 0, 0)
        parts, row_potential = pl.pallas_call(
            lambda *refs: later_columns(col_bits, *refs),
            in_specs=[vmem] * 4 + [anywhere],
            out_specs=[vmem] * 2,
            out_shape=[
                jax.ShapeDtypeStruct((plane,) + col_shape, f32),
                jax.ShapeDtypeStruct(row_shape, f32),
            ],
            scratch_shapes=[
                pltpu.VMEM((rows, LANES), f32),
                pltpu.VMEM(col_shape, f32),
                pltpu.VMEM((rows, cols), f32),
                pltpu.SemaphoreType.DMA,
            ],
            compiler_params=limit,
            name="later_columns",
        )(gathered, plan, row_base, peaks, scores)
        columns = lax.all_to_all(parts, PLANE, 0, 0)

    column_potential = (unit * (row_bits - combine(columns))).reshape(cols)
    other = lax.ppermute(column_potential, "core", [(0, 1), (1, 0)])
    column_potential = jnp.where(
        core == 0,
        jnp.concatenate([column_potential, other]),
        jnp.concatenate([other, column_potential]),
    )
    row_potential = lax.dynamic_slice(row_potential.reshape(rows), (core * own,), (own,)) * unit
    return (row_potential, column_potential)


def solution(mesh):
    fine = Mesh(mesh.devices.reshape(8, 4, 2, 4), ("z", "y", "core", "x"))
    return jax.shard_map(
        local,
        mesh=fine,
        in_specs=(P(("z", "y", "core"), None), P("x", None)),
        out_specs=(P(("z", "y", "core")), P("x")),
        check_vma=False,
    )
```

time: 2100 us -> 136 us (0.06)
  blocking collectives: 2040 us -> 82.4 us
  other arithmetic: 44.7 us -> 1.35 us
    pmax x8 -> x0, blocking collectives: 1030 us -> none  [the longest x4 999 us: local(): peak = lax.pmax(local_peak, 'row')]
    psum x8 -> x0, blocking collectives: 1010 us -> none  [the longest x4 985 us: local(): total = lax.psum(jnp.sum(jnp.exp(scores - peak[None, :]), axis=0), 'row')]
    all_to_all x0 -> x6, blocking collectives: none -> 82.4 us  [the longest x3 52.2 us: local(): columns = lax.all_to_all(parts, PLANE, 0, 0)]
    reduce_sum x8 -> x1, other arithmetic: 24.9 us -> 0.06 us  [combine(): return peak + jnp.log2(jnp.sum(jnp.exp2(parts - peak[None]), axis=0))]
  transfers between devices with their start and end apart: 0 -> 4, of which waited for: 0 -> 2; matrix products, arithmetic and copies ran while one was open for 0% -> 0% of each run, Pallas kernels for 0% -> 1%
where the time goes in v2:
time: 136 us; the launch traced here: 135 us
  blocking collectives  82.4 us (61%)
  Pallas kernels  16.9 us (12%)
  starting transfers between devices  12.7 us (9%)
  waiting for transfers between devices  12 us (9%)
  local copies, waits for them, and re-layouts  9.12 us (7%)
    all_to_all x3, blocking collectives, local(): columns = lax.all_to_all(parts, PLANE, 0, 0)  52.2 us
    all_to_all x3, blocking collectives, local(): gathered = lax.all_to_all(parts, LINE, 0, 0)  30.2 us
    all_to_all x1, waiting for transfers between devices, local(): columns = lax.all_to_all(parts, PLANE, 0, 0)  11.8 us
    unnamed x12, local copies, waits for them, and re-layouts  9.12 us
    pallas_call x3, Pallas kernels, local(): pl.pallas_call(lambda *refs: later_rows(row_bits, *refs), in_specs=[vmem]...  7.1 us
    pallas_call x3, Pallas kernels, local(): pl.pallas_call(lambda *refs: later_columns(col_bits, *refs), in_specs=[vm...  4.03 us
    all_to_all x1, starting transfers between devices, local(): columns = lax.all_to_all(parts, PLANE, 0, 0)  3.88 us
    ppermute x1, starting transfers between devices, local(): other = lax.ppermute(mine, 'core', [(0, 1), (1, 0)])  3.33 us
  transfers between devices with their start and end apart: 4, of which 2 were waited for; matrix products, arithmetic and copies ran while one was open for 0% of the time, Pallas kernels for 1%

profile of v2, /device:TPU:1, one launch (start us, length us, event | category | flops | bytes accessed | tf_op | source)
XLA Modules:
  0.0 135.2 jit_solution(6680847364173847119)
XLA Ops:
  0.6 0.0 copy-start.2
  0.6 1.6 %copy-done.2 = bf16[4096,256]{1,0:T(8,128)(2,1)S(1)} copy-done((bf16[4096,256]{1,0:T(8,128)(2,1)S(1)}, bf16[4096,256]{1,0:T(8,128)(2,1)}, u32[]{:S(2)}) %copy-start.2) | copy-done | bytes 2097176
  2.2 0.0 copy-start.4
  2.2 0.9 copy-done.4
  3.1 2.9 %first_rows.1 = (f32[8,2,128]{2,1,0:T(2,128)}, f32[256,256]{1,0:T(8,128)S(1)}) custom-call(bf16[256,256]{1,0:T(8,128)(2,1)S(1)} %copy-done.4, bf16[4096,256]{1,0:T(8,128)(2,1)S(1)} %copy-done.2), custom_call_target="tpu_custom_call" | custom-call | tf_op jit(solution)/shard_map/first_rows/pallas_call | solution.py:256
  6.0 3.3 %collective-permute-start = (f32[256,256]{1,0:T(8,128)S(1)}, f32[256,256]{1,0:T(8,128)S(1)}, u32[]{:S(2)}, u32[]{:S(2)}) collective-permute-start(f32[256,256]{1,0:T(8,128)S(1)} %get-tuple-element.12), channel_id=1, source_target_pairs={{0,4},{4,0},{1,5},{5,1},{2,6},{6,2},{3,7},{7,3},{8,12},{12,8},{9,1... | collective-permute-start | bytes 786440 | tf_op jit(solution)/shard_map/ppermute | solution.py:274
  9.3 3.3 %all-to-all-start = ((f32[8,2,128]{2,1,0:T(2,128)}), f32[8,2,128]{2,1,0:T(2,128)S(1)}, u32[]{:S(2)}, u32[]{:S(2)}) async-start(f32[8,2,128]{2,1,0:T(2,128)} %get-tuple-element.13), calls=%async_computation | async-start | bytes 16384 | tf_op jit(solution)/shard_map/all_to_all | solution.py:275
  12.6 0.0 collective-permute-done.refs_2_
  12.6 0.0 copy-start.3
  12.6 1.6 %copy-done.3 = bf16[4096,256]{1,0:T(8,128)(2,1)S(1)} copy-done((bf16[4096,256]{1,0:T(8,128)(2,1)S(1)}, bf16[4096,256]{1,0:T(8,128)(2,1)}, u32[]{:S(2)}) %copy-start.3) | copy-done | bytes 2097176
  14.2 0.0 copy-start.5
  14.2 0.9 copy-done.5
  15.1 1.5 %all_scores.1.refs_0_.refs_4_ = f32[512,2048]{1,0:T(8,128)S(1)} custom-call(s32[1]{0:T(128)} %bitcast.refs_0_, bf16[256,256]{1,0:T(8,128)(2,1)S(1)} %copy-done.5, f32[256,256]{1,0:T(8,128)S(1)} %collective-permute-done.refs_2_, bf16[4096,256]{1,0:T(8,128)(2,1)S(1)} %copy-done.3), custom_call_target="tpu_custom_call" | custom-call | tf_op jit(solution)/shard_map/all_scores/pallas_call | solution.py:276
  16.6 0.0 copy-start
  16.6 1.9 %copy-done = f32[512,2048]{1,0:T(8,128)} copy-done((f32[512,2048]{1,0:T(8,128)}, f32[512,2048]{1,0:T(8,128)S(1)}, u32[]{:S(2)}) %copy-start) | copy-done | bytes 4194328
  18.6 0.0 all-to-all-done.refs_1_
  18.6 0.0 copy-start.1
  18.6 2.2 %copy-done.1 = f32[512,2048]{1,0:T(8,128)S(1)} copy-done((f32[512,2048]{1,0:T(8,128)S(1)}, f32[512,2048]{1,0:T(8,128)}, u32[]{:S(2)}) %copy-start.1) | copy-done | bytes 4194328
  20.8 1.4 %first_columns.1 = (f32[32,16,128]{2,1,0:T(8,128)S(1)}, f32[512,2048]{1,0:T(8,128)S(1)}, f32[4,128]{1,0:T(4,128)S(1)}, f32[16,128]{1,0:T(8,128)S(1)}) custom-call(f32[512,2048]{1,0:T(8,128)S(1)} %copy-done.1, f32[8,2,128]{2,1,0:T(2,128)S(1)} %all-to-all-done.refs_1_), custom_call_target="tpu_custom_call" | custom-call | tf_op jit(solution)/shard_map/first_columns/pallas_call | solution.py:289
  22.1 22.4 %all_to_all.40.refs_0_ = f32[32,16,128]{2,1,0:T(8,128)S(1)} all-to-all(f32[32,16,128]{2,1,0:T(8,128)S(1)} %get-tuple-element.14), channel_id=1, replica_groups=mesh['z'=8,'y'=4,'core'=2,'x'=4] {'z','y'}, dimensions={0} | all-to-all | bytes 524288 | tf_op jit(solution)/shard_map/all_to_all | solution.py:303
  44.5 2.4 %later_rows.3 = f32[8,4,128]{2,1,0:T(4,128)S(1)} custom-call(f32[32,16,128]{2,1,0:T(8,128)S(1)} %all_to_all.40.refs_0_, f32[512,2048]{1,0:T(8,128)S(1)} %get-tuple-element.15.refs_1_, f32[4,128]{1,0:T(4,128)S(1)} %get-tuple-element.16.refs_2_, f32[16,128]{1,0:T(8,128)S(1)} %get-tuple-element.17.refs_3_, f32[512,2048]{1,0:T(8,128)S(1)} %copy-done.1), custom_call_target="tpu_custom_call" | custom-call | tf_op jit(solution)/shard_map/later_rows/pallas_call | solution.py:306
  46.9 11.0 %all_to_all.41.refs_0_ = f32[8,4,128]{2,1,0:T(4,128)S(1)} all-to-all(f32[8,4,128]{2,1,0:T(4,128)S(1)} %later_rows.3), channel_id=1, replica_groups=mesh['z'=8,'y'=4,'core'=2,'x'=4] {'core','x'}, dimensions={0} | all-to-all | bytes 32768 | tf_op jit(solution)/shard_map/all_to_all | solution.py:320
  57.9 1.3 later_columns.3
  59.2 14.9 %all_to_all.42.refs_0_ = f32[32,16,128]{2,1,0:T(8,128)S(1)} all-to-all(f32[32,16,128]{2,1,0:T(8,128)S(1)} %get-tuple-element.18), channel_id=1, replica_groups=mesh['z'=8,'y'=4,'core'=2,'x'=4] {'z','y'}, dimensions={0} | all-to-all | bytes 524288 | tf_op jit(solution)/shard_map/all_to_all | solution.py:338
  74.2 2.4 %later_rows.4 = f32[8,4,128]{2,1,0:T(4,128)S(1)} custom-call(f32[32,16,128]{2,1,0:T(8,128)S(1)} %all_to_all.42.refs_0_, f32[512,2048]{1,0:T(8,128)S(1)} %get-tuple-element.15.refs_1_, f32[4,128]{1,0:T(4,128)S(1)} %get-tuple-element.16.refs_2_, f32[16,128]{1,0:T(8,128)S(1)} %get-tuple-element.17.refs_3_, f32[512,2048]{1,0:T(8,128)S(1)} %copy-done.1), custom_call_target="tpu_custom_call" | custom-call | tf_op jit(solution)/shard_map/later_rows/pallas_call | solution.py:306
  76.5 9.6 %all_to_all.43.refs_0_ = f32[8,4,128]{2,1,0:T(4,128)S(1)} all-to-all(f32[8,4,128]{2,1,0:T(4,128)S(1)} %later_rows.4), channel_id=1, replica_groups=mesh['z'=8,'y'=4,'core'=2,'x'=4] {'core','x'}, dimensions={0} | all-to-all | bytes 32768 | tf_op jit(solution)/shard_map/all_to_all | solution.py:320
  86.1 1.3 later_columns.4
  87.4 14.9 %all_to_all.44.refs_0_ = f32[32,16,128]{2,1,0:T(8,128)S(1)} all-to-all(f32[32,16,128]{2,1,0:T(8,128)S(1)} %get-tuple-element.19), channel_id=1, replica_groups=mesh['z'=8,'y'=4,'core'=2,'x'=4] {'z','y'}, dimensions={0} | all-to-all | bytes 524288 | tf_op jit(solution)/shard_map/all_to_all | solution.py:338
  102.4 2.4 %later_rows.5 = f32[8,4,128]{2,1,0:T(4,128)S(1)} custom-call(f32[32,16,128]{2,1,0:T(8,128)S(1)} %all_to_all.44.refs_0_, f32[512,2048]{1,0:T(8,128)S(1)} %get-tuple-element.15.refs_1_, f32[4,128]{1,0:T(4,128)S(1)} %get-tuple-element.16.refs_2_, f32[16,128]{1,0:T(8,128)S(1)} %get-tuple-element.17.refs_3_, f32[512,2048]{1,0:T(8,128)S(1)} %copy-done.1), custom_call_target="tpu_custom_call" | custom-call | tf_op jit(solution)/shard_map/later_rows/pallas_call | solution.py:306
  104.7 9.6 %all_to_all.45.refs_0_ = f32[8,4,128]{2,1,0:T(4,128)S(1)} all-to-all(f32[8,4,128]{2,1,0:T(4,128)S(1)} %later_rows.5), channel_id=1, replica_groups=mesh['z'=8,'y'=4,'core'=2,'x'=4] {'core','x'}, dimensions={0} | all-to-all | bytes 32768 | tf_op jit(solution)/shard_map/all_to_all | solution.py:320
  114.3 1.4 %later_columns.5 = (f32[32,16,128]{2,1,0:T(8,128)}, f32[4,128]{1,0:T(4,128)S(1)}) custom-call(f32[8,4,128]{2,1,0:T(4,128)S(1)} %all_to_all.45.refs_0_, f32[512,2048]{1,0:T(8,128)S(1)} %get-tuple-element.15.refs_1_, f32[4,128]{1,0:T(4,128)S(1)} %get-tuple-element.16.refs_2_, f32[16,128]{1,0:T(8,128)S(1)} %get-tuple-element.17.refs_3_, f32[512,2048]{1,0:T(8,128)S(1)} %copy-done.1), custom_call_target="tpu_custom_call" | custom-call | tf_op jit(solution)/shard_map/later_columns/pallas_call | solution.py:321
  115.7 3.9 %all-to-all-start.7 = ((f32[32,16,128]{2,1,0:T(8,128)}), f32[32,16,128]{2,1,0:T(8,128)S(1)}, u32[]{:S(2)}, u32[]{:S(2)}) async-start(f32[32,16,128]{2,1,0:T(8,128)} %get-tuple-element.21), calls=%async_computation.7 | async-start | bytes 524288 | tf_op jit(solution)/shard_map/all_to_all | solution.py:338
  119.6 11.8 %all-to-all-done.7 = f32[32,16,128]{2,1,0:T(8,128)S(1)} async-done(((f32[32,16,128]{2,1,0:T(8,128)}), f32[32,16,128]{2,1,0:T(8,128)S(1)}, u32[]{:S(2)}, u32[]{:S(2)}) %all-to-all-start.7) | async-done | bytes 262176 | tf_op jit(solution)/shard_map/all_to_all | solution.py:338
  131.5 0.1 exponential_reduce_fusion
  131.5 2.2 %collective-permute-start.1 = (f32[2048]{0:T(1024)S(1)}, f32[2048]{0:T(1024)S(1)}, u32[]{:S(2)}, u32[]{:S(2)}) collective-permute-start(f32[2048]{0:T(1024)S(1)} %multiply_bitcast_fusion), channel_id=1, source_target_pairs={{0,4},{4,0},{1,5},{5,1},{2,6},{6,2},{3,7},{7,3},{8,12},{12,8},{9,1... | collective-permute-start | bytes 24584 | tf_op jit(solution)/shard_map/ppermute | solution.py:341
  133.7 0.6 dynamic-slice_multiply_fusion
  134.4 0.2 collective-permute-done.1
  134.6 0.6 maximum_select_fusion
  (2 shorter events, 0.0 us)
Async XLA Ops:
  0.6 1.6 %copy-start.2 = (bf16[4096,256]{1,0:T(8,128)(2,1)S(1)}, bf16[4096,256]{1,0:T(8,128)(2,1)}, u32[]{:S(2)}) copy-start(bf16[4096,256]{1,0:T(8,128)(2,1)} %refs_3_.1) | copy-start | bytes 6291460
  2.2 0.9 copy-start.4
  6.0 6.6 %collective-permute-start = (f32[256,256]{1,0:T(8,128)S(1)}, f32[256,256]{1,0:T(8,128)S(1)}, u32[]{:S(2)}, u32[]{:S(2)}) collective-permute-start(f32[256,256]{1,0:T(8,128)S(1)} %get-tuple-element.12), channel_id=1, source_target_pairs={{0,4},{4,0},{1,5},{5,1},{2,6},{6,2},{3,7},{7,3},{8,12},{12,8},{9,1... | collective-permute-start | bytes 786440 | tf_op jit(solution)/shard_map/ppermute | solution.py:274
  9.3 9.3 %all-to-all-start = ((f32[8,2,128]{2,1,0:T(2,128)}), f32[8,2,128]{2,1,0:T(2,128)S(1)}, u32[]{:S(2)}, u32[]{:S(2)}) async-start(f32[8,2,128]{2,1,0:T(2,128)} %get-tuple-element.13), calls=%async_computation | async-start | bytes 16384 | tf_op jit(solution)/shard_map/all_to_all | solution.py:275
  12.6 1.6 %copy-start.3 = (bf16[4096,256]{1,0:T(8,128)(2,1)S(1)}, bf16[4096,256]{1,0:T(8,128)(2,1)}, u32[]{:S(2)}) copy-start(bf16[4096,256]{1,0:T(8,128)(2,1)} %refs_3_.1) | copy-start | bytes 6291460
  14.2 0.9 copy-start.5
  16.6 2.0 %copy-start = (f32[512,2048]{1,0:T(8,128)}, f32[512,2048]{1,0:T(8,128)S(1)}, u32[]{:S(2)}) copy-start(f32[512,2048]{1,0:T(8,128)S(1)} %all_scores.1.refs_0_.refs_4_) | copy-start | bytes 12582916
  18.6 2.2 %copy-start.1 = (f32[512,2048]{1,0:T(8,128)S(1)}, f32[512,2048]{1,0:T(8,128)}, u32[]{:S(2)}) copy-start(f32[512,2048]{1,0:T(8,128)} %copy-done) | copy-start | bytes 12582916
  115.7 15.7 %all-to-all-start.7 = ((f32[32,16,128]{2,1,0:T(8,128)}), f32[32,16,128]{2,1,0:T(8,128)S(1)}, u32[]{:S(2)}, u32[]{:S(2)}) async-start(f32[32,16,128]{2,1,0:T(8,128)} %get-tuple-element.21), calls=%async_computation.7 | async-start | bytes 524288 | tf_op jit(solution)/shard_map/all_to_all | solution.py:338
  131.5 3.0 %collective-permute-start.1 = (f32[2048]{0:T(1024)S(1)}, f32[2048]{0:T(1024)S(1)}, u32[]{:S(2)}, u32[]{:S(2)}) collective-permute-start(f32[2048]{0:T(1024)S(1)} %multiply_bitcast_fusion), channel_id=1, source_target_pairs={{0,4},{4,0},{1,5},{5,1},{2,6},{6,2},{3,7},{7,3},{8,12},{12,8},{9,1... | collective-permute-start | bytes 24584 | tf_op jit(solution)/shard_map/ppermute | solution.py:341

commit v3 on v2

v3 whole, which is shorter than its diff:
```python
import math

import jax
import jax.numpy as jnp
from jax import lax
from jax.experimental import pallas as pl
from jax.experimental.pallas import tpu as pltpu
from jax.sharding import Mesh, PartitionSpec as P

ITERS = 4
EPSILON = 0.1
TILE = 256
LANES = 128
SUBLANES = 8
CHUNKS = 2
SAFE = 2.0**-80

PLANE = ("z", "p", "q")
ALIKE = ()
LINE = ("core", "x")


def combine(parts):
    peak = jnp.max(parts, axis=0)
    return peak + jnp.log2(jnp.sum(jnp.exp2(parts - peak[None]), axis=0))


def largest(values):
    return jnp.max(jnp.max(values, axis=1, keepdims=True), axis=0, keepdims=True)


def smallest(values):
    return jnp.min(jnp.min(values, axis=1, keepdims=True), axis=0, keepdims=True)


def stand(ref, values):
    for k in range(values.shape[0]):
        ref[k * LANES : (k + 1) * LANES, :] = jnp.broadcast_to(values[k : k + 1], (LANES, LANES)).T


def fold(ref, row):
    for k in range(ref.shape[0]):
        ref[k : k + 1, :] = row[:, k * LANES : (k + 1) * LANES]
    return ref[...]


def spread(row, count):
    return jnp.concatenate([row] * count, axis=1)


def send(out_ref, values):
    for slot in range(out_ref.shape[0]):
        out_ref[slot] = values


def score(source, target, scale):
    return scale * lax.dot_general(
        source, target, (((1,), (1,)), ((), ())), preferred_element_type=jnp.float32
    )


def first_rows(
    scale, source_ref, target_ref, out_ref, wide_ref, half_ref, source, rest, scores, peaks, line, arrived
):
    core = lax.axis_index("core")
    rows, half = source.shape[0], half_ref.shape[0]
    chunk = half // CHUNKS
    fetch = pltpu.make_async_copy(source_ref, source, arrived.at[2 * CHUNKS])
    fetch.start()
    copies = []
    for side, place in ((core, half_ref), (1 - core, rest)):
        for k in range(CHUNKS):
            copies.append(
                pltpu.make_async_copy(
                    target_ref.at[pl.ds(pl.multiple_of(side * half + k * chunk, chunk), chunk)],
                    place.at[pl.ds(k * chunk, chunk)],
                    arrived.at[len(copies)],
                )
            )
            copies[-1].start()
    fetch.wait()
    wide_ref[...] = source[...].astype(jnp.float32)
    for start in range(0, 2 * half, TILE):
        if start % chunk == 0:
            copies[start // chunk].wait()
        place = half_ref if start < half else rest
        tile = slice(start, start + TILE)
        part = score(source[...], place[start % half : start % half + TILE, :], scale)
        scores[:, tile] = part
        high = part[:, :LANES]
        for lane in range(LANES, TILE, LANES):
            high = jnp.maximum(high, part[:, lane : lane + LANES])
        peaks[...] = high if start == 0 else jnp.maximum(peaks[...], high)
    for k in range(rows // LANES):
        block = slice(k * LANES, (k + 1) * LANES)
        peak = jnp.max(peaks[block, :], axis=1, keepdims=True)
        total = jnp.sum(jnp.exp2(scores[block, :] - peak), axis=1, keepdims=True)
        line[k : k + 1, :] = jnp.broadcast_to(peak + jnp.log2(total), (LANES, LANES)).T[:1]
    send(out_ref, line[...])


def column_sums(rows, width, get):
    total = lax.fori_loop(
        0,
        rows // SUBLANES,
        lambda k, total: total + get(pl.ds(pl.multiple_of(k * SUBLANES, SUBLANES), SUBLANES)),
        jnp.zeros((SUBLANES, width), jnp.float32),
        unroll=16,
    )
    return jnp.sum(total, axis=0, keepdims=True)


def first_columns(
    scale, bits, each, *refs
):
    pieces = refs[: 2 * (1 + len(ALIKE))]
    half_ref, gathered_ref, out_ref, plan_ref, row_ref, peak_ref, source_ref, standing, folded = refs[len(pieces) :]
    rows, cols = plan_ref.shape
    own = pieces[0].shape[0]
    core = lax.axis_index("core")
    group = lax.axis_index(ALIKE) if ALIKE else 0
    for index, piece in enumerate(pieces):
        here = (core + index % 2) % 2
        there = (group + index // 2) % 2 if ALIKE else 0
        start = pl.multiple_of((there * 2 + here) * own, own)
        source_ref[pl.ds(start, own), :] = piece[...].astype(source_ref.dtype)
    parts = gathered_ref[...]
    potential = bits - jnp.concatenate(
        [combine(parts[k : k + each]) for k in range(0, parts.shape[0], each)], axis=0
    )
    row_ref[...] = potential
    stand(standing, potential)
    highs = []
    for start in range(0, cols, TILE):
        tile = slice(start, start + TILE)
        part = score(source_ref[...], half_ref[tile, :], scale) + spread(standing[...], TILE // LANES)
        plan_ref[:, tile] = part
        highs.append(jnp.max(part, axis=0, keepdims=True))
    peak = jnp.concatenate(highs, axis=1)
    shift = jnp.broadcast_to(peak, (SUBLANES, cols))

    def term(block):
        value = jnp.exp2(plan_ref[block, :] - shift)
        plan_ref[block, :] = value
        return value

    total = column_sums(rows, cols, term)
    send(out_ref, fold(peak_ref, peak) + jnp.log2(fold(folded, total)))


def later_rows(
    scale, bits, gathered_ref, plan_ref, row_ref, peak_ref, source_ref, half_ref, out_ref, factor, totals
):
    rows, cols = plan_ref.shape
    potential = bits - combine(gathered_ref[...])
    change = potential + peak_ref[...]
    shift = largest(change)
    factor[...] = jnp.exp2(change - shift)
    for k in range(rows // LANES):
        block = slice(k * LANES, (k + 1) * LANES)
        total = jnp.zeros((LANES, LANES), jnp.float32)
        for t in range(cols // LANES):
            total = total + plan_ref[block, t * LANES : (t + 1) * LANES] * factor[t : t + 1, :]
        totals[k : k + 1, :] = jnp.sum(total.T, axis=0, keepdims=True)
    total = totals[...]
    send(out_ref, shift - row_ref[...] + jnp.log2(total))

    @pl.when(jnp.logical_not(smallest(total)[0, 0] >= SAFE))
    def _():
        wide = jnp.concatenate([potential[t : t + 1] for t in range(cols // LANES)], axis=1)
        for k in range(rows // LANES):
            block = slice(k * LANES, (k + 1) * LANES)
            part = score(source_ref[block, :], half_ref[...], scale) + wide
            peak = jnp.max(part, axis=1, keepdims=True)
            total = jnp.sum(jnp.exp2(part - peak), axis=1, keepdims=True)
            totals[k : k + 1, :] = jnp.broadcast_to(peak + jnp.log2(total), (LANES, LANES)).T[:1]
        send(out_ref, totals[...])


def later_columns(
    scale, bits, gathered_ref, plan_ref, row_ref, peak_ref, source_ref, half_ref, out_ref, potential_ref, standing, folded
):
    rows, cols = plan_ref.shape
    potential = bits - combine(gathered_ref[...])
    potential_ref[...] = potential
    change = potential - row_ref[...]
    shift = largest(change)
    stand(standing, jnp.exp2(change - shift))
    total = fold(
        folded,
        column_sums(rows, cols, lambda block: plan_ref[block, :] * spread(standing[block, :], cols // LANES)),
    )
    send(out_ref, peak_ref[...] + shift + jnp.log2(total))

    @pl.when(jnp.logical_not(smallest(total)[0, 0] >= SAFE))
    def _():
        stand(standing, potential_ref[...])
        for start in range(0, cols, TILE):
            part = score(source_ref[...], half_ref[start : start + TILE, :], scale) + spread(
                standing[...], TILE // LANES
            )
            peak = jnp.max(part, axis=0, keepdims=True)
            result = peak + jnp.log2(jnp.sum(jnp.exp2(part - peak), axis=0, keepdims=True))
            for lane in range(0, TILE, LANES):
                t = (start + lane) // LANES
                folded[t : t + 1, :] = result[:, lane : lane + LANES]
        send(out_ref, folded[...])


def local(source, target):
    f32 = jnp.float32
    own, width = source.shape
    plane = lax.axis_size(PLANE)
    line = lax.axis_size(LINE)
    cores = lax.axis_size("core")
    alike = lax.axis_size(ALIKE) if ALIKE else 1
    rows = own * cores * alike
    cols = target.shape[0] // cores
    row_bits = math.log2(rows * plane)
    col_bits = math.log2(cols * line)
    scale = math.log2(math.e) / (math.sqrt(width) * EPSILON)
    unit = EPSILON * math.log(2.0)
    core = lax.axis_index("core")
    swap = [(0, 1), (1, 0)]
    vmem = pl.BlockSpec(memory_space=pltpu.VMEM)
    hbm = pl.BlockSpec(memory_space=pltpu.HBM)
    row_shape = (rows // LANES, LANES)
    col_shape = (cols // LANES, LANES)
    limit = pltpu.CompilerParams(vmem_limit_bytes=32 * 2**20)

    parts, mine, half = pl.pallas_call(
        lambda *refs: first_rows(scale, *refs),
        in_specs=[hbm, hbm],
        out_specs=[vmem, vmem, vmem],
        out_shape=[
            jax.ShapeDtypeStruct((alike * line, own // LANES, LANES), f32),
            jax.ShapeDtypeStruct((own, width), f32),
            jax.ShapeDtypeStruct((cols, width), target.dtype),
        ],
        scratch_shapes=[
            pltpu.VMEM(source.shape, source.dtype),
            pltpu.VMEM((cols, width), target.dtype),
            pltpu.VMEM((own, target.shape[0]), f32),
            pltpu.VMEM((own, LANES), f32),
            pltpu.VMEM((own // LANES, LANES), f32),
            pltpu.SemaphoreType.DMA((2 * CHUNKS + 1,)),
        ],
        compiler_params=limit,
        name="first_rows",
    )(source, target)
    pieces = [mine]
    if ALIKE:
        pieces.append(lax.ppermute(mine, ALIKE, swap))
    pieces = [form for piece in pieces for form in (piece, lax.ppermute(piece, "core", swap))]
    gathered = lax.all_to_all(parts, ALIKE + LINE, 0, 0)
    parts, plan, row_base, peaks, source = pl.pallas_call(
        lambda *refs: first_columns(scale, col_bits, line // cores, *refs),
        in_specs=[vmem] * (len(pieces) + 2),
        out_specs=[vmem] * 5,
        out_shape=[
            jax.ShapeDtypeStruct((plane,) + col_shape, f32),
            jax.ShapeDtypeStruct((rows, cols), f32),
            jax.ShapeDtypeStruct(row_shape, f32),
            jax.ShapeDtypeStruct(col_shape, f32),
            jax.ShapeDtypeStruct((rows, width), source.dtype),
        ],
        scratch_shapes=[pltpu.VMEM((rows, LANES), f32), pltpu.VMEM(col_shape, f32)],
        compiler_params=limit,
        name="first_columns",
    )(*pieces, half, gathered)
    columns = lax.all_to_all(parts, PLANE, 0, 0)

    for step in range(1, ITERS):
        parts = pl.pallas_call(
            lambda *refs: later_rows(scale, row_bits, *refs),
            in_specs=[vmem] * 6,
            out_specs=vmem,
            out_shape=jax.ShapeDtypeStruct((line,) + row_shape, f32),
            scratch_shapes=[pltpu.VMEM(col_shape, f32), pltpu.VMEM(row_shape, f32)],
            compiler_params=limit,
            name="later_rows",
        )(columns, plan, row_base, peaks, source, half)
        gathered = lax.all_to_all(parts, LINE, 0, 0)
        last = step == ITERS - 1
        outs = [jax.ShapeDtypeStruct((plane,) + col_shape, f32)]
        scratch = [pltpu.VMEM((rows, LANES), f32), pltpu.VMEM(col_shape, f32)]
        if last:
            outs.append(jax.ShapeDtypeStruct(row_shape, f32))
        else:
            scratch.insert(0, pltpu.VMEM(row_shape, f32))
        parts, *row_potential = pl.pallas_call(
            lambda *refs: later_columns(scale, col_bits, *refs),
            in_specs=[vmem] * 6,
            out_specs=[vmem] * len(outs),
            out_shape=outs,
            scratch_shapes=scratch,
            compiler_params=limit,
            name="later_columns",
        )(gathered, plan, row_base, peaks, source, half)
        columns = lax.all_to_all(parts, PLANE, 0, 0)

    column_potential = (unit * (row_bits - combine(columns))).reshape(cols)
    other = lax.ppermute(column_potential, "core", swap)
    column_potential = jnp.where(
        core == 0,
        jnp.concatenate([column_potential, other]),
        jnp.concatenate([other, column_potential]),
    )
    start = lax.axis_index(ALIKE + ("core",)) * own
    row_potential = lax.dynamic_slice(row_potential[0].reshape(rows), (start,), (own,)) * unit
    return (row_potential, column_potential)


def solution(mesh):
    fine = Mesh(mesh.devices.reshape(8, 2, 2, 2, 4), ("z", "p", "q", "core", "x"))
    return jax.shard_map(
        local,
        mesh=fine,
        in_specs=(P(("z", "p", "q", "core"), None), P("x", None)),
        out_specs=(P(("z", "p", "q", "core")), P("x")),
        check_vma=False,
    )
```

time: 136 us -> 130 us (0.956)
  local copies, waits for them, and re-layouts: 9.12 us -> 2.49 us
  blocking collectives: 82.4 us -> 88.6 us
  starting transfers between devices: 12.7 us -> 9.38 us
  Pallas kernels: 16.9 us -> 15.1 us
    all_to_all x0 -> x1, blocking collectives: none -> 7.34 us  [local(): gathered = lax.all_to_all(parts, ALIKE + LINE, 0, 0)]
    unnamed x12 -> x4, local copies, waits for them, and re-layouts: 9.12 us -> 2.49 us
    all_to_all x1 -> x0, starting transfers between devices: 3.28 us -> none  [local(): gathered = lax.all_to_all(parts, LINE, 0, 0)]
    pallas_call x9 -> x8, Pallas kernels: 16.9 us -> 15.1 us  [the longest x3 8.02 us: local(): pl.pallas_call(lambda *refs: later_rows(scale, row_bits, *refs), in_specs...]
    all_to_all x3, blocking collectives: 30.2 us -> 28.8 us  [local(): gathered = lax.all_to_all(parts, LINE, 0, 0)]
  transfers between devices with their start and end apart: 4 -> 3, of which waited for: 2 -> 2; matrix products, arithmetic and copies ran while one was open for 0% -> 0% of each run, Pallas kernels for 1% -> 0%
where the time goes in v3:
time: 130 us
  blocking collectives  88.6 us (68%)
  Pallas kernels  15.1 us (12%)
  waiting for transfers between devices  12 us (9%)
  starting transfers between devices  9.38 us (7%)
  local copies, waits for them, and re-layouts  2.49 us (2%)
  other arithmetic  1.35 us (1%)
    all_to_all x3, blocking collectives, local(): columns = lax.all_to_all(parts, PLANE, 0, 0)  52.4 us
    all_to_all x3, blocking collectives, local(): gathered = lax.all_to_all(parts, LINE, 0, 0)  28.8 us
    all_to_all x1, waiting for transfers between devices, local(): columns = lax.all_to_all(parts, PLANE, 0, 0)  11.8 us
    pallas_call x3, Pallas kernels, local(): pl.pallas_call(lambda *refs: later_rows(scale, row_bits, *refs), in_specs...  8.02 us
    all_to_all x1, blocking collectives, local(): gathered = lax.all_to_all(parts, ALIKE + LINE, 0, 0)  7.34 us
    all_to_all x1, starting transfers between devices, local(): columns = lax.all_to_all(parts, PLANE, 0, 0)  3.87 us
    ppermute x1, starting transfers between devices, local(): lax.ppermute(piece, 'core', swap)  3.33 us
    pallas_call x3, Pallas kernels, local(): pl.pallas_call(lambda *refs: later_columns(scale, col_bits, *refs), in_sp...  2.8 us
  transfers between devices with their start and end apart: 3, of which 2 were waited for; matrix products, arithmetic and copies ran while one was open for 0% of the time, Pallas kernels for 0%

profile of v3, /device:TPU:1, one launch (start us, length us, event | category | flops | bytes accessed | tf_op | source)
XLA Modules:
  0.0 129.6 jit_solution(8425411682001193892)
XLA Ops:
  0.6 0.0 copy-start
  0.6 1.6 %copy-done = bf16[4096,256]{1,0:T(8,128)(2,1)S(1)} copy-done((bf16[4096,256]{1,0:T(8,128)(2,1)S(1)}, bf16[4096,256]{1,0:T(8,128)(2,1)}, u32[]{:S(2)}) %copy-start) | copy-done | bytes 2097176
  2.2 0.0 copy-start.1
  2.2 0.9 copy-done.1
  3.1 2.4 %first_rows.1 = (f32[8,2,128]{2,1,0:T(2,128)S(1)}, f32[256,256]{1,0:T(8,128)S(1)}, bf16[2048,256]{1,0:T(8,128)(2,1)S(1)}) custom-call(bf16[256,256]{1,0:T(8,128)(2,1)S(1)} %copy-done.1, bf16[4096,256]{1,0:T(8,128)(2,1)S(1)} %copy-done), custom_call_target="tpu_custom_call" | custom-call | tf_op jit(solution)/shard_map/first_rows/pallas_call | solution.py:231
  5.5 3.3 %collective-permute-start = (f32[256,256]{1,0:T(8,128)S(1)}, f32[256,256]{1,0:T(8,128)S(1)}, u32[]{:S(2)}, u32[]{:S(2)}) collective-permute-start(f32[256,256]{1,0:T(8,128)S(1)} %get-tuple-element.12.refs_0_), channel_id=1, source_target_pairs={{0,4},{4,0},{1,5},{5,1},{2,6},{6,2},{3,7},{7,3},{8,12},{12,8},{9,1... | collective-permute-start | bytes 786440 | tf_op jit(solution)/shard_map/ppermute | solution.py:254
  8.9 7.3 %all_to_all.40.refs_3_ = f32[8,2,128]{2,1,0:T(2,128)S(1)} all-to-all(f32[8,2,128]{2,1,0:T(2,128)S(1)} %get-tuple-element.14), channel_id=1, replica_groups=mesh['z'=8,'p'=2,'q'=2,'core'=2,'x'=4] {'core','x'}, dimensions={0} | all-to-all | bytes 16384 | tf_op jit(solution)/shard_map/all_to_all | solution.py:255
  16.2 0.0 collective-permute-done.refs_1_
  16.2 1.9 %first_columns.1 = (f32[32,16,128]{2,1,0:T(8,128)S(1)}, f32[512,2048]{1,0:T(8,128)S(1)}, f32[4,128]{1,0:T(4,128)S(1)}, f32[16,128]{1,0:T(8,128)S(1)}, bf16[512,256]{1,0:T(8,128)(2,1)S(1)}) custom-call(f32[256,256]{1,0:T(8,128)S(1)} %get-tuple-element.12.refs_0_, f32[256,256]{1,0:T(8,128)S(1)} %collective-permute-done.refs_1_, ...), custom_call_target="tpu_custom_call" | custom-call | tf_op jit(solution)/shard_map/first_columns/pallas_call | solution.py:256
  18.1 22.6 %all_to_all.41.refs_0_ = f32[32,16,128]{2,1,0:T(8,128)S(1)} all-to-all(f32[32,16,128]{2,1,0:T(8,128)S(1)} %get-tuple-element.15), channel_id=1, replica_groups=mesh['z'=8,'p'=2,'q'=2,'core'=2,'x'=4] {'z','p','q'}, dimensions={0} | all-to-all | bytes 524288 | tf_op jit(solution)/shard_map/all_to_all | solution.py:271
  40.7 2.7 %later_rows.3 = f32[8,4,128]{2,1,0:T(4,128)S(1)} custom-call(f32[32,16,128]{2,1,0:T(8,128)S(1)} %all_to_all.41.refs_0_, f32[512,2048]{1,0:T(8,128)S(1)} %get-tuple-element.16.refs_1_, f32[4,128]{1,0:T(4,128)S(1)} %get-tuple-element.17.refs_2_, f32[16,128]{1,0:T(8,128)S(1)} %get-tuple-element.18.refs_3_, bf16[512,256]{1,0:T(8,128)(2,1)S(1)} %get-tuple-element.19.refs_4_, ...), custom_call_target="tpu_custom_call" | custom-call | tf_op jit(solution)/shard_map/later_rows/pallas_call | solution.py:274
  43.3 9.6 %all_to_all.42.refs_0_ = f32[8,4,128]{2,1,0:T(4,128)S(1)} all-to-all(f32[8,4,128]{2,1,0:T(4,128)S(1)} %later_rows.3), channel_id=1, replica_groups=mesh['z'=8,'p'=2,'q'=2,'core'=2,'x'=4] {'core','x'}, dimensions={0} | all-to-all | bytes 32768 | tf_op jit(solution)/shard_map/all_to_all | solution.py:283
  52.9 0.7 later_columns.3
  53.6 14.9 %all_to_all.43.refs_0_ = f32[32,16,128]{2,1,0:T(8,128)S(1)} all-to-all(f32[32,16,128]{2,1,0:T(8,128)S(1)} %later_columns.3), channel_id=1, replica_groups=mesh['z'=8,'p'=2,'q'=2,'core'=2,'x'=4] {'z','p','q'}, dimensions={0} | all-to-all | bytes 524288 | tf_op jit(solution)/shard_map/all_to_all | solution.py:300
  68.6 2.7 %later_rows.4 = f32[8,4,128]{2,1,0:T(4,128)S(1)} custom-call(f32[32,16,128]{2,1,0:T(8,128)S(1)} %all_to_all.43.refs_0_, f32[512,2048]{1,0:T(8,128)S(1)} %get-tuple-element.16.refs_1_, f32[4,128]{1,0:T(4,128)S(1)} %get-tuple-element.17.refs_2_, f32[16,128]{1,0:T(8,128)S(1)} %get-tuple-element.18.refs_3_, bf16[512,256]{1,0:T(8,128)(2,1)S(1)} %get-tuple-element.19.refs_4_, ...), custom_call_target="tpu_custom_call" | custom-call | tf_op jit(solution)/shard_map/later_rows/pallas_call | solution.py:274
  71.2 9.6 %all_to_all.44.refs_0_ = f32[8,4,128]{2,1,0:T(4,128)S(1)} all-to-all(f32[8,4,128]{2,1,0:T(4,128)S(1)} %later_rows.4), channel_id=1, replica_groups=mesh['z'=8,'p'=2,'q'=2,'core'=2,'x'=4] {'core','x'}, dimensions={0} | all-to-all | bytes 32768 | tf_op jit(solution)/shard_map/all_to_all | solution.py:283
  80.8 0.7 later_columns.4
  81.5 14.9 %all_to_all.45.refs_0_ = f32[32,16,128]{2,1,0:T(8,128)S(1)} all-to-all(f32[32,16,128]{2,1,0:T(8,128)S(1)} %later_columns.4), channel_id=1, replica_groups=mesh['z'=8,'p'=2,'q'=2,'core'=2,'x'=4] {'z','p','q'}, dimensions={0} | all-to-all | bytes 524288 | tf_op jit(solution)/shard_map/all_to_all | solution.py:300
  96.5 2.7 %later_rows.5 = f32[8,4,128]{2,1,0:T(4,128)S(1)} custom-call(f32[32,16,128]{2,1,0:T(8,128)S(1)} %all_to_all.45.refs_0_, f32[512,2048]{1,0:T(8,128)S(1)} %get-tuple-element.16.refs_1_, f32[4,128]{1,0:T(4,128)S(1)} %get-tuple-element.17.refs_2_, f32[16,128]{1,0:T(8,128)S(1)} %get-tuple-element.18.refs_3_, bf16[512,256]{1,0:T(8,128)(2,1)S(1)} %get-tuple-element.19.refs_4_, ...), custom_call_target="tpu_custom_call" | custom-call | tf_op jit(solution)/shard_map/later_rows/pallas_call | solution.py:274
  99.1 9.6 %all_to_all.46.refs_0_ = f32[8,4,128]{2,1,0:T(4,128)S(1)} all-to-all(f32[8,4,128]{2,1,0:T(4,128)S(1)} %later_rows.5), channel_id=1, replica_groups=mesh['z'=8,'p'=2,'q'=2,'core'=2,'x'=4] {'core','x'}, dimensions={0} | all-to-all | bytes 32768 | tf_op jit(solution)/shard_map/all_to_all | solution.py:283
  108.7 1.4 %later_columns.5 = (f32[32,16,128]{2,1,0:T(8,128)}, f32[4,128]{1,0:T(4,128)S(1)}) custom-call(f32[8,4,128]{2,1,0:T(4,128)S(1)} %all_to_all.46.refs_0_, f32[512,2048]{1,0:T(8,128)S(1)} %get-tuple-element.16.refs_1_, f32[4,128]{1,0:T(4,128)S(1)} %get-tuple-element.17.refs_2_, f32[16,128]{1,0:T(8,128)S(1)} %get-tuple-element.18.refs_3_, ...), custom_call_target="tpu_custom_call" | custom-call | tf_op jit(solution)/shard_map/later_columns/pallas_call | solution.py:291
  110.1 3.9 %all-to-all-start.7 = ((f32[32,16,128]{2,1,0:T(8,128)}), f32[32,16,128]{2,1,0:T(8,128)S(1)}, u32[]{:S(2)}, u32[]{:S(2)}) async-start(f32[32,16,128]{2,1,0:T(8,128)} %get-tuple-element.21), calls=%async_computation.7 | async-start | bytes 524288 | tf_op jit(solution)/shard_map/all_to_all | solution.py:300
  114.0 11.8 %all-to-all-done.7 = f32[32,16,128]{2,1,0:T(8,128)S(1)} async-done(((f32[32,16,128]{2,1,0:T(8,128)}), f32[32,16,128]{2,1,0:T(8,128)S(1)}, u32[]{:S(2)}, u32[]{:S(2)}) %all-to-all-start.7) | async-done | bytes 262176 | tf_op jit(solution)/shard_map/all_to_all | solution.py:300
  125.9 0.1 exponential_reduce_fusion
  125.9 2.2 %collective-permute-start.1 = (f32[2048]{0:T(1024)S(1)}, f32[2048]{0:T(1024)S(1)}, u32[]{:S(2)}, u32[]{:S(2)}) collective-permute-start(f32[2048]{0:T(1024)S(1)} %multiply_bitcast_fusion), channel_id=1, source_target_pairs={{0,4},{4,0},{1,5},{5,1},{2,6},{6,2},{3,7},{7,3},{8,12},{12,8},{9,1... | collective-permute-start | bytes 24584 | tf_op jit(solution)/shard_map/ppermute | solution.py:303
  128.1 0.6 dynamic-slice_multiply_fusion
  128.8 0.2 collective-permute-done.1
  128.9 0.6 maximum_select_fusion
  (2 shorter events, 0.0 us)
Async XLA Ops:
  0.6 1.6 %copy-start = (bf16[4096,256]{1,0:T(8,128)(2,1)S(1)}, bf16[4096,256]{1,0:T(8,128)(2,1)}, u32[]{:S(2)}) copy-start(bf16[4096,256]{1,0:T(8,128)(2,1)} %refs_1_.1) | copy-start | bytes 6291460
  2.2 0.9 copy-start.1
  5.5 10.7 %collective-permute-start = (f32[256,256]{1,0:T(8,128)S(1)}, f32[256,256]{1,0:T(8,128)S(1)}, u32[]{:S(2)}, u32[]{:S(2)}) collective-permute-start(f32[256,256]{1,0:T(8,128)S(1)} %get-tuple-element.12.refs_0_), channel_id=1, source_target_pairs={{0,4},{4,0},{1,5},{5,1},{2,6},{6,2},{3,7},{7,3},{8,12},{12,8},{9,1... | collective-permute-start | bytes 786440 | tf_op jit(solution)/shard_map/ppermute | solution.py:254
  110.1 15.7 %all-to-all-start.7 = ((f32[32,16,128]{2,1,0:T(8,128)}), f32[32,16,128]{2,1,0:T(8,128)S(1)}, u32[]{:S(2)}, u32[]{:S(2)}) async-start(f32[32,16,128]{2,1,0:T(8,128)} %get-tuple-element.21), calls=%async_computation.7 | async-start | bytes 524288 | tf_op jit(solution)/shard_map/all_to_all | solution.py:300
  125.9 3.0 %collective-permute-start.1 = (f32[2048]{0:T(1024)S(1)}, f32[2048]{0:T(1024)S(1)}, u32[]{:S(2)}, u32[]{:S(2)}) collective-permute-start(f32[2048]{0:T(1024)S(1)} %multiply_bitcast_fusion), channel_id=1, source_target_pairs={{0,4},{4,0},{1,5},{5,1},{2,6},{6,2},{3,7},{7,3},{8,12},{12,8},{9,1... | collective-permute-start | bytes 24584 | tf_op jit(solution)/shard_map/ppermute | solution.py:303

commit v4 on v3

--- a/solution.py
+++ b/solution.py
@@ -110,9 +110,7 @@
     return jnp.sum(total, axis=0, keepdims=True)
 
 
-def first_columns(
-    scale, bits, each, *refs
-):
+def first_columns(scale, bits, each, *refs):
     pieces = refs[: 2 * (1 + len(ALIKE))]
     half_ref, gathered_ref, out_ref, plan_ref, row_ref, peak_ref, source_ref, standing, folded = refs[len(pieces) :]
     rows, cols = plan_ref.shape
@@ -178,11 +176,10 @@
 
 
 def later_columns(
-    scale, bits, gathered_ref, plan_ref, row_ref, peak_ref, source_ref, half_ref, out_ref, potential_ref, standing, folded
+    scale, bits, gathered_ref, plan_ref, row_ref, peak_ref, source_ref, half_ref, out_ref, standing, folded
 ):
     rows, cols = plan_ref.shape
     potential = bits - combine(gathered_ref[...])
-    potential_ref[...] = potential
     change = potential - row_ref[...]
     shift = largest(change)
     stand(standing, jnp.exp2(change - shift))
@@ -194,7 +191,7 @@
 
     @pl.when(jnp.logical_not(smallest(total)[0, 0] >= SAFE))
     def _():
-        stand(standing, potential_ref[...])
+        stand(standing, potential)
         for start in range(0, cols, TILE):
             part = score(source_ref[...], half_ref[start : start + TILE, :], scale) + spread(
                 standing[...], TILE // LANES
@@ -205,6 +202,11 @@
                 t = (start + lane) // LANES
                 folded[t : t + 1, :] = result[:, lane : lane + LANES]
         send(out_ref, folded[...])
+
+
+def finish(unit, row_bits, col_bits, row_parts_ref, column_parts_ref, row_ref, column_ref):
+    row_ref[...] = unit * (col_bits - combine(row_parts_ref[...]))
+    column_ref[...] = unit * (row_bits - combine(column_parts_ref[...]))
 
 
 def local(source, target):
@@ -245,7 +247,7 @@
             pltpu.VMEM((own // LANES, LANES), f32),
             pltpu.SemaphoreType.DMA((2 * CHUNKS + 1,)),
         ],
-        compiler_params=limit,
+        compiler_params=pltpu.CompilerParams(vmem_limit_bytes=52 * 2**20),
         name="first_rows",
     )(source, target)
     pieces = [mine]
@@ -281,25 +283,26 @@
             name="later_rows",
         )(columns, plan, row_base, peaks, source, half)
         gathered = lax.all_to_all(parts, LINE, 0, 0)
-        last = step == ITERS - 1
-        outs = [jax.ShapeDtypeStruct((plane,) + col_shape, f32)]
-        scratch = [pltpu.VMEM((rows, LANES), f32), pltpu.VMEM(col_shape, f32)]
-        if last:
-            outs.append(jax.ShapeDtypeStruct(row_shape, f32))
-        else:
-            scratch.insert(0, pltpu.VMEM(row_shape, f32))
-        parts, *row_potential = pl.pallas_call(
+        parts = pl.pallas_call(
             lambda *refs: later_columns(scale, col_bits, *refs),
             in_specs=[vmem] * 6,
-            out_specs=[vmem] * len(outs),
-            out_shape=outs,
-            scratch_shapes=scratch,
+            out_specs=vmem,
+            out_shape=jax.ShapeDtypeStruct((plane,) + col_shape, f32),
+            scratch_shapes=[pltpu.VMEM((rows, LANES), f32), pltpu.VMEM(col_shape, f32)],
             compiler_params=limit,
             name="later_columns",
         )(gathered, plan, row_base, peaks, source, half)
         columns = lax.all_to_all(parts, PLANE, 0, 0)
 
-    column_potential = (unit * (row_bits - combine(columns))).reshape(cols)
+    row_potential, column_potential = pl.pallas_call(
+        lambda *refs: finish(unit, row_bits, col_bits, *refs),
+        in_specs=[vmem] * 2,
+        out_specs=[vmem] * 2,
+        out_shape=[jax.ShapeDtypeStruct(row_shape, f32), jax.ShapeDtypeStruct(col_shape, f32)],
+        compiler_params=limit,
+        name="finish",
+    )(gathered, columns)
+    column_potential = column_potential.reshape(cols)
     other = lax.ppermute(column_potential, "core", swap)
     column_potential = jnp.where(
         core == 0,
@@ -307,7 +310,7 @@
         jnp.concatenate([other, column_potential]),
     )
     start = lax.axis_index(ALIKE + ("core",)) * own
-    row_potential = lax.dynamic_slice(row_potential[0].reshape(rows), (start,), (own,)) * unit
+    row_potential = lax.dynamic_slice(row_potential.reshape(rows), (start,), (own,))
     return (row_potential, column_potential)
 
 

time: 130 us -> 128 us (0.985)
  blocking collectives: 88.6 us -> 103 us
  waiting for transfers between devices: 12 us -> 0.2 us
  starting transfers between devices: 9.38 us -> 5.74 us
    all_to_all x3 -> x4, blocking collectives: 52.4 us -> 67.3 us  [local(): columns = lax.all_to_all(parts, PLANE, 0, 0)]
    all_to_all x1 -> x0, waiting for transfers between devices: 11.8 us -> none  [local(): columns = lax.all_to_all(parts, PLANE, 0, 0)]
    all_to_all x1 -> x0, starting transfers between devices: 3.87 us -> none  [local(): columns = lax.all_to_all(parts, PLANE, 0, 0)]
    unnamed x4 -> x2, local copies, waits for them, and re-layouts: 2.49 us -> 0.9 us
  transfers between devices with their start and end apart: 3 -> 2, of which waited for: 2 -> 1; matrix products, arithmetic and copies ran while one was open for 0% -> 0% of each run, Pallas kernels for 0% -> 0%
where the time goes in v4:
time: 128 us
  blocking collectives  103 us (80%)
  Pallas kernels  15.4 us (12%)
  starting transfers between devices  5.74 us (4%)
  local copies, waits for them, and re-layouts  1.53 us (1%)
    all_to_all x4, blocking collectives, local(): columns = lax.all_to_all(parts, PLANE, 0, 0)  67.3 us
    all_to_all x3, blocking collectives, local(): gathered = lax.all_to_all(parts, LINE, 0, 0)  28.8 us
    pallas_call x3, Pallas kernels, local(): pl.pallas_call(lambda *refs: later_rows(scale, row_bits, *refs), in_specs...  8.03 us
    all_to_all x1, blocking collectives, local(): gathered = lax.all_to_all(parts, ALIKE + LINE, 0, 0)  7.34 us
    ppermute x1, starting transfers between devices, local(): lax.ppermute(piece, 'core', swap)  3.33 us
    pallas_call x1, Pallas kernels, local(): pl.pallas_call(lambda *refs: first_rows(scale, *refs), in_specs=[hbm, hbm...  3.27 us
  transfers between devices with their start and end apart: 2, of which 1 were waited for; matrix products, arithmetic and copies ran while one was open for 0% of the time, Pallas kernels for 0%

profile of v4, /device:TPU:1, one launch (start us, length us, event | category | flops | bytes accessed | tf_op | source)
XLA Modules:
  0.0 127.6 jit_solution(13817034935747251964)
XLA Ops:
  0.6 0.0 copy-start
  0.6 0.9 copy-done
  1.5 3.3 %first_rows.1 = (f32[8,2,128]{2,1,0:T(2,128)S(1)}, f32[256,256]{1,0:T(8,128)S(1)}, bf16[2048,256]{1,0:T(8,128)(2,1)S(1)}) custom-call(bf16[256,256]{1,0:T(8,128)(2,1)S(1)} %copy-done, bf16[4096,256]{1,0:T(8,128)(2,1)} %refs_1_.1), custom_call_target="tpu_custom_call" | custom-call | tf_op jit(solution)/shard_map/first_rows/pallas_call | solution.py:233
  4.8 3.3 %collective-permute-start = (f32[256,256]{1,0:T(8,128)S(1)}, f32[256,256]{1,0:T(8,128)S(1)}, u32[]{:S(2)}, u32[]{:S(2)}) collective-permute-start(f32[256,256]{1,0:T(8,128)S(1)} %get-tuple-element.12.refs_0_), channel_id=1, source_target_pairs={{0,4},{4,0},{1,5},{5,1},{2,6},{6,2},{3,7},{7,3},{8,12},{12,8},{9,1... | collective-permute-start | bytes 786440 | tf_op jit(solution)/shard_map/ppermute | solution.py:256
  8.1 7.3 %all_to_all.40.refs_3_ = f32[8,2,128]{2,1,0:T(2,128)S(1)} all-to-all(f32[8,2,128]{2,1,0:T(2,128)S(1)} %get-tuple-element.14), channel_id=1, replica_groups=mesh['z'=8,'p'=2,'q'=2,'core'=2,'x'=4] {'core','x'}, dimensions={0} | all-to-all | bytes 16384 | tf_op jit(solution)/shard_map/all_to_all | solution.py:257
  15.5 0.0 collective-permute-done.refs_1_
  15.5 1.9 %first_columns.1 = (f32[32,16,128]{2,1,0:T(8,128)S(1)}, f32[512,2048]{1,0:T(8,128)S(1)}, f32[4,128]{1,0:T(4,128)S(1)}, f32[16,128]{1,0:T(8,128)S(1)}, bf16[512,256]{1,0:T(8,128)(2,1)S(1)}) custom-call(f32[256,256]{1,0:T(8,128)S(1)} %get-tuple-element.12.refs_0_, f32[256,256]{1,0:T(8,128)S(1)} %collective-permute-done.refs_1_, ...), custom_call_target="tpu_custom_call" | custom-call | tf_op jit(solution)/shard_map/first_columns/pallas_call | solution.py:258
  17.4 22.6 %all_to_all.41.refs_0_ = f32[32,16,128]{2,1,0:T(8,128)S(1)} all-to-all(f32[32,16,128]{2,1,0:T(8,128)S(1)} %get-tuple-element.15), channel_id=1, replica_groups=mesh['z'=8,'p'=2,'q'=2,'core'=2,'x'=4] {'z','p','q'}, dimensions={0} | all-to-all | bytes 524288 | tf_op jit(solution)/shard_map/all_to_all | solution.py:273
  39.9 2.7 %later_rows.3 = f32[8,4,128]{2,1,0:T(4,128)S(1)} custom-call(f32[32,16,128]{2,1,0:T(8,128)S(1)} %all_to_all.41.refs_0_, f32[512,2048]{1,0:T(8,128)S(1)} %get-tuple-element.16.refs_1_, f32[4,128]{1,0:T(4,128)S(1)} %get-tuple-element.17.refs_2_, f32[16,128]{1,0:T(8,128)S(1)} %get-tuple-element.18.refs_3_, bf16[512,256]{1,0:T(8,128)(2,1)S(1)} %get-tuple-element.19.refs_4_, ...), custom_call_target="tpu_custom_call" | custom-call | tf_op jit(solution)/shard_map/later_rows/pallas_call | solution.py:276
  42.6 9.6 %all_to_all.42.refs_0_ = f32[8,4,128]{2,1,0:T(4,128)S(1)} all-to-all(f32[8,4,128]{2,1,0:T(4,128)S(1)} %later_rows.3), channel_id=1, replica_groups=mesh['z'=8,'p'=2,'q'=2,'core'=2,'x'=4] {'core','x'}, dimensions={0} | all-to-all | bytes 32768 | tf_op jit(solution)/shard_map/all_to_all | solution.py:285
  52.2 0.7 later_columns.3
  52.9 14.9 %all_to_all.43.refs_0_ = f32[32,16,128]{2,1,0:T(8,128)S(1)} all-to-all(f32[32,16,128]{2,1,0:T(8,128)S(1)} %later_columns.3), channel_id=1, replica_groups=mesh['z'=8,'p'=2,'q'=2,'core'=2,'x'=4] {'z','p','q'}, dimensions={0} | all-to-all | bytes 524288 | tf_op jit(solution)/shard_map/all_to_all | solution.py:295
  67.8 2.7 %later_rows.4 = f32[8,4,128]{2,1,0:T(4,128)S(1)} custom-call(f32[32,16,128]{2,1,0:T(8,128)S(1)} %all_to_all.43.refs_0_, f32[512,2048]{1,0:T(8,128)S(1)} %get-tuple-element.16.refs_1_, f32[4,128]{1,0:T(4,128)S(1)} %get-tuple-element.17.refs_2_, f32[16,128]{1,0:T(8,128)S(1)} %get-tuple-element.18.refs_3_, bf16[512,256]{1,0:T(8,128)(2,1)S(1)} %get-tuple-element.19.refs_4_, ...), custom_call_target="tpu_custom_call" | custom-call | tf_op jit(solution)/shard_map/later_rows/pallas_call | solution.py:276
  70.5 9.6 %all_to_all.44.refs_0_ = f32[8,4,128]{2,1,0:T(4,128)S(1)} all-to-all(f32[8,4,128]{2,1,0:T(4,128)S(1)} %later_rows.4), channel_id=1, replica_groups=mesh['z'=8,'p'=2,'q'=2,'core'=2,'x'=4] {'core','x'}, dimensions={0} | all-to-all | bytes 32768 | tf_op jit(solution)/shard_map/all_to_all | solution.py:285
  80.1 0.7 later_columns.4
  80.8 14.9 %all_to_all.45.refs_0_ = f32[32,16,128]{2,1,0:T(8,128)S(1)} all-to-all(f32[32,16,128]{2,1,0:T(8,128)S(1)} %later_columns.4), channel_id=1, replica_groups=mesh['z'=8,'p'=2,'q'=2,'core'=2,'x'=4] {'z','p','q'}, dimensions={0} | all-to-all | bytes 524288 | tf_op jit(solution)/shard_map/all_to_all | solution.py:295
  95.7 2.7 %later_rows.5 = f32[8,4,128]{2,1,0:T(4,128)S(1)} custom-call(f32[32,16,128]{2,1,0:T(8,128)S(1)} %all_to_all.45.refs_0_, f32[512,2048]{1,0:T(8,128)S(1)} %get-tuple-element.16.refs_1_, f32[4,128]{1,0:T(4,128)S(1)} %get-tuple-element.17.refs_2_, f32[16,128]{1,0:T(8,128)S(1)} %get-tuple-element.18.refs_3_, bf16[512,256]{1,0:T(8,128)(2,1)S(1)} %get-tuple-element.19.refs_4_, ...), custom_call_target="tpu_custom_call" | custom-call | tf_op jit(solution)/shard_map/later_rows/pallas_call | solution.py:276
  98.4 9.6 %all_to_all.46.refs_0_ = f32[8,4,128]{2,1,0:T(4,128)S(1)} all-to-all(f32[8,4,128]{2,1,0:T(4,128)S(1)} %later_rows.5), channel_id=1, replica_groups=mesh['z'=8,'p'=2,'q'=2,'core'=2,'x'=4] {'core','x'}, dimensions={0} | all-to-all | bytes 32768 | tf_op jit(solution)/shard_map/all_to_all | solution.py:285
  108.0 0.7 later_columns.5
  108.7 14.9 %all_to_all.47.refs_1_ = f32[32,16,128]{2,1,0:T(8,128)S(1)} all-to-all(f32[32,16,128]{2,1,0:T(8,128)S(1)} %later_columns.5), channel_id=1, replica_groups=mesh['z'=8,'p'=2,'q'=2,'core'=2,'x'=4] {'z','p','q'}, dimensions={0} | all-to-all | bytes 524288 | tf_op jit(solution)/shard_map/all_to_all | solution.py:295
  123.7 0.1 finish.1
  123.7 2.4 %collective-permute-start.1 = (f32[2048]{0:T(1024)S(1)}, f32[2048]{0:T(1024)S(1)}, u32[]{:S(2)}, u32[]{:S(2)}) collective-permute-start(f32[2048]{0:T(1024)S(1)} %bitcast.2), channel_id=1, source_target_pairs={{0,4},{4,0},{1,5},{5,1},{2,6},{6,2},{3,7},{7,3},{8,12},{12,8},{9,1... | collective-permute-start | bytes 24584 | tf_op jit(solution)/shard_map/ppermute | solution.py:306
  126.2 0.6 dynamic_slice.3
  126.8 0.2 collective-permute-done.1
  127.0 0.6 maximum_select_fusion
Async XLA Ops:
  0.6 0.9 copy-start
  4.8 10.7 %collective-permute-start = (f32[256,256]{1,0:T(8,128)S(1)}, f32[256,256]{1,0:T(8,128)S(1)}, u32[]{:S(2)}, u32[]{:S(2)}) collective-permute-start(f32[256,256]{1,0:T(8,128)S(1)} %get-tuple-element.12.refs_0_), channel_id=1, source_target_pairs={{0,4},{4,0},{1,5},{5,1},{2,6},{6,2},{3,7},{7,3},{8,12},{12,8},{9,1... | collective-permute-start | bytes 786440 | tf_op jit(solution)/shard_map/ppermute | solution.py:256
  123.7 3.2 %collective-permute-start.1 = (f32[2048]{0:T(1024)S(1)}, f32[2048]{0:T(1024)S(1)}, u32[]{:S(2)}, u32[]{:S(2)}) collective-permute-start(f32[2048]{0:T(1024)S(1)} %bitcast.2), channel_id=1, source_target_pairs={{0,4},{4,0},{1,5},{5,1},{2,6},{6,2},{3,7},{7,3},{8,12},{12,8},{9,1... | collective-permute-start | bytes 24584 | tf_op jit(solution)/shard_map/ppermute | solution.py:306

commit v5 on v4

v5 whole, which is shorter than its diff:
```python
import math

import jax
import jax.numpy as jnp
from jax import lax
from jax.experimental import pallas as pl
from jax.experimental.pallas import tpu as pltpu
from jax.sharding import Mesh, PartitionSpec as P

ITERS = 4
EPSILON = 0.1
TILE = 256
LANES = 128
SUBLANES = 8
CHUNKS = 2
SAFE = 2.0**-80

FIRST_PLANE = ("z", "p", "q")
PLANE = ("z", "q")
LINE = ("core", "x")


def combine(parts):
    peak = jnp.max(parts, axis=0)
    return peak + jnp.log2(jnp.sum(jnp.exp2(parts - peak[None]), axis=0))


def largest(values):
    return jnp.max(jnp.max(values, axis=1, keepdims=True), axis=0, keepdims=True)


def smallest(values):
    return jnp.min(jnp.min(values, axis=1, keepdims=True), axis=0, keepdims=True)


def stand(ref, values):
    for k in range(values.shape[0]):
        ref[k * LANES : (k + 1) * LANES, :] = jnp.broadcast_to(values[k : k + 1], (LANES, LANES)).T


def fold(ref, row):
    for k in range(ref.shape[0]):
        ref[k : k + 1, :] = row[:, k * LANES : (k + 1) * LANES]
    return ref[...]


def spread(row, count):
    return jnp.concatenate([row] * count, axis=1)


def send(out_ref, values):
    for slot in range(out_ref.shape[0]):
        out_ref[slot] = values


def score(source, target, scale):
    return scale * lax.dot_general(
        source, target, (((1,), (1,)), ((), ())), preferred_element_type=jnp.float32
    )


def first_rows(
    scale, source_ref, target_ref, out_ref, wide_ref, half_ref, source, rest, scores, peaks, line, arrived
):
    core = lax.axis_index("core")
    rows, half = source.shape[0], half_ref.shape[0]
    chunk = half // CHUNKS
    fetch = pltpu.make_async_copy(source_ref, source, arrived.at[2 * CHUNKS])
    fetch.start()
    copies = []
    for side, place in ((core, half_ref), (1 - core, rest)):
        for k in range(CHUNKS):
            copies.append(
                pltpu.make_async_copy(
                    target_ref.at[pl.ds(pl.multiple_of(side * half + k * chunk, chunk), chunk)],
                    place.at[pl.ds(k * chunk, chunk)],
                    arrived.at[len(copies)],
                )
            )
            copies[-1].start()
    fetch.wait()
    wide_ref[...] = source[...].astype(jnp.float32)
    for start in range(0, 2 * half, TILE):
        if start % chunk == 0:
            copies[start // chunk].wait()
        place = half_ref if start < half else rest
        tile = slice(start, start + TILE)
        part = score(source[...], place[start % half : start % half + TILE, :], scale)
        scores[:, tile] = part
        high = part[:, :LANES]
        for lane in range(LANES, TILE, LANES):
            high = jnp.maximum(high, part[:, lane : lane + LANES])
        peaks[...] = high if start == 0 else jnp.maximum(peaks[...], high)
    for k in range(rows // LANES):
        block = slice(k * LANES, (k + 1) * LANES)
        peak = jnp.max(peaks[block, :], axis=1, keepdims=True)
        total = jnp.sum(jnp.exp2(scores[block, :] - peak), axis=1, keepdims=True)
        line[k : k + 1, :] = jnp.broadcast_to(peak + jnp.log2(total), (LANES, LANES)).T[:1]
    send(out_ref, line[...])


def column_sums(rows, width, get):
    total = lax.fori_loop(
        0,
        rows // SUBLANES,
        lambda k, total: total + get(pl.ds(pl.multiple_of(k * SUBLANES, SUBLANES), SUBLANES)),
        jnp.zeros((SUBLANES, width), jnp.float32),
        unroll=16,
    )
    return jnp.sum(total, axis=0, keepdims=True)


def place(source_ref, mine_ref, other_ref):
    core = lax.axis_index("core")
    own = mine_ref.shape[0]
    for side, piece in ((core, mine_ref), (1 - core, other_ref)):
        source_ref[pl.ds(pl.multiple_of(side * own, own), own), :] = piece[...].astype(source_ref.dtype)


def exponentials(scale, source_ref, half_ref, plan_ref, standing):
    rows, cols = plan_ref.shape
    highs = []
    for start in range(0, cols, TILE):
        tile = slice(start, start + TILE)
        part = score(source_ref[...], half_ref[tile, :], scale)
        if standing is not None:
            part = part + spread(standing[...], TILE // LANES)
        plan_ref[:, tile] = part
        highs.append(jnp.max(part, axis=0, keepdims=True))
    peak = jnp.concatenate(highs, axis=1)
    shift = jnp.broadcast_to(peak, (SUBLANES, cols))

    def term(block):
        value = jnp.exp2(plan_ref[block, :] - shift)
        plan_ref[block, :] = value
        return value

    return peak, column_sums(rows, cols, term)


def first_potential(bits, gathered_ref, away_ref, potential_ref, passed_ref):
    passed_ref[...] = away_ref[...]
    parts = gathered_ref[...]
    each = parts.shape[0] // 2
    potential_ref[...] = bits - jnp.concatenate([combine(parts[:each]), combine(parts[each:])], axis=0)


def first_columns(
    scale,
    mine_ref,
    other_ref,
    half_ref,
    potential_ref,
    out_ref,
    plan_ref,
    row_ref,
    peak_ref,
    source_ref,
    standing,
    folded,
):
    place(source_ref, mine_ref, other_ref)
    row_ref[...] = potential_ref[...]
    stand(standing, potential_ref[...])
    peak, total = exponentials(scale, source_ref, half_ref, plan_ref, standing)
    out_ref[...] = fold(peak_ref, peak) + jnp.log2(fold(folded, total))


def partner_rows(
    scale, mine_ref, other_ref, half_ref, columns_ref, out_ref, plan_ref, row_ref, peak_ref, source_ref
):
    send(out_ref, columns_ref[...])
    place(source_ref, mine_ref, other_ref)
    row_ref[...] = jnp.zeros_like(row_ref)
    peak, _ = exponentials(scale, source_ref, half_ref, plan_ref, None)
    fold(peak_ref, peak)


def later_rows(scale, bits, gathered_ref, half_ref, *refs):
    blocks, (out_ref, factor, totals) = (refs[:4], refs[4:8]), refs[8:]
    potential = bits - combine(gathered_ref[...])
    low = None
    for index, (plan_ref, row_ref, peak_ref, _) in enumerate(blocks):
        rows, cols = plan_ref.shape
        first = index * rows // LANES
        change = potential + peak_ref[...]
        shift = largest(change)
        factor[...] = jnp.exp2(change - shift)
        for k in range(rows // LANES):
            block = slice(k * LANES, (k + 1) * LANES)
            total = jnp.zeros((LANES, LANES), jnp.float32)
            for t in range(cols // LANES):
                total = total + plan_ref[block, t * LANES : (t + 1) * LANES] * factor[t : t + 1, :]
            totals[first + k : first + k + 1, :] = jnp.sum(total.T, axis=0, keepdims=True)
        part = slice(first, first + rows // LANES)
        total = totals[part, :]
        low = total if low is None else jnp.minimum(low, total)
        totals[part, :] = shift - row_ref[...] + jnp.log2(total)
    send(out_ref, totals[...])

    @pl.when(jnp.logical_not(smallest(low)[0, 0] >= SAFE))
    def _():
        wide = jnp.concatenate([potential[t : t + 1] for t in range(potential.shape[0])], axis=1)
        for index, (plan_ref, _, _, source_ref) in enumerate(blocks):
            count = plan_ref.shape[0] // LANES
            for k in range(count):
                part = score(source_ref[k * LANES : (k + 1) * LANES, :], half_ref[...], scale) + wide
                peak = jnp.max(part, axis=1, keepdims=True)
                total = jnp.sum(jnp.exp2(part - peak), axis=1, keepdims=True)
                row = index * count + k
                totals[row : row + 1, :] = jnp.broadcast_to(peak + jnp.log2(total), (LANES, LANES)).T[:1]
        send(out_ref, totals[...])


def later_columns(scale, bits, gathered_ref, half_ref, *refs):
    blocks, (out_ref, standing, folded) = (refs[:4], refs[4:8]), refs[8:]
    potential = bits - combine(gathered_ref[...])
    low = None
    results = []
    for index, (plan_ref, row_ref, peak_ref, _) in enumerate(blocks):
        rows, cols = plan_ref.shape
        count = cols // LANES
        change = potential[index * rows // LANES : (index + 1) * rows // LANES] - row_ref[...]
        shift = largest(change)
        stand(standing, jnp.exp2(change - shift))
        total = column_sums(rows, cols, lambda block: plan_ref[block, :] * spread(standing[block, :], count))
        total = fold(folded, total)
        low = total if low is None else jnp.minimum(low, total)
        results.append(peak_ref[...] + shift + jnp.log2(total))
    send(out_ref, combine(jnp.stack(results)))

    @pl.when(jnp.logical_not(smallest(low)[0, 0] >= SAFE))
    def _():
        for start in range(0, half_ref.shape[0], TILE):
            results = []
            for index, (plan_ref, _, _, source_ref) in enumerate(blocks):
                rows = plan_ref.shape[0]
                stand(standing, potential[index * rows // LANES : (index + 1) * rows // LANES])
                part = score(source_ref[...], half_ref[start : start + TILE, :], scale) + spread(
                    standing[...], TILE // LANES
                )
                peak = jnp.max(part, axis=0, keepdims=True)
                results.append(peak + jnp.log2(jnp.sum(jnp.exp2(part - peak), axis=0, keepdims=True)))
            result = combine(jnp.stack(results))
            for lane in range(0, TILE, LANES):
                t = (start + lane) // LANES
                folded[t : t + 1, :] = result[:, lane : lane + LANES]
        send(out_ref, folded[...])


def finish(unit, row_bits, col_bits, row_parts_ref, column_parts_ref, row_ref, column_ref):
    row_ref[...] = unit * (col_bits - combine(row_parts_ref[...]))
    column_ref[...] = unit * (row_bits - combine(column_parts_ref[...]))


def local(source, target):
    f32 = jnp.float32
    own, width = source.shape
    first_plane = lax.axis_size(FIRST_PLANE)
    plane = lax.axis_size(PLANE)
    line = lax.axis_size(LINE)
    cores = lax.axis_size("core")
    rows = own * cores
    cols = target.shape[0] // cores
    row_bits = math.log2(rows * first_plane)
    col_bits = math.log2(cols * line)
    scale = math.log2(math.e) / (math.sqrt(width) * EPSILON)
    unit = EPSILON * math.log(2.0)
    core = lax.axis_index("core")
    swap = [(0, 1), (1, 0)]
    vmem = pl.BlockSpec(memory_space=pltpu.VMEM)
    hbm = pl.BlockSpec(memory_space=pltpu.HBM)
    chip_shape = (rows // LANES, LANES)
    row_shape = (2 * rows // LANES, LANES)
    col_shape = (cols // LANES, LANES)
    limit = pltpu.CompilerParams(vmem_limit_bytes=24 * 2**20)
    block_out = [
        jax.ShapeDtypeStruct((rows, cols), f32),
        jax.ShapeDtypeStruct(chip_shape, f32),
        jax.ShapeDtypeStruct(col_shape, f32),
        jax.ShapeDtypeStruct((rows, width), source.dtype),
    ]

    parts, mine, half = pl.pallas_call(
        lambda *refs: first_rows(scale, *refs),
        in_specs=[hbm, hbm],
        out_specs=[vmem] * 3,
        out_shape=[
            jax.ShapeDtypeStruct((line, own // LANES, LANES), f32),
            jax.ShapeDtypeStruct((own, width), f32),
            jax.ShapeDtypeStruct((cols, width), target.dtype),
        ],
        scratch_shapes=[
            pltpu.VMEM(source.shape, source.dtype),
            pltpu.VMEM((cols, width), target.dtype),
            pltpu.VMEM((own, target.shape[0]), f32),
            pltpu.VMEM((own, LANES), f32),
            pltpu.VMEM((own // LANES, LANES), f32),
            pltpu.SemaphoreType.DMA((2 * CHUNKS + 1,)),
        ],
        compiler_params=pltpu.CompilerParams(vmem_limit_bytes=52 * 2**20),
        name="first_rows",
    )(source, target)
    other = lax.ppermute(mine, "core", swap)
    away = lax.ppermute(mine, ("p", "q"), [(0, 3), (3, 0), (1, 2), (2, 1)])
    gathered = lax.all_to_all(parts, LINE, 0, 0)
    potential, away = pl.pallas_call(
        lambda *refs: first_potential(col_bits, *refs),
        in_specs=[vmem] * 2,
        out_specs=[vmem] * 2,
        out_shape=[jax.ShapeDtypeStruct(chip_shape, f32), jax.ShapeDtypeStruct((own, width), f32)],
        compiler_params=limit,
        name="first_potential",
    )(gathered, away)
    columns, *mine_block = pl.pallas_call(
        lambda *refs: first_columns(scale, *refs),
        in_specs=[vmem] * 4,
        out_specs=[vmem] * 5,
        out_shape=[jax.ShapeDtypeStruct(col_shape, f32)] + block_out,
        scratch_shapes=[pltpu.VMEM((rows, LANES), f32), pltpu.VMEM(col_shape, f32)],
        compiler_params=limit,
        name="first_columns",
    )(mine, other, half, potential)
    parts, *away_block = pl.pallas_call(
        lambda *refs: partner_rows(scale, *refs),
        in_specs=[vmem] * 4,
        out_specs=[vmem] * 5,
        out_shape=[jax.ShapeDtypeStruct((first_plane,) + col_shape, f32)] + block_out,
        compiler_params=limit,
        name="partner_rows",
    )(away, lax.ppermute(away, "core", swap), half, columns)
    columns = lax.all_to_all(parts, FIRST_PLANE, 0, 0)

    for step in range(1, ITERS):
        parts = pl.pallas_call(
            lambda *refs: later_rows(scale, row_bits, *refs),
            in_specs=[vmem] * 10,
            out_specs=vmem,
            out_shape=jax.ShapeDtypeStruct((line,) + row_shape, f32),
            scratch_shapes=[pltpu.VMEM(col_shape, f32), pltpu.VMEM(row_shape, f32)],
            compiler_params=limit,
            name="later_rows",
        )(columns, half, *mine_block, *away_block)
        gathered = lax.all_to_all(parts, LINE, 0, 0)
        parts = pl.pallas_call(
            lambda *refs: later_columns(scale, col_bits, *refs),
            in_specs=[vmem] * 10,
            out_specs=vmem,
            out_shape=jax.ShapeDtypeStruct((plane,) + col_shape, f32),
            scratch_shapes=[pltpu.VMEM((rows, LANES), f32), pltpu.VMEM(col_shape, f32)],
            compiler_params=limit,
            name="later_columns",
        )(gathered, half, *mine_block, *away_block)
        columns = lax.all_to_all(parts, PLANE, 0, 0)

    row_potential, column_potential = pl.pallas_call(
        lambda *refs: finish(unit, row_bits, col_bits, *refs),
        in_specs=[vmem] * 2,
        out_specs=[vmem] * 2,
        out_shape=[jax.ShapeDtypeStruct(row_shape, f32), jax.ShapeDtypeStruct(col_shape, f32)],
        compiler_params=limit,
        name="finish",
    )(gathered, columns)
    column_potential = column_potential.reshape(cols)
    other = lax.ppermute(column_potential, "core", swap)
    column_potential = jnp.where(
        core == 0,
        jnp.concatenate([column_potential, other]),
        jnp.concatenate([other, column_potential]),
    )
    row_potential = lax.dynamic_slice(row_potential.reshape(2 * rows), (core * own,), (own,))
    return (row_potential, column_potential)


def solution(mesh):
    fine = Mesh(mesh.devices.reshape(8, 2, 2, 2, 4), ("z", "p", "q", "core", "x"))
    return jax.shard_map(
        local,
        mesh=fine,
        in_specs=(P(("z", "p", "q", "core"), None), P("x", None)),
        out_specs=(P(("z", "p", "q", "core")), P("x")),
        check_vma=False,
    )
```

time: 128 us -> 136 us (1.062)
  blocking collectives: 103 us -> 83.1 us
  Pallas kernels: 15.4 us -> 33.2 us
  starting transfers between devices: 5.74 us -> 11.3 us
  waiting for transfers between devices: 0.2 us -> 5.08 us
    all_to_all x4 -> x3, blocking collectives: 67.3 us -> 34.4 us  [local(): columns = lax.all_to_all(parts, PLANE, 0, 0)]
    all_to_all x1, blocking collectives: 7.34 us -> 20.4 us  [local(): columns = lax.all_to_all(parts, FIRST_PLANE, 0, 0)]
    pallas_call x3, Pallas kernels: 2.09 us -> 12 us  [local(): pl.pallas_call(lambda *refs: later_columns(scale, col_bits, *refs), in_sp...]
    pallas_call x3, Pallas kernels: 8.03 us -> 13.6 us  [local(): pl.pallas_call(lambda *refs: later_rows(scale, row_bits, *refs), in_specs...]
    all_to_all x0 -> x1, starting transfers between devices: none -> 5.26 us  [local(): gathered = lax.all_to_all(parts, LINE, 0, 0)]
    all_to_all x0 -> x1, waiting for transfers between devices: none -> 4.88 us  [local(): gathered = lax.all_to_all(parts, LINE, 0, 0)]
    pallas_call x1 -> x3, Pallas kernels: 1.88 us -> 3.7 us  [the longest x1 1.86 us: local(): pl.pallas_call(lambda *refs: first_columns(scale, *refs), in_specs=[vmem]...]
    ppermute x1 -> x3, starting transfers between devices: 3.33 us -> 4.13 us  [the longest x1 3.65 us: local(): away = lax.ppermute(mine, ('p', 'q'), [(0, 3), (3, 0), (1, 2), (2, 1)])]
  transfers between devices with their start and end apart: 2 -> 5, of which waited for: 1 -> 2; matrix products, arithmetic and copies ran while one was open for 0% -> 0% of each run, Pallas kernels for 0% -> 1%
where the time goes in v5:
time: 136 us
  blocking collectives  83.1 us (61%)
  Pallas kernels  33.2 us (24%)
  starting transfers between devices  11.3 us (8%)
  waiting for transfers between devices  5.08 us (4%)
  local copies, waits for them, and re-layouts  1.53 us (1%)
    all_to_all x3, blocking collectives, local(): columns = lax.all_to_all(parts, PLANE, 0, 0)  34.4 us
    all_to_all x3, blocking collectives, local(): gathered = lax.all_to_all(parts, LINE, 0, 0)  28.4 us
    all_to_all x1, blocking collectives, local(): columns = lax.all_to_all(parts, FIRST_PLANE, 0, 0)  20.4 us
    pallas_call x3, Pallas kernels, local(): pl.pallas_call(lambda *refs: later_rows(scale, row_bits, *refs), in_specs...  13.6 us
    pallas_call x3, Pallas kernels, local(): pl.pallas_call(lambda *refs: later_columns(scale, col_bits, *refs), in_sp...  12 us
    all_to_all x1, starting transfers between devices, local(): gathered = lax.all_to_all(parts, LINE, 0, 0)  5.26 us
    all_to_all x1, waiting for transfers between devices, local(): gathered = lax.all_to_all(parts, LINE, 0, 0)  4.88 us
    pallas_call x1, Pallas kernels, local(): pl.pallas_call(lambda *refs: first_rows(scale, *refs), in_specs=[hbm, hbm...  3.87 us
  transfers between devices with their start and end apart: 5, of which 2 were waited for; matrix products, arithmetic and copies ran while one was open for 0% of the time, Pallas kernels for 1%

profile of v5, /device:TPU:1, one launch (start us, length us, event | category | flops | bytes accessed | tf_op | source)
XLA Modules:
  0.0 135.6 jit_solution(3175970925899243439)
XLA Ops:
  0.6 0.0 copy-start
  0.6 0.9 copy-done
  1.5 3.9 %first_rows.1 = (f32[8,2,128]{2,1,0:T(2,128)}, f32[256,256]{1,0:T(8,128)S(1)}, bf16[2048,256]{1,0:T(8,128)(2,1)S(1)}) custom-call(bf16[256,256]{1,0:T(8,128)(2,1)S(1)} %copy-done, bf16[4096,256]{1,0:T(8,128)(2,1)} %refs_1_.1), custom_call_target="tpu_custom_call" | custom-call | tf_op jit(solution)/shard_map/first_rows/pallas_call | solution.py:284
  5.4 3.6 %collective-permute-start = (f32[256,256]{1,0:T(8,128)S(1)}, f32[256,256]{1,0:T(8,128)S(1)}, u32[]{:S(2)}, u32[]{:S(2)}) collective-permute-start(f32[256,256]{1,0:T(8,128)S(1)} %get-tuple-element.20.refs_0_), channel_id=1, source_target_pairs={{0,24},{24,0},{8,16},{16,8},{1,25},{25,1},{9,17},{17,9},{2,26},{26... | collective-permute-start | bytes 786440 | tf_op jit(solution)/shard_map/ppermute | solution.py:305
  9.1 5.3 %all-to-all-start = ((f32[8,2,128]{2,1,0:T(2,128)}), f32[8,2,128]{2,1,0:T(2,128)S(1)}, u32[]{:S(2)}, u32[]{:S(2)}) async-start(f32[8,2,128]{2,1,0:T(2,128)} %get-tuple-element.19), calls=%async_computation | async-start | bytes 16384 | tf_op jit(solution)/shard_map/all_to_all | solution.py:306
  14.3 0.0 collective-permute-start.2
  14.3 4.9 %all-to-all-done.refs_0_ = f32[8,2,128]{2,1,0:T(2,128)S(1)} async-done(((f32[8,2,128]{2,1,0:T(2,128)}), f32[8,2,128]{2,1,0:T(2,128)S(1)}, u32[]{:S(2)}, u32[]{:S(2)}) %all-to-all-start) | async-done | bytes 8224 | tf_op jit(solution)/shard_map/all_to_all | solution.py:306
  19.2 0.0 collective-permute-done.refs_1_
  19.2 0.5 collective-permute-start.1
  19.7 0.0 collective-permute-done.2.refs_1_
  19.7 1.9 %first_columns.1 = (f32[16,128]{1,0:T(8,128)S(1)}, f32[512,2048]{1,0:T(8,128)S(1)}, f32[4,128]{1,0:T(4,128)S(1)}, f32[16,128]{1,0:T(8,128)S(1)}, bf16[512,256]{1,0:T(8,128)(2,1)S(1)}) custom-call(f32[256,256]{1,0:T(8,128)S(1)} %get-tuple-element.20.refs_0_, f32[256,256]{1,0:T(8,128)S(1)} %collective-permute-done.2.refs_1_, ...), custom_call_target="tpu_custom_call" | custom-call | tf_op jit(solution)/shard_map/first_columns/pallas_call | solution.py:315
  21.6 0.0 collective-permute-done.1.refs_1_
  21.6 1.8 %partner_rows.1 = (f32[32,16,128]{2,1,0:T(8,128)S(1)}, f32[512,2048]{1,0:T(8,128)S(1)}, f32[4,128]{1,0:T(4,128)S(1)}, f32[16,128]{1,0:T(8,128)S(1)}, bf16[512,256]{1,0:T(8,128)(2,1)S(1)}) custom-call(f32[256,256]{1,0:T(8,128)S(1)} %get-tuple-element.21.refs_0_, f32[256,256]{1,0:T(8,128)S(1)} %collective-permute-done.1.refs_1_, ...), custom_call_target="tpu_custom_call" | custom-call | tf_op jit(solution)/shard_map/partner_rows/pallas_call | solution.py:324
  23.4 20.4 %all_to_all.40.refs_0_ = f32[32,16,128]{2,1,0:T(8,128)S(1)} all-to-all(f32[32,16,128]{2,1,0:T(8,128)S(1)} %get-tuple-element.25), channel_id=1, replica_groups=mesh['z'=8,'p'=2,'q'=2,'core'=2,'x'=4] {'z','p','q'}, dimensions={0} | all-to-all | bytes 524288 | tf_op jit(solution)/shard_map/all_to_all | solution.py:332
  43.8 4.5 %later_rows.3 = f32[8,8,128]{2,1,0:T(8,128)S(1)} custom-call(f32[32,16,128]{2,1,0:T(8,128)S(1)} %all_to_all.40.refs_0_, bf16[2048,256]{1,0:T(8,128)(2,1)S(1)} %get-tuple-element.22.refs_2_.refs_1_, f32[512,2048]{1,0:T(8,128)S(1)} %get-tuple-element.26.refs_2_, f32[4,128]{1,0:T(4,128)S(1)} %get-tuple-element.27.refs_3_, ...), custom_call_target="tpu_custom_call" | custom-call | tf_op jit(solution)/shard_map/later_rows/pallas_call | solution.py:335
  48.3 10.1 %all_to_all.41.refs_0_ = f32[8,8,128]{2,1,0:T(8,128)S(1)} all-to-all(f32[8,8,128]{2,1,0:T(8,128)S(1)} %later_rows.3), channel_id=1, replica_groups=mesh['z'=8,'p'=2,'q'=2,'core'=2,'x'=4] {'core','x'}, dimensions={0} | all-to-all | bytes 65536 | tf_op jit(solution)/shard_map/all_to_all | solution.py:344
  58.4 4.1 %later_columns.3 = f32[16,16,128]{2,1,0:T(8,128)S(1)} custom-call(f32[8,8,128]{2,1,0:T(8,128)S(1)} %all_to_all.41.refs_0_, bf16[2048,256]{1,0:T(8,128)(2,1)S(1)} %get-tuple-element.22.refs_2_.refs_1_, f32[512,2048]{1,0:T(8,128)S(1)} %get-tuple-element.26.refs_2_, f32[4,128]{1,0:T(4,128)S(1)} %get-tuple-element.27.refs_3_, ...), custom_call_target="tpu_custom_call" | custom-call | tf_op jit(solution)/shard_map/later_columns/pallas_call | solution.py:345
  62.5 11.4 %all_to_all.42.refs_0_ = f32[16,16,128]{2,1,0:T(8,128)S(1)} all-to-all(f32[16,16,128]{2,1,0:T(8,128)S(1)} %later_columns.3), channel_id=1, replica_groups=mesh['z'=8,'p'=2,'q'=2,'core'=2,'x'=4] {'z','q'}, dimensions={0} | all-to-all | bytes 262144 | tf_op jit(solution)/shard_map/all_to_all | solution.py:354
  74.0 4.5 %later_rows.4 = f32[8,8,128]{2,1,0:T(8,128)S(1)} custom-call(f32[16,16,128]{2,1,0:T(8,128)S(1)} %all_to_all.42.refs_0_, bf16[2048,256]{1,0:T(8,128)(2,1)S(1)} %get-tuple-element.22.refs_2_.refs_1_, f32[512,2048]{1,0:T(8,128)S(1)} %get-tuple-element.26.refs_2_, f32[4,128]{1,0:T(4,128)S(1)} %get-tuple-element.27.refs_3_, ...), custom_call_target="tpu_custom_call" | custom-call | tf_op jit(solution)/shard_map/later_rows/pallas_call | solution.py:335
  78.4 9.1 %all_to_all.43.refs_0_ = f32[8,8,128]{2,1,0:T(8,128)S(1)} all-to-all(f32[8,8,128]{2,1,0:T(8,128)S(1)} %later_rows.4), channel_id=1, replica_groups=mesh['z'=8,'p'=2,'q'=2,'core'=2,'x'=4] {'core','x'}, dimensions={0} | all-to-all | bytes 65536 | tf_op jit(solution)/shard_map/all_to_all | solution.py:344
  87.6 3.9 %later_columns.4 = f32[16,16,128]{2,1,0:T(8,128)S(1)} custom-call(f32[8,8,128]{2,1,0:T(8,128)S(1)} %all_to_all.43.refs_0_, bf16[2048,256]{1,0:T(8,128)(2,1)S(1)} %get-tuple-element.22.refs_2_.refs_1_, f32[512,2048]{1,0:T(8,128)S(1)} %get-tuple-element.26.refs_2_, f32[4,128]{1,0:T(4,128)S(1)} %get-tuple-element.27.refs_3_, ...), custom_call_target="tpu_custom_call" | custom-call | tf_op jit(solution)/shard_map/later_columns/pallas_call | solution.py:345
  91.5 11.4 %all_to_all.44.refs_0_ = f32[16,16,128]{2,1,0:T(8,128)S(1)} all-to-all(f32[16,16,128]{2,1,0:T(8,128)S(1)} %later_columns.4), channel_id=1, replica_groups=mesh['z'=8,'p'=2,'q'=2,'core'=2,'x'=4] {'z','q'}, dimensions={0} | all-to-all | bytes 262144 | tf_op jit(solution)/shard_map/all_to_all | solution.py:354
  103.0 4.7 %later_rows.5 = f32[8,8,128]{2,1,0:T(8,128)S(1)} custom-call(f32[16,16,128]{2,1,0:T(8,128)S(1)} %all_to_all.44.refs_0_, bf16[2048,256]{1,0:T(8,128)(2,1)S(1)} %get-tuple-element.22.refs_2_.refs_1_, f32[512,2048]{1,0:T(8,128)S(1)} %get-tuple-element.26.refs_2_, f32[4,128]{1,0:T(4,128)S(1)} %get-tuple-element.27.refs_3_, ...), custom_call_target="tpu_custom_call" | custom-call | tf_op jit(solution)/shard_map/later_rows/pallas_call | solution.py:335
  107.6 9.1 %all_to_all.45.refs_0_ = f32[8,8,128]{2,1,0:T(8,128)S(1)} all-to-all(f32[8,8,128]{2,1,0:T(8,128)S(1)} %later_rows.5), channel_id=1, replica_groups=mesh['z'=8,'p'=2,'q'=2,'core'=2,'x'=4] {'core','x'}, dimensions={0} | all-to-all | bytes 65536 | tf_op jit(solution)/shard_map/all_to_all | solution.py:344
  116.8 3.9 %later_columns.5 = f32[16,16,128]{2,1,0:T(8,128)S(1)} custom-call(f32[8,8,128]{2,1,0:T(8,128)S(1)} %all_to_all.45.refs_0_, bf16[2048,256]{1,0:T(8,128)(2,1)S(1)} %get-tuple-element.22.refs_2_.refs_1_, f32[512,2048]{1,0:T(8,128)S(1)} %get-tuple-element.26.refs_2_, f32[4,128]{1,0:T(4,128)S(1)} %get-tuple-element.27.refs_3_, ...), custom_call_target="tpu_custom_call" | custom-call | tf_op jit(solution)/shard_map/later_columns/pallas_call | solution.py:345
  120.7 11.4 %all_to_all.46.refs_1_ = f32[16,16,128]{2,1,0:T(8,128)S(1)} all-to-all(f32[16,16,128]{2,1,0:T(8,128)S(1)} %later_columns.5), channel_id=1, replica_groups=mesh['z'=8,'p'=2,'q'=2,'core'=2,'x'=4] {'z','q'}, dimensions={0} | all-to-all | bytes 262144 | tf_op jit(solution)/shard_map/all_to_all | solution.py:354
  132.2 1.9 %collective-permute-start.3 = (f32[2048]{0:T(1024)S(1)}, f32[2048]{0:T(1024)S(1)}, u32[]{:S(2)}, u32[]{:S(2)}) collective-permute-start(f32[2048]{0:T(1024)S(1)} %bitcast.2), channel_id=1, source_target_pairs={{0,4},{4,0},{1,5},{5,1},{2,6},{6,2},{3,7},{7,3},{8,12},{12,8},{9,1... | collective-permute-start | bytes 24584 | tf_op jit(solution)/shard_map/ppermute | solution.py:365
  134.2 0.6 dynamic_slice.3
  134.8 0.2 collective-permute-done.3
  135.0 0.6 maximum_select_fusion
  (2 shorter events, 0.1 us)
Async XLA Ops:
  0.6 0.9 copy-start
  5.4 13.8 %collective-permute-start = (f32[256,256]{1,0:T(8,128)S(1)}, f32[256,256]{1,0:T(8,128)S(1)}, u32[]{:S(2)}, u32[]{:S(2)}) collective-permute-start(f32[256,256]{1,0:T(8,128)S(1)} %get-tuple-element.20.refs_0_), channel_id=1, source_target_pairs={{0,24},{24,0},{8,16},{16,8},{1,25},{25,1},{9,17},{17,9},{2,26},{26... | collective-permute-start | bytes 786440 | tf_op jit(solution)/shard_map/ppermute | solution.py:305
  9.1 10.1 %all-to-all-start = ((f32[8,2,128]{2,1,0:T(2,128)}), f32[8,2,128]{2,1,0:T(2,128)S(1)}, u32[]{:S(2)}, u32[]{:S(2)}) async-start(f32[8,2,128]{2,1,0:T(2,128)} %get-tuple-element.19), calls=%async_computation | async-start | bytes 16384 | tf_op jit(solution)/shard_map/all_to_all | solution.py:306
  14.3 5.4 %collective-permute-start.2 = (f32[256,256]{1,0:T(8,128)S(1)}, f32[256,256]{1,0:T(8,128)S(1)}, u32[]{:S(2)}, u32[]{:S(2)}) collective-permute-start(f32[256,256]{1,0:T(8,128)S(1)} %get-tuple-element.20.refs_0_), channel_id=1, source_target_pairs={{0,4},{4,0},{1,5},{5,1},{2,6},{6,2},{3,7},{7,3},{8,12},{12,8},{9,1... | collective-permute-start | bytes 786440 | tf_op jit(solution)/shard_map/ppermute | solution.py:304
  19.2 2.3 %collective-permute-start.1 = (f32[256,256]{1,0:T(8,128)S(1)}, f32[256,256]{1,0:T(8,128)S(1)}, u32[]{:S(2)}, u32[]{:S(2)}) collective-permute-start(f32[256,256]{1,0:T(8,128)S(1)} %get-tuple-element.21.refs_0_), channel_id=1, source_target_pairs={{0,4},{4,0},{1,5},{5,1},{2,6},{6,2},{3,7},{7,3},{8,12},{12,8},{9,1... | collective-permute-start | bytes 786440 | tf_op jit(solution)/shard_map/ppermute | solution.py:331
  132.2 2.8 %collective-permute-start.3 = (f32[2048]{0:T(1024)S(1)}, f32[2048]{0:T(1024)S(1)}, u32[]{:S(2)}, u32[]{:S(2)}) collective-permute-start(f32[2048]{0:T(1024)S(1)} %bitcast.2), channel_id=1, source_target_pairs={{0,4},{4,0},{1,5},{5,1},{2,6},{6,2},{3,7},{7,3},{8,12},{12,8},{9,1... | collective-permute-start | bytes 24584 | tf_op jit(solution)/shard_map/ppermute | solution.py:365

commit v6 on v5

--- a/solution.py
+++ b/solution.py
@@ -12,7 +12,6 @@
 TILE = 256
 LANES = 128
 SUBLANES = 8
-CHUNKS = 2
 SAFE = 2.0**-80
 
 FIRST_PLANE = ("z", "p", "q")
@@ -59,33 +58,26 @@
     )
 
 
-def first_rows(
-    scale, source_ref, target_ref, out_ref, wide_ref, half_ref, source, rest, scores, peaks, line, arrived
-):
+def fetch(target_ref, half_ref, rest_ref, arrived):
     core = lax.axis_index("core")
-    rows, half = source.shape[0], half_ref.shape[0]
-    chunk = half // CHUNKS
-    fetch = pltpu.make_async_copy(source_ref, source, arrived.at[2 * CHUNKS])
-    fetch.start()
-    copies = []
-    for side, place in ((core, half_ref), (1 - core, rest)):
-        for k in range(CHUNKS):
-            copies.append(
-                pltpu.make_async_copy(
-                    target_ref.at[pl.ds(pl.multiple_of(side * half + k * chunk, chunk), chunk)],
-                    place.at[pl.ds(k * chunk, chunk)],
-                    arrived.at[len(copies)],
-                )
-            )
-            copies[-1].start()
-    fetch.wait()
-    wide_ref[...] = source[...].astype(jnp.float32)
+    half = half_ref.shape[0]
+    copies = [
+        pltpu.make_async_copy(target_ref.at[pl.ds(pl.multiple_of(side * half, half), half)], place, arrived.at[k])
+        for k, (side, place) in enumerate(((core, half_ref), (1 - core, rest_ref)))
+    ]
+    for copy in copies:
+        copy.start()
+    for copy in copies:
+        copy.wait()
+
+
+def first_rows(scale, source_ref, half_ref, rest_ref, out_ref, wide_ref, scores, peaks, line):
+    rows, half = source_ref.shape[0], half_ref.shape[0]
+    wide_ref[...] = source_ref[...].astype(jnp.float32)
     for start in range(0, 2 * half, TILE):
-        if start % chunk == 0:
-            copies[start // chunk].wait()
-        place = half_ref if start < half else rest
+        place = half_ref if start < half else rest_ref
         tile = slice(start, start + TILE)
-        part = score(source[...], place[start % half : start % half + TILE, :], scale)
+        part = score(source_ref[...], place[start % half : start % half + TILE, :], scale)
         scores[:, tile] = part
         high = part[:, :LANES]
         for lane in range(LANES, TILE, LANES):
@@ -167,9 +159,8 @@
 
 
 def partner_rows(
-    scale, mine_ref, other_ref, half_ref, columns_ref, out_ref, plan_ref, row_ref, peak_ref, source_ref
+    scale, mine_ref, other_ref, half_ref, plan_ref, row_ref, peak_ref, source_ref
 ):
-    send(out_ref, columns_ref[...])
     place(source_ref, mine_ref, other_ref)
     row_ref[...] = jnp.zeros_like(row_ref)
     peak, _ = exponentials(scale, source_ref, half_ref, plan_ref, None)
@@ -212,18 +203,18 @@
         send(out_ref, totals[...])
 
 
-def later_columns(scale, bits, gathered_ref, half_ref, *refs):
-    blocks, (out_ref, standing, folded) = (refs[:4], refs[4:8]), refs[8:]
-    potential = bits - combine(gathered_ref[...])
+def scaled_columns(scale, potential, start_from, half_ref, blocks, out_ref, standing, folded):
+    rows, cols = blocks[0][0].shape
+    count = rows // LANES
     low = None
-    results = []
+    results = list(start_from)
     for index, (plan_ref, row_ref, peak_ref, _) in enumerate(blocks):
-        rows, cols = plan_ref.shape
-        count = cols // LANES
-        change = potential[index * rows // LANES : (index + 1) * rows // LANES] - row_ref[...]
+        change = potential[index * count : (index + 1) * count] - row_ref[...]
         shift = largest(change)
         stand(standing, jnp.exp2(change - shift))
-        total = column_sums(rows, cols, lambda block: plan_ref[block, :] * spread(standing[block, :], count))
+        total = column_sums(
+            rows, cols, lambda block: plan_ref[block, :] * spread(standing[block, :], cols // LANES)
+        )
         total = fold(folded, total)
         low = total if low is None else jnp.minimum(low, total)
         results.append(peak_ref[...] + shift + jnp.log2(total))
@@ -231,11 +222,10 @@
 
     @pl.when(jnp.logical_not(smallest(low)[0, 0] >= SAFE))
     def _():
-        for start in range(0, half_ref.shape[0], TILE):
+        for start in range(0, cols, TILE):
             results = []
-            for index, (plan_ref, _, _, source_ref) in enumerate(blocks):
-                rows = plan_ref.shape[0]
-                stand(standing, potential[index * rows // LANES : (index + 1) * rows // LANES])
+            for index, (_, _, _, source_ref) in enumerate(blocks):
+                stand(standing, potential[index * count : (index + 1) * count])
                 part = score(source_ref[...], half_ref[start : start + TILE, :], scale) + spread(
                     standing[...], TILE // LANES
                 )
@@ -245,7 +235,16 @@
             for lane in range(0, TILE, LANES):
                 t = (start + lane) // LANES
                 folded[t : t + 1, :] = result[:, lane : lane + LANES]
-        send(out_ref, folded[...])
+        send(out_ref, combine(jnp.stack(list(start_from) + [folded[...]])))
+
+
+def partner_columns(scale, columns_ref, potential_ref, half_ref, *refs):
+    scaled_columns(scale, potential_ref[...], [columns_ref[...]], half_ref, (refs[:4],), *refs[4:])
+
+
+def later_columns(scale, bits, gathered_ref, half_ref, *refs):
+    potential = bits - combine(gathered_ref[...])
+    scaled_columns(scale, potential, [], half_ref, (refs[:4], refs[4:8]), *refs[8:])
 
 
 def finish(unit, row_bits, col_bits, row_parts_ref, column_parts_ref, row_ref, column_ref):
@@ -268,6 +267,7 @@
     unit = EPSILON * math.log(2.0)
     core = lax.axis_index("core")
     swap = [(0, 1), (1, 0)]
+    partner = [(0, 3), (3, 0), (1, 2), (2, 1)]
     vmem = pl.BlockSpec(memory_space=pltpu.VMEM)
     hbm = pl.BlockSpec(memory_space=pltpu.HBM)
     chip_shape = (rows // LANES, LANES)
@@ -281,28 +281,33 @@
         jax.ShapeDtypeStruct((rows, width), source.dtype),
     ]
 
-    parts, mine, half = pl.pallas_call(
+    half, rest = pl.pallas_call(
+        fetch,
+        in_specs=[hbm],
+        out_specs=[vmem] * 2,
+        out_shape=[jax.ShapeDtypeStruct((cols, width), target.dtype)] * 2,
+        scratch_shapes=[pltpu.SemaphoreType.DMA((2,))],
+        compiler_params=pltpu.CompilerParams(vmem_limit_bytes=51 * 2**20),
+        name="fetch",
+    )(target)
+    parts, mine = pl.pallas_call(
         lambda *refs: first_rows(scale, *refs),
-        in_specs=[hbm, hbm],
-        out_specs=[vmem] * 3,
+        in_specs=[vmem] * 3,
+        out_specs=[vmem] * 2,
         out_shape=[
             jax.ShapeDtypeStruct((line, own // LANES, LANES), f32),
             jax.ShapeDtypeStruct((own, width), f32),
-            jax.ShapeDtypeStruct((cols, width), target.dtype),
         ],
         scratch_shapes=[
-            pltpu.VMEM(source.shape, source.dtype),
-            pltpu.VMEM((cols, width), target.dtype),
             pltpu.VMEM((own, target.shape[0]), f32),
             pltpu.VMEM((own, LANES), f32),
             pltpu.VMEM((own // LANES, LANES), f32),
-            pltpu.SemaphoreType.DMA((2 * CHUNKS + 1,)),
         ],
-        compiler_params=pltpu.CompilerParams(vmem_limit_bytes=52 * 2**20),
+        compiler_params=limit,
         name="first_rows",
-    )(source, target)
+    )(source, half, rest)
     other = lax.ppermute(mine, "core", swap)
-    away = lax.ppermute(mine, ("p", "q"), [(0, 3), (3, 0), (1, 2), (2, 1)])
+    away = lax.ppermute(mine, ("p", "q"), partner)
     gathered = lax.all_to_all(parts, LINE, 0, 0)
     potential, away = pl.pallas_call(
         lambda *refs: first_potential(col_bits, *refs),
@@ -312,6 +317,7 @@
         compiler_params=limit,
         name="first_potential",
     )(gathered, away)
+    away_potential = lax.ppermute(potential, ("p", "q"), partner)
     columns, *mine_block = pl.pallas_call(
         lambda *refs: first_columns(scale, *refs),
         in_specs=[vmem] * 4,
@@ -321,15 +327,26 @@
         compiler_params=limit,
         name="first_columns",
     )(mine, other, half, potential)
-    parts, *away_block = pl.pallas_call(
+    away_block = pl.pallas_call(
         lambda *refs: partner_rows(scale, *refs),
-        in_specs=[vmem] * 4,
-        out_specs=[vmem] * 5,
-        out_shape=[jax.ShapeDtypeStruct((first_plane,) + col_shape, f32)] + block_out,
+        in_specs=[vmem] * 3,
+        out_specs=[vmem] * 4,
+        out_shape=block_out,
         compiler_params=limit,
         name="partner_rows",
-    )(away, lax.ppermute(away, "core", swap), half, columns)
-    columns = lax.all_to_all(parts, FIRST_PLANE, 0, 0)
+    )(away, lax.ppermute(away, "core", swap), half)
+    column_out = jax.ShapeDtypeStruct((plane,) + col_shape, f32)
+    column_scratch = [pltpu.VMEM((rows, LANES), f32), pltpu.VMEM(col_shape, f32)]
+    parts = pl.pallas_call(
+        lambda *refs: partner_columns(scale, *refs),
+        in_specs=[vmem] * 7,
+        out_specs=vmem,
+        out_shape=column_out,
+        scratch_shapes=column_scratch,
+        compiler_params=limit,
+        name="partner_columns",
+    )(columns, away_potential, half, *away_block)
+    columns = lax.all_to_all(parts, PLANE, 0, 0)
 
     for step in range(1, ITERS):
         parts = pl.pallas_call(
@@ -346,8 +363,8 @@
             lambda *refs: later_columns(scale, col_bits, *refs),
             in_specs=[vmem] * 10,
             out_specs=vmem,
-            out_shape=jax.ShapeDtypeStruct((plane,) + col_shape, f32),
-            scratch_shapes=[pltpu.VMEM((rows, LANES), f32), pltpu.VMEM(col_shape, f32)],
+            out_shape=column_out,
+            scratch_shapes=column_scratch,
             compiler_params=limit,
             name="later_columns",
         )(gathered, half, *mine_block, *away_block)

time: 136 us -> 134 us (0.985)
  blocking collectives: 83.1 us -> 79 us
  Pallas kernels: 33.2 us -> 35.1 us
    all_to_all x1 -> x0, blocking collectives: 20.4 us -> none  [local(): columns = lax.all_to_all(parts, FIRST_PLANE, 0, 0)]
    all_to_all x3 -> x4, blocking collectives: 34.4 us -> 50.3 us  [local(): columns = lax.all_to_all(parts, PLANE, 0, 0)]
    pallas_call x1 -> x3, Pallas kernels: 3.87 us -> 5.86 us  [the longest x1 2.18 us: local(): pl.pallas_call(lambda *refs: first_rows(scale, *refs), in_specs=[vmem] *...]
    ppermute x1 -> x2, starting transfers between devices: 3.65 us -> 4.19 us  [the longest x1 3.57 us: local(): away = lax.ppermute(mine, ('p', 'q'), partner)]
  transfers between devices with their start and end apart: 5 -> 6, of which waited for: 2 -> 2; matrix products, arithmetic and copies ran while one was open for 0% -> 0% of each run, Pallas kernels for 1% -> 3%
where the time goes in v6:
time: 134 us
  blocking collectives  79 us (59%)
  Pallas kernels  35.1 us (26%)
  starting transfers between devices  11.9 us (9%)
  waiting for transfers between devices  5.09 us (4%)
  local copies, waits for them, and re-layouts  1.53 us (1%)
    all_to_all x4, blocking collectives, local(): columns = lax.all_to_all(parts, PLANE, 0, 0)  50.3 us
    all_to_all x3, blocking collectives, local(): gathered = lax.all_to_all(parts, LINE, 0, 0)  28.7 us
    pallas_call x3, Pallas kernels, local(): pl.pallas_call(lambda *refs: later_rows(scale, row_bits, *refs), in_specs...  13.5 us
    pallas_call x3, Pallas kernels, local(): pl.pallas_call(lambda *refs: later_columns(scale, col_bits, *refs), in_sp...  12 us
    all_to_all x1, starting transfers between devices, local(): gathered = lax.all_to_all(parts, LINE, 0, 0)  5.25 us
    all_to_all x1, waiting for transfers between devices, local(): gathered = lax.all_to_all(parts, LINE, 0, 0)  4.88 us
    ppermute x1, starting transfers between devices, local(): away = lax.ppermute(mine, ('p', 'q'), partner)  3.57 us
  transfers between devices with their start and end apart: 6, of which 2 were waited for; matrix products, arithmetic and copies ran while one was open for 0% of the time, Pallas kernels for 3%

profile of v6, /device:TPU:1, one launch (start us, length us, event | category | flops | bytes accessed | tf_op | source)
XLA Modules:
  0.0 134.0 jit_solution(12804948971549915705)
XLA Ops:
  0.6 1.6 %fetch.1 = (bf16[2048,256]{1,0:T(8,128)(2,1)S(1)}, bf16[2048,256]{1,0:T(8,128)(2,1)S(1)}) custom-call(bf16[4096,256]{1,0:T(8,128)(2,1)} %target_ref.1), custom_call_target="tpu_custom_call" | custom-call | tf_op jit(solution)/shard_map/fetch/pallas_call | solution.py:284
  2.2 0.0 copy-start
  2.2 0.9 copy-done
  3.1 2.2 %first_rows.1 = (f32[8,2,128]{2,1,0:T(2,128)}, f32[256,256]{1,0:T(8,128)S(1)}) custom-call(bf16[256,256]{1,0:T(8,128)(2,1)S(1)} %copy-done, bf16[2048,256]{1,0:T(8,128)(2,1)S(1)} %get-tuple-element.19.refs_1_.refs_2_, bf16[2048,256]{1,0:T(8,128)(2,1)S(1)} %get-tuple-element.20.refs_2_), custom_call_target="tpu_custom_call" | custom-call | tf_op jit(solution)/shard_map/first_rows/pallas_call | solution.py:293
  5.3 3.6 %collective-permute-start.1 = (f32[256,256]{1,0:T(8,128)S(1)}, f32[256,256]{1,0:T(8,128)S(1)}, u32[]{:S(2)}, u32[]{:S(2)}) collective-permute-start(f32[256,256]{1,0:T(8,128)S(1)} %get-tuple-element.21.refs_0_), channel_id=1, source_target_pairs={{0,24},{24,0},{8,16},{16,8},{1,25},{25,1},{9,17},{17,9},{2,26},{26... | collective-permute-start | bytes 786440 | tf_op jit(solution)/shard_map/ppermute | solution.py:310
  8.9 5.3 %all-to-all-start = ((f32[8,2,128]{2,1,0:T(2,128)}), f32[8,2,128]{2,1,0:T(2,128)S(1)}, u32[]{:S(2)}, u32[]{:S(2)}) async-start(f32[8,2,128]{2,1,0:T(2,128)} %get-tuple-element.22), calls=%async_computation | async-start | bytes 16384 | tf_op jit(solution)/shard_map/all_to_all | solution.py:311
  14.1 0.0 collective-permute-start
  14.1 4.9 %all-to-all-done.refs_0_ = f32[8,2,128]{2,1,0:T(2,128)S(1)} async-done(((f32[8,2,128]{2,1,0:T(2,128)}), f32[8,2,128]{2,1,0:T(2,128)S(1)}, u32[]{:S(2)}, u32[]{:S(2)}) %all-to-all-start) | async-done | bytes 8224 | tf_op jit(solution)/shard_map/all_to_all | solution.py:311
  19.0 0.0 collective-permute-done.1.refs_1_
  19.0 0.5 collective-permute-start.3
  19.5 0.6 collective-permute-start.2
  20.2 0.0 collective-permute-done.refs_1_
  20.2 1.9 %first_columns.1 = (f32[16,128]{1,0:T(8,128)S(1)}, f32[512,2048]{1,0:T(8,128)S(1)}, f32[4,128]{1,0:T(4,128)S(1)}, f32[16,128]{1,0:T(8,128)S(1)}, bf16[512,256]{1,0:T(8,128)(2,1)S(1)}) custom-call(f32[256,256]{1,0:T(8,128)S(1)} %get-tuple-element.21.refs_0_, f32[256,256]{1,0:T(8,128)S(1)} %collective-permute-done.refs_1_, ...), custom_call_target="tpu_custom_call" | custom-call | tf_op jit(solution)/shard_map/first_columns/pallas_call | solution.py:321
  22.0 0.0 collective-permute-done.3.refs_1_
  22.0 1.8 %partner_rows.1 = (f32[512,2048]{1,0:T(8,128)S(1)}, f32[4,128]{1,0:T(4,128)S(1)}, f32[16,128]{1,0:T(8,128)S(1)}, bf16[512,256]{1,0:T(8,128)(2,1)S(1)}) custom-call(f32[256,256]{1,0:T(8,128)S(1)} %get-tuple-element.25.refs_0_, f32[256,256]{1,0:T(8,128)S(1)} %collective-permute-done.3.refs_1_, bf16[2048,256]{1,0:T(8,128)(2,1)S(1)} %get-tuple-element.19.refs_1_.refs_2_), custom_call_target="tpu_custom_call" | custom-call | tf_op jit(solution)/shard_map/partner_rows/pallas_call | solution.py:330
  23.9 0.0 collective-permute-done.2.refs_1_
  23.9 2.1 %partner_columns.1 = f32[16,16,128]{2,1,0:T(8,128)S(1)} custom-call(f32[16,128]{1,0:T(8,128)S(1)} %get-tuple-element.24.refs_0_, f32[4,128]{1,0:T(4,128)S(1)} %collective-permute-done.2.refs_1_, bf16[2048,256]{1,0:T(8,128)(2,1)S(1)} %get-tuple-element.19.refs_1_.refs_2_, f32[512,2048]{1,0:T(8,128)S(1)} %get-tuple-element.26.refs_3_.refs_6_, ...), custom_call_target="tpu_custom_call" | custom-call | tf_op jit(solution)/shard_map/partner_columns/pallas_call | solution.py:340
  26.0 15.9 %all_to_all.40.refs_0_ = f32[16,16,128]{2,1,0:T(8,128)S(1)} all-to-all(f32[16,16,128]{2,1,0:T(8,128)S(1)} %partner_columns.1), channel_id=1, replica_groups=mesh['z'=8,'p'=2,'q'=2,'core'=2,'x'=4] {'z','q'}, dimensions={0} | all-to-all | bytes 262144 | tf_op jit(solution)/shard_map/all_to_all | solution.py:349
  41.9 4.4 %later_rows.3 = f32[8,8,128]{2,1,0:T(8,128)S(1)} custom-call(f32[16,16,128]{2,1,0:T(8,128)S(1)} %all_to_all.40.refs_0_, bf16[2048,256]{1,0:T(8,128)(2,1)S(1)} %get-tuple-element.19.refs_1_.refs_2_, f32[512,2048]{1,0:T(8,128)S(1)} %get-tuple-element.30.refs_2_, f32[4,128]{1,0:T(4,128)S(1)} %get-tuple-element.31.refs_3_, ...), custom_call_target="tpu_custom_call" | custom-call | tf_op jit(solution)/shard_map/later_rows/pallas_call | solution.py:352
  46.3 10.5 %all_to_all.41.refs_0_ = f32[8,8,128]{2,1,0:T(8,128)S(1)} all-to-all(f32[8,8,128]{2,1,0:T(8,128)S(1)} %later_rows.3), channel_id=1, replica_groups=mesh['z'=8,'p'=2,'q'=2,'core'=2,'x'=4] {'core','x'}, dimensions={0} | all-to-all | bytes 65536 | tf_op jit(solution)/shard_map/all_to_all | solution.py:361
  56.8 4.1 %later_columns.3 = f32[16,16,128]{2,1,0:T(8,128)S(1)} custom-call(f32[8,8,128]{2,1,0:T(8,128)S(1)} %all_to_all.41.refs_0_, bf16[2048,256]{1,0:T(8,128)(2,1)S(1)} %get-tuple-element.19.refs_1_.refs_2_, f32[512,2048]{1,0:T(8,128)S(1)} %get-tuple-element.30.refs_2_, f32[4,128]{1,0:T(4,128)S(1)} %get-tuple-element.31.refs_3_, ...), custom_call_target="tpu_custom_call" | custom-call | tf_op jit(solution)/shard_map/later_columns/pallas_call | solution.py:362
  60.9 11.5 %all_to_all.42.refs_0_ = f32[16,16,128]{2,1,0:T(8,128)S(1)} all-to-all(f32[16,16,128]{2,1,0:T(8,128)S(1)} %later_columns.3), channel_id=1, replica_groups=mesh['z'=8,'p'=2,'q'=2,'core'=2,'x'=4] {'z','q'}, dimensions={0} | all-to-all | bytes 262144 | tf_op jit(solution)/shard_map/all_to_all | solution.py:371
  72.4 4.4 %later_rows.4 = f32[8,8,128]{2,1,0:T(8,128)S(1)} custom-call(f32[16,16,128]{2,1,0:T(8,128)S(1)} %all_to_all.42.refs_0_, bf16[2048,256]{1,0:T(8,128)(2,1)S(1)} %get-tuple-element.19.refs_1_.refs_2_, f32[512,2048]{1,0:T(8,128)S(1)} %get-tuple-element.30.refs_2_, f32[4,128]{1,0:T(4,128)S(1)} %get-tuple-element.31.refs_3_, ...), custom_call_target="tpu_custom_call" | custom-call | tf_op jit(solution)/shard_map/later_rows/pallas_call | solution.py:352
  76.8 9.1 %all_to_all.43.refs_0_ = f32[8,8,128]{2,1,0:T(8,128)S(1)} all-to-all(f32[8,8,128]{2,1,0:T(8,128)S(1)} %later_rows.4), channel_id=1, replica_groups=mesh['z'=8,'p'=2,'q'=2,'core'=2,'x'=4] {'core','x'}, dimensions={0} | all-to-all | bytes 65536 | tf_op jit(solution)/shard_map/all_to_all | solution.py:361
  86.0 3.9 %later_columns.4 = f32[16,16,128]{2,1,0:T(8,128)S(1)} custom-call(f32[8,8,128]{2,1,0:T(8,128)S(1)} %all_to_all.43.refs_0_, bf16[2048,256]{1,0:T(8,128)(2,1)S(1)} %get-tuple-element.19.refs_1_.refs_2_, f32[512,2048]{1,0:T(8,128)S(1)} %get-tuple-element.30.refs_2_, f32[4,128]{1,0:T(4,128)S(1)} %get-tuple-element.31.refs_3_, ...), custom_call_target="tpu_custom_call" | custom-call | tf_op jit(solution)/shard_map/later_columns/pallas_call | solution.py:362
  89.9 11.5 %all_to_all.44.refs_0_ = f32[16,16,128]{2,1,0:T(8,128)S(1)} all-to-all(f32[16,16,128]{2,1,0:T(8,128)S(1)} %later_columns.4), channel_id=1, replica_groups=mesh['z'=8,'p'=2,'q'=2,'core'=2,'x'=4] {'z','q'}, dimensions={0} | all-to-all | bytes 262144 | tf_op jit(solution)/shard_map/all_to_all | solution.py:371
  101.4 4.6 %later_rows.5 = f32[8,8,128]{2,1,0:T(8,128)S(1)} custom-call(f32[16,16,128]{2,1,0:T(8,128)S(1)} %all_to_all.44.refs_0_, bf16[2048,256]{1,0:T(8,128)(2,1)S(1)} %get-tuple-element.19.refs_1_.refs_2_, f32[512,2048]{1,0:T(8,128)S(1)} %get-tuple-element.30.refs_2_, f32[4,128]{1,0:T(4,128)S(1)} %get-tuple-element.31.refs_3_, ...), custom_call_target="tpu_custom_call" | custom-call | tf_op jit(solution)/shard_map/later_rows/pallas_call | solution.py:352
  106.0 9.1 %all_to_all.45.refs_0_ = f32[8,8,128]{2,1,0:T(8,128)S(1)} all-to-all(f32[8,8,128]{2,1,0:T(8,128)S(1)} %later_rows.5), channel_id=1, replica_groups=mesh['z'=8,'p'=2,'q'=2,'core'=2,'x'=4] {'core','x'}, dimensions={0} | all-to-all | bytes 65536 | tf_op jit(solution)/shard_map/all_to_all | solution.py:361
  115.1 3.9 %later_columns.5 = f32[16,16,128]{2,1,0:T(8,128)S(1)} custom-call(f32[8,8,128]{2,1,0:T(8,128)S(1)} %all_to_all.45.refs_0_, bf16[2048,256]{1,0:T(8,128)(2,1)S(1)} %get-tuple-element.19.refs_1_.refs_2_, f32[512,2048]{1,0:T(8,128)S(1)} %get-tuple-element.30.refs_2_, f32[4,128]{1,0:T(4,128)S(1)} %get-tuple-element.31.refs_3_, ...), custom_call_target="tpu_custom_call" | custom-call | tf_op jit(solution)/shard_map/later_columns/pallas_call | solution.py:362
  119.1 11.5 %all_to_all.46.refs_1_ = f32[16,16,128]{2,1,0:T(8,128)S(1)} all-to-all(f32[16,16,128]{2,1,0:T(8,128)S(1)} %later_columns.5), channel_id=1, replica_groups=mesh['z'=8,'p'=2,'q'=2,'core'=2,'x'=4] {'z','q'}, dimensions={0} | all-to-all | bytes 262144 | tf_op jit(solution)/shard_map/all_to_all | solution.py:371
  130.6 1.9 %collective-permute-start.4 = (f32[2048]{0:T(1024)S(1)}, f32[2048]{0:T(1024)S(1)}, u32[]{:S(2)}, u32[]{:S(2)}) collective-permute-start(f32[2048]{0:T(1024)S(1)} %bitcast.2), channel_id=1, source_target_pairs={{0,4},{4,0},{1,5},{5,1},{2,6},{6,2},{3,7},{7,3},{8,12},{12,8},{9,1... | collective-permute-start | bytes 24584 | tf_op jit(solution)/shard_map/ppermute | solution.py:382
  132.5 0.6 dynamic_slice.3
  133.2 0.2 collective-permute-done.4
  133.4 0.6 maximum_select_fusion
  (2 shorter events, 0.1 us)
Async XLA Ops:
  2.2 0.9 copy-start
  5.3 13.7 %collective-permute-start.1 = (f32[256,256]{1,0:T(8,128)S(1)}, f32[256,256]{1,0:T(8,128)S(1)}, u32[]{:S(2)}, u32[]{:S(2)}) collective-permute-start(f32[256,256]{1,0:T(8,128)S(1)} %get-tuple-element.21.refs_0_), channel_id=1, source_target_pairs={{0,24},{24,0},{8,16},{16,8},{1,25},{25,1},{9,17},{17,9},{2,26},{26... | collective-permute-start | bytes 786440 | tf_op jit(solution)/shard_map/ppermute | solution.py:310
  8.9 10.1 %all-to-all-start = ((f32[8,2,128]{2,1,0:T(2,128)}), f32[8,2,128]{2,1,0:T(2,128)S(1)}, u32[]{:S(2)}, u32[]{:S(2)}) async-start(f32[8,2,128]{2,1,0:T(2,128)} %get-tuple-element.22), calls=%async_computation | async-start | bytes 16384 | tf_op jit(solution)/shard_map/all_to_all | solution.py:311
  14.1 6.0 %collective-permute-start = (f32[256,256]{1,0:T(8,128)S(1)}, f32[256,256]{1,0:T(8,128)S(1)}, u32[]{:S(2)}, u32[]{:S(2)}) collective-permute-start(f32[256,256]{1,0:T(8,128)S(1)} %get-tuple-element.21.refs_0_), channel_id=1, source_target_pairs={{0,4},{4,0},{1,5},{5,1},{2,6},{6,2},{3,7},{7,3},{8,12},{12,8},{9,1... | collective-permute-start | bytes 786440 | tf_op jit(solution)/shard_map/ppermute | solution.py:309
  19.0 3.0 %collective-permute-start.3 = (f32[256,256]{1,0:T(8,128)S(1)}, f32[256,256]{1,0:T(8,128)S(1)}, u32[]{:S(2)}, u32[]{:S(2)}) collective-permute-start(f32[256,256]{1,0:T(8,128)S(1)} %get-tuple-element.25.refs_0_), channel_id=1, source_target_pairs={{0,4},{4,0},{1,5},{5,1},{2,6},{6,2},{3,7},{7,3},{8,12},{12,8},{9,1... | collective-permute-start | bytes 786440 | tf_op jit(solution)/shard_map/ppermute | solution.py:337
  19.5 4.3 %collective-permute-start.2 = (f32[4,128]{1,0:T(4,128)S(1)}, f32[4,128]{1,0:T(4,128)S(1)}, u32[]{:S(2)}, u32[]{:S(2)}) collective-permute-start(f32[4,128]{1,0:T(4,128)S(1)} %get-tuple-element.23.refs_3_), channel_id=1, source_target_pairs={{0,24},{24,0},{8,16},{16,8},{1,25},{25,1},{9,17},{17,9},{2,26},{26... | collective-permute-start | bytes 6152 | tf_op jit(solution)/shard_map/ppermute | solution.py:320
  130.6 2.8 %collective-permute-start.4 = (f32[2048]{0:T(1024)S(1)}, f32[2048]{0:T(1024)S(1)}, u32[]{:S(2)}, u32[]{:S(2)}) collective-permute-start(f32[2048]{0:T(1024)S(1)} %bitcast.2), channel_id=1, source_target_pairs={{0,4},{4,0},{1,5},{5,1},{2,6},{6,2},{3,7},{7,3},{8,12},{12,8},{9,1... | collective-permute-start | bytes 24584 | tf_op jit(solution)/shard_map/ppermute | solution.py:382

commit v7 on v6

--- a/solution.py
+++ b/solution.py
@@ -97,7 +97,7 @@
         rows // SUBLANES,
         lambda k, total: total + get(pl.ds(pl.multiple_of(k * SUBLANES, SUBLANES), SUBLANES)),
         jnp.zeros((SUBLANES, width), jnp.float32),
-        unroll=16,
+        unroll=64,
     )
     return jnp.sum(total, axis=0, keepdims=True)
 
@@ -130,8 +130,9 @@
     return peak, column_sums(rows, cols, term)
 
 
-def first_potential(bits, gathered_ref, away_ref, potential_ref, passed_ref):
-    passed_ref[...] = away_ref[...]
+def first_potential(bits, gathered_ref, mine_ref, away_ref, potential_ref, mine_out, away_out):
+    mine_out[...] = mine_ref[...]
+    away_out[...] = away_ref[...]
     parts = gathered_ref[...]
     each = parts.shape[0] // 2
     potential_ref[...] = bits - jnp.concatenate([combine(parts[:each]), combine(parts[each:])], axis=0)
@@ -306,17 +307,17 @@
         compiler_params=limit,
         name="first_rows",
     )(source, half, rest)
-    other = lax.ppermute(mine, "core", swap)
     away = lax.ppermute(mine, ("p", "q"), partner)
     gathered = lax.all_to_all(parts, LINE, 0, 0)
-    potential, away = pl.pallas_call(
+    potential, mine, away = pl.pallas_call(
         lambda *refs: first_potential(col_bits, *refs),
-        in_specs=[vmem] * 2,
-        out_specs=[vmem] * 2,
-        out_shape=[jax.ShapeDtypeStruct(chip_shape, f32), jax.ShapeDtypeStruct((own, width), f32)],
+        in_specs=[vmem] * 3,
+        out_specs=[vmem] * 3,
+        out_shape=[jax.ShapeDtypeStruct(chip_shape, f32)] + [jax.ShapeDtypeStruct((own, width), f32)] * 2,
         compiler_params=limit,
         name="first_potential",
-    )(gathered, away)
+    )(gathered, mine, away)
+    other = lax.ppermute(mine, "core", swap)
     away_potential = lax.ppermute(potential, ("p", "q"), partner)
     columns, *mine_block = pl.pallas_call(
         lambda *refs: first_columns(scale, *refs),

time: 134 us -> 133 us (level)
  blocking collectives: 79 us -> 89.4 us
  starting transfers between devices: 11.9 us -> 6.15 us
  waiting for transfers between devices: 5.09 us -> 1.25 us
  Pallas kernels: 35.1 us -> 32.5 us
    all_to_all x3 -> x4, blocking collectives: 28.7 us -> 38.4 us  [local(): gathered = lax.all_to_all(parts, LINE, 0, 0)]
    all_to_all x1 -> x0, starting transfers between devices: 5.25 us -> none  [local(): gathered = lax.all_to_all(parts, LINE, 0, 0)]
    all_to_all x1 -> x0, waiting for transfers between devices: 4.88 us -> none  [local(): gathered = lax.all_to_all(parts, LINE, 0, 0)]
  transfers between devices with their start and end apart: 6 -> 5, of which waited for: 2 -> 2; matrix products, arithmetic and copies ran while one was open for 0% -> 0% of each run, Pallas kernels for 3% -> 2%
where the time goes in v7:
time: 133 us; the launch traced here: 132 us
  blocking collectives  89.4 us (67%)
  Pallas kernels  32.5 us (24%)
  starting transfers between devices  6.15 us (5%)
  local copies, waits for them, and re-layouts  1.53 us (1%)
    all_to_all x4, blocking collectives, local(): columns = lax.all_to_all(parts, PLANE, 0, 0)  50.9 us
    all_to_all x4, blocking collectives, local(): gathered = lax.all_to_all(parts, LINE, 0, 0)  38.4 us
    pallas_call x3, Pallas kernels, local(): pl.pallas_call(lambda *refs: later_rows(scale, row_bits, *refs), in_specs...  13.5 us
    pallas_call x3, Pallas kernels, local(): pl.pallas_call(lambda *refs: later_columns(scale, col_bits, *refs), in_sp...  10.9 us
    ppermute x1, starting transfers between devices, local(): away = lax.ppermute(mine, ('p', 'q'), partner)  3.62 us
  transfers between devices with their start and end apart: 5, of which 2 were waited for; matrix products, arithmetic and copies ran while one was open for 0% of the time, Pallas kernels for 2%

profile of v7, /device:TPU:1, one launch (start us, length us, event | category | flops | bytes accessed | tf_op | source)
XLA Modules:
  0.0 132.1 jit_solution(11565310998202721644)
XLA Ops:
  0.6 1.6 %fetch.1 = (bf16[2048,256]{1,0:T(8,128)(2,1)S(1)}, bf16[2048,256]{1,0:T(8,128)(2,1)S(1)}) custom-call(bf16[4096,256]{1,0:T(8,128)(2,1)} %target_ref.1), custom_call_target="tpu_custom_call" | custom-call | tf_op jit(solution)/shard_map/fetch/pallas_call | solution.py:285
  2.2 0.0 copy-start
  2.2 0.9 copy-done
  3.1 1.6 %first_rows.1 = (f32[8,2,128]{2,1,0:T(2,128)S(1)}, f32[256,256]{1,0:T(8,128)S(1)}) custom-call(bf16[256,256]{1,0:T(8,128)(2,1)S(1)} %copy-done, bf16[2048,256]{1,0:T(8,128)(2,1)S(1)} %get-tuple-element.20.refs_1_.refs_2_, bf16[2048,256]{1,0:T(8,128)(2,1)S(1)} %get-tuple-element.21.refs_2_), custom_call_target="tpu_custom_call" | custom-call | tf_op jit(solution)/shard_map/first_rows/pallas_call | solution.py:294
  4.7 3.6 %collective-permute-start = (f32[256,256]{1,0:T(8,128)S(1)}, f32[256,256]{1,0:T(8,128)S(1)}, u32[]{:S(2)}, u32[]{:S(2)}) collective-permute-start(f32[256,256]{1,0:T(8,128)S(1)} %get-tuple-element.23.refs_1_), channel_id=1, source_target_pairs={{0,24},{24,0},{8,16},{16,8},{1,25},{25,1},{9,17},{17,9},{2,26},{26... | collective-permute-start | bytes 786440 | tf_op jit(solution)/shard_map/ppermute | solution.py:310
  8.3 9.9 %all_to_all.40.refs_0_ = f32[8,2,128]{2,1,0:T(2,128)S(1)} all-to-all(f32[8,2,128]{2,1,0:T(2,128)S(1)} %get-tuple-element.22), channel_id=1, replica_groups=mesh['z'=8,'p'=2,'q'=2,'core'=2,'x'=4] {'core','x'}, dimensions={0} | all-to-all | bytes 16384 | tf_op jit(solution)/shard_map/all_to_all | solution.py:311
  18.2 0.0 collective-permute-done.refs_2_
  18.2 0.1 first_potential.1
  18.3 0.5 collective-permute-start.3
  18.8 0.1 collective-permute-start.1
  18.9 0.0 collective-permute-start.2
  18.9 1.0 collective-permute-done.3.refs_1_
  19.9 1.3 partner_rows.1
  21.3 0.0 collective-permute-done.1.refs_1_
  21.3 1.5 %first_columns.1 = (f32[16,128]{1,0:T(8,128)S(1)}, f32[512,2048]{1,0:T(8,128)S(1)}, f32[4,128]{1,0:T(4,128)S(1)}, f32[16,128]{1,0:T(8,128)S(1)}, bf16[512,256]{1,0:T(8,128)(2,1)S(1)}) custom-call(f32[256,256]{1,0:T(8,128)S(1)} %get-tuple-element.24.refs_0_, f32[256,256]{1,0:T(8,128)S(1)} %collective-permute-done.1.refs_1_, ...), custom_call_target="tpu_custom_call" | custom-call | tf_op jit(solution)/shard_map/first_columns/pallas_call | solution.py:322
  22.7 0.0 collective-permute-done.2.refs_1_
  22.8 2.0 %partner_columns.1 = f32[16,16,128]{2,1,0:T(8,128)S(1)} custom-call(f32[16,128]{1,0:T(8,128)S(1)} %get-tuple-element.26.refs_0_, f32[4,128]{1,0:T(4,128)S(1)} %collective-permute-done.2.refs_1_, bf16[2048,256]{1,0:T(8,128)(2,1)S(1)} %get-tuple-element.20.refs_1_.refs_2_, f32[512,2048]{1,0:T(8,128)S(1)} %get-tuple-element.28.refs_3_.refs_6_, ...), custom_call_target="tpu_custom_call" | custom-call | tf_op jit(solution)/shard_map/partner_columns/pallas_call | solution.py:341
  24.8 16.6 %all_to_all.41.refs_0_ = f32[16,16,128]{2,1,0:T(8,128)S(1)} all-to-all(f32[16,16,128]{2,1,0:T(8,128)S(1)} %partner_columns.1), channel_id=1, replica_groups=mesh['z'=8,'p'=2,'q'=2,'core'=2,'x'=4] {'z','q'}, dimensions={0} | all-to-all | bytes 262144 | tf_op jit(solution)/shard_map/all_to_all | solution.py:350
  41.4 4.4 %later_rows.3 = f32[8,8,128]{2,1,0:T(8,128)S(1)} custom-call(f32[16,16,128]{2,1,0:T(8,128)S(1)} %all_to_all.41.refs_0_, bf16[2048,256]{1,0:T(8,128)(2,1)S(1)} %get-tuple-element.20.refs_1_.refs_2_, f32[512,2048]{1,0:T(8,128)S(1)} %get-tuple-element.32.refs_2_, f32[4,128]{1,0:T(4,128)S(1)} %get-tuple-element.33.refs_3_, ...), custom_call_target="tpu_custom_call" | custom-call | tf_op jit(solution)/shard_map/later_rows/pallas_call | solution.py:353
  45.8 10.2 %all_to_all.42.refs_0_ = f32[8,8,128]{2,1,0:T(8,128)S(1)} all-to-all(f32[8,8,128]{2,1,0:T(8,128)S(1)} %later_rows.3), channel_id=1, replica_groups=mesh['z'=8,'p'=2,'q'=2,'core'=2,'x'=4] {'core','x'}, dimensions={0} | all-to-all | bytes 65536 | tf_op jit(solution)/shard_map/all_to_all | solution.py:362
  56.0 3.6 %later_columns.3 = f32[16,16,128]{2,1,0:T(8,128)S(1)} custom-call(f32[8,8,128]{2,1,0:T(8,128)S(1)} %all_to_all.42.refs_0_, bf16[2048,256]{1,0:T(8,128)(2,1)S(1)} %get-tuple-element.20.refs_1_.refs_2_, f32[512,2048]{1,0:T(8,128)S(1)} %get-tuple-element.32.refs_2_, f32[4,128]{1,0:T(4,128)S(1)} %get-tuple-element.33.refs_3_, ...), custom_call_target="tpu_custom_call" | custom-call | tf_op jit(solution)/shard_map/later_columns/pallas_call | solution.py:363
  59.7 11.5 %all_to_all.43.refs_0_ = f32[16,16,128]{2,1,0:T(8,128)S(1)} all-to-all(f32[16,16,128]{2,1,0:T(8,128)S(1)} %later_columns.3), channel_id=1, replica_groups=mesh['z'=8,'p'=2,'q'=2,'core'=2,'x'=4] {'z','q'}, dimensions={0} | all-to-all | bytes 262144 | tf_op jit(solution)/shard_map/all_to_all | solution.py:372
  71.1 4.4 %later_rows.4 = f32[8,8,128]{2,1,0:T(8,128)S(1)} custom-call(f32[16,16,128]{2,1,0:T(8,128)S(1)} %all_to_all.43.refs_0_, bf16[2048,256]{1,0:T(8,128)(2,1)S(1)} %get-tuple-element.20.refs_1_.refs_2_, f32[512,2048]{1,0:T(8,128)S(1)} %get-tuple-element.32.refs_2_, f32[4,128]{1,0:T(4,128)S(1)} %get-tuple-element.33.refs_3_, ...), custom_call_target="tpu_custom_call" | custom-call | tf_op jit(solution)/shard_map/later_rows/pallas_call | solution.py:353
  75.5 9.1 %all_to_all.44.refs_0_ = f32[8,8,128]{2,1,0:T(8,128)S(1)} all-to-all(f32[8,8,128]{2,1,0:T(8,128)S(1)} %later_rows.4), channel_id=1, replica_groups=mesh['z'=8,'p'=2,'q'=2,'core'=2,'x'=4] {'core','x'}, dimensions={0} | all-to-all | bytes 65536 | tf_op jit(solution)/shard_map/all_to_all | solution.py:362
  84.7 3.6 %later_columns.4 = f32[16,16,128]{2,1,0:T(8,128)S(1)} custom-call(f32[8,8,128]{2,1,0:T(8,128)S(1)} %all_to_all.44.refs_0_, bf16[2048,256]{1,0:T(8,128)(2,1)S(1)} %get-tuple-element.20.refs_1_.refs_2_, f32[512,2048]{1,0:T(8,128)S(1)} %get-tuple-element.32.refs_2_, f32[4,128]{1,0:T(4,128)S(1)} %get-tuple-element.33.refs_3_, ...), custom_call_target="tpu_custom_call" | custom-call | tf_op jit(solution)/shard_map/later_columns/pallas_call | solution.py:363
  88.3 11.5 %all_to_all.45.refs_0_ = f32[16,16,128]{2,1,0:T(8,128)S(1)} all-to-all(f32[16,16,128]{2,1,0:T(8,128)S(1)} %later_columns.4), channel_id=1, replica_groups=mesh['z'=8,'p'=2,'q'=2,'core'=2,'x'=4] {'z','q'}, dimensions={0} | all-to-all | bytes 262144 | tf_op jit(solution)/shard_map/all_to_all | solution.py:372
  99.8 4.6 %later_rows.5 = f32[8,8,128]{2,1,0:T(8,128)S(1)} custom-call(f32[16,16,128]{2,1,0:T(8,128)S(1)} %all_to_all.45.refs_0_, bf16[2048,256]{1,0:T(8,128)(2,1)S(1)} %get-tuple-element.20.refs_1_.refs_2_, f32[512,2048]{1,0:T(8,128)S(1)} %get-tuple-element.32.refs_2_, f32[4,128]{1,0:T(4,128)S(1)} %get-tuple-element.33.refs_3_, ...), custom_call_target="tpu_custom_call" | custom-call | tf_op jit(solution)/shard_map/later_rows/pallas_call | solution.py:353
  104.4 9.1 %all_to_all.46.refs_0_ = f32[8,8,128]{2,1,0:T(8,128)S(1)} all-to-all(f32[8,8,128]{2,1,0:T(8,128)S(1)} %later_rows.5), channel_id=1, replica_groups=mesh['z'=8,'p'=2,'q'=2,'core'=2,'x'=4] {'core','x'}, dimensions={0} | all-to-all | bytes 65536 | tf_op jit(solution)/shard_map/all_to_all | solution.py:362
  113.6 3.6 %later_columns.5 = f32[16,16,128]{2,1,0:T(8,128)S(1)} custom-call(f32[8,8,128]{2,1,0:T(8,128)S(1)} %all_to_all.46.refs_0_, bf16[2048,256]{1,0:T(8,128)(2,1)S(1)} %get-tuple-element.20.refs_1_.refs_2_, f32[512,2048]{1,0:T(8,128)S(1)} %get-tuple-element.32.refs_2_, f32[4,128]{1,0:T(4,128)S(1)} %get-tuple-element.33.refs_3_, ...), custom_call_target="tpu_custom_call" | custom-call | tf_op jit(solution)/shard_map/later_columns/pallas_call | solution.py:363
  117.2 11.5 %all_to_all.47.refs_1_ = f32[16,16,128]{2,1,0:T(8,128)S(1)} all-to-all(f32[16,16,128]{2,1,0:T(8,128)S(1)} %later_columns.5), channel_id=1, replica_groups=mesh['z'=8,'p'=2,'q'=2,'core'=2,'x'=4] {'z','q'}, dimensions={0} | all-to-all | bytes 262144 | tf_op jit(solution)/shard_map/all_to_all | solution.py:372
  128.7 1.9 %collective-permute-start.4 = (f32[2048]{0:T(1024)S(1)}, f32[2048]{0:T(1024)S(1)}, u32[]{:S(2)}, u32[]{:S(2)}) collective-permute-start(f32[2048]{0:T(1024)S(1)} %bitcast.2), channel_id=1, source_target_pairs={{0,4},{4,0},{1,5},{5,1},{2,6},{6,2},{3,7},{7,3},{8,12},{12,8},{9,1... | collective-permute-start | bytes 24584 | tf_op jit(solution)/shard_map/ppermute | solution.py:383
  130.6 0.6 dynamic_slice.3
  131.3 0.2 collective-permute-done.4
  131.5 0.6 maximum_select_fusion
  (1 shorter events, 0.0 us)
Async XLA Ops:
  2.2 0.9 copy-start
  4.7 13.5 %collective-permute-start = (f32[256,256]{1,0:T(8,128)S(1)}, f32[256,256]{1,0:T(8,128)S(1)}, u32[]{:S(2)}, u32[]{:S(2)}) collective-permute-start(f32[256,256]{1,0:T(8,128)S(1)} %get-tuple-element.23.refs_1_), channel_id=1, source_target_pairs={{0,24},{24,0},{8,16},{16,8},{1,25},{25,1},{9,17},{17,9},{2,26},{26... | collective-permute-start | bytes 786440 | tf_op jit(solution)/shard_map/ppermute | solution.py:310
  18.3 1.6 %collective-permute-start.3 = (f32[256,256]{1,0:T(8,128)S(1)}, f32[256,256]{1,0:T(8,128)S(1)}, u32[]{:S(2)}, u32[]{:S(2)}) collective-permute-start(f32[256,256]{1,0:T(8,128)S(1)} %get-tuple-element.27.refs_0_), channel_id=1, source_target_pairs={{0,4},{4,0},{1,5},{5,1},{2,6},{6,2},{3,7},{7,3},{8,12},{12,8},{9,1... | collective-permute-start | bytes 786440 | tf_op jit(solution)/shard_map/ppermute | solution.py:338
  18.8 2.5 %collective-permute-start.1 = (f32[256,256]{1,0:T(8,128)S(1)}, f32[256,256]{1,0:T(8,128)S(1)}, u32[]{:S(2)}, u32[]{:S(2)}) collective-permute-start(f32[256,256]{1,0:T(8,128)S(1)} %get-tuple-element.24.refs_0_), channel_id=1, source_target_pairs={{0,4},{4,0},{1,5},{5,1},{2,6},{6,2},{3,7},{7,3},{8,12},{12,8},{9,1... | collective-permute-start | bytes 786440 | tf_op jit(solution)/shard_map/ppermute | solution.py:320
  18.9 3.9 %collective-permute-start.2 = (f32[4,128]{1,0:T(4,128)S(1)}, f32[4,128]{1,0:T(4,128)S(1)}, u32[]{:S(2)}, u32[]{:S(2)}) collective-permute-start(f32[4,128]{1,0:T(4,128)S(1)} %get-tuple-element.25.refs_3_), channel_id=1, source_target_pairs={{0,24},{24,0},{8,16},{16,8},{1,25},{25,1},{9,17},{17,9},{2,26},{26... | collective-permute-start | bytes 6152 | tf_op jit(solution)/shard_map/ppermute | solution.py:321
  128.7 2.8 %collective-permute-start.4 = (f32[2048]{0:T(1024)S(1)}, f32[2048]{0:T(1024)S(1)}, u32[]{:S(2)}, u32[]{:S(2)}) collective-permute-start(f32[2048]{0:T(1024)S(1)} %bitcast.2), channel_id=1, source_target_pairs={{0,4},{4,0},{1,5},{5,1},{2,6},{6,2},{3,7},{7,3},{8,12},{12,8},{9,1... | collective-permute-start | bytes 24584 | tf_op jit(solution)/shard_map/ppermute | solution.py:383

commit v8 on v7

--- a/solution.py
+++ b/solution.py
@@ -15,7 +15,7 @@
 SAFE = 2.0**-80
 
 FIRST_PLANE = ("z", "p", "q")
-PLANE = ("z", "q")
+PLANE = ("q", "z")
 LINE = ("core", "x")
 
 

time: 133 us -> 128 us (0.962)
  blocking collectives: 89.4 us -> 85.1 us
    all_to_all x4, blocking collectives: 50.9 us -> 46.4 us  [local(): columns = lax.all_to_all(parts, PLANE, 0, 0)]
where the time goes in v8:
time: 128 us
  blocking collectives  85.1 us (66%)
  Pallas kernels  32.5 us (25%)
  starting transfers between devices  6.29 us (5%)
  local copies, waits for them, and re-layouts  1.53 us (1%)
    all_to_all x4, blocking collectives, local(): columns = lax.all_to_all(parts, PLANE, 0, 0)  46.4 us
    all_to_all x4, blocking collectives, local(): gathered = lax.all_to_all(parts, LINE, 0, 0)  38.7 us
    pallas_call x3, Pallas kernels, local(): pl.pallas_call(lambda *refs: later_rows(scale, row_bits, *refs), in_specs...  13.5 us
    pallas_call x3, Pallas kernels, local(): pl.pallas_call(lambda *refs: later_columns(scale, col_bits, *refs), in_sp...  10.9 us
    ppermute x1, starting transfers between devices, local(): away = lax.ppermute(mine, ('p', 'q'), partner)  3.62 us
  transfers between devices with their start and end apart: 5, of which 2 were waited for; matrix products, arithmetic and copies ran while one was open for 0% of the time, Pallas kernels for 2%

profile of v8, /device:TPU:1, one launch (start us, length us, event | category | flops | bytes accessed | tf_op | source)
XLA Modules:
  0.0 127.9 jit_solution(12872464867134188506)
XLA Ops:
  0.6 1.6 %fetch.1 = (bf16[2048,256]{1,0:T(8,128)(2,1)S(1)}, bf16[2048,256]{1,0:T(8,128)(2,1)S(1)}) custom-call(bf16[4096,256]{1,0:T(8,128)(2,1)} %target_ref.1), custom_call_target="tpu_custom_call" | custom-call | tf_op jit(solution)/shard_map/fetch/pallas_call | solution.py:285
  2.2 0.0 copy-start
  2.2 0.9 copy-done
  3.1 1.6 %first_rows.1 = (f32[8,2,128]{2,1,0:T(2,128)S(1)}, f32[256,256]{1,0:T(8,128)S(1)}) custom-call(bf16[256,256]{1,0:T(8,128)(2,1)S(1)} %copy-done, bf16[2048,256]{1,0:T(8,128)(2,1)S(1)} %get-tuple-element.20.refs_1_.refs_2_, bf16[2048,256]{1,0:T(8,128)(2,1)S(1)} %get-tuple-element.21.refs_2_), custom_call_target="tpu_custom_call" | custom-call | tf_op jit(solution)/shard_map/first_rows/pallas_call | solution.py:294
  4.7 3.6 %collective-permute-start = (f32[256,256]{1,0:T(8,128)S(1)}, f32[256,256]{1,0:T(8,128)S(1)}, u32[]{:S(2)}, u32[]{:S(2)}) collective-permute-start(f32[256,256]{1,0:T(8,128)S(1)} %get-tuple-element.23.refs_1_), channel_id=1, source_target_pairs={{0,24},{24,0},{8,16},{16,8},{1,25},{25,1},{9,17},{17,9},{2,26},{26... | collective-permute-start | bytes 786440 | tf_op jit(solution)/shard_map/ppermute | solution.py:310
  8.3 9.9 %all_to_all.40.refs_0_ = f32[8,2,128]{2,1,0:T(2,128)S(1)} all-to-all(f32[8,2,128]{2,1,0:T(2,128)S(1)} %get-tuple-element.22), channel_id=1, replica_groups=mesh['z'=8,'p'=2,'q'=2,'core'=2,'x'=4] {'core','x'}, dimensions={0} | all-to-all | bytes 16384 | tf_op jit(solution)/shard_map/all_to_all | solution.py:311
  18.2 0.0 collective-permute-done.refs_2_
  18.2 0.1 first_potential.1
  18.3 0.5 collective-permute-start.3
  18.8 0.1 collective-permute-start.1
  18.9 0.0 collective-permute-start.2
  18.9 1.0 collective-permute-done.3.refs_1_
  19.9 1.3 %partner_rows.1 = (f32[512,2048]{1,0:T(8,128)S(1)}, f32[4,128]{1,0:T(4,128)S(1)}, f32[16,128]{1,0:T(8,128)S(1)}, bf16[512,256]{1,0:T(8,128)(2,1)S(1)}) custom-call(f32[256,256]{1,0:T(8,128)S(1)} %get-tuple-element.27.refs_0_, f32[256,256]{1,0:T(8,128)S(1)} %collective-permute-done.3.refs_1_, bf16[2048,256]{1,0:T(8,128)(2,1)S(1)} %get-tuple-element.20.refs_1_.refs_2_), custom_call_target="tpu_custom_call" | custom-call | tf_op jit(solution)/shard_map/partner_rows/pallas_call | solution.py:331
  21.3 0.0 collective-permute-done.1.refs_1_
  21.3 1.5 %first_columns.1 = (f32[16,128]{1,0:T(8,128)S(1)}, f32[512,2048]{1,0:T(8,128)S(1)}, f32[4,128]{1,0:T(4,128)S(1)}, f32[16,128]{1,0:T(8,128)S(1)}, bf16[512,256]{1,0:T(8,128)(2,1)S(1)}) custom-call(f32[256,256]{1,0:T(8,128)S(1)} %get-tuple-element.24.refs_0_, f32[256,256]{1,0:T(8,128)S(1)} %collective-permute-done.1.refs_1_, ...), custom_call_target="tpu_custom_call" | custom-call | tf_op jit(solution)/shard_map/first_columns/pallas_call | solution.py:322
  22.7 0.0 collective-permute-done.2.refs_1_
  22.8 2.0 %partner_columns.1 = f32[16,16,128]{2,1,0:T(8,128)S(1)} custom-call(f32[16,128]{1,0:T(8,128)S(1)} %get-tuple-element.26.refs_0_, f32[4,128]{1,0:T(4,128)S(1)} %collective-permute-done.2.refs_1_, bf16[2048,256]{1,0:T(8,128)(2,1)S(1)} %get-tuple-element.20.refs_1_.refs_2_, f32[512,2048]{1,0:T(8,128)S(1)} %get-tuple-element.28.refs_3_.refs_6_, ...), custom_call_target="tpu_custom_call" | custom-call | tf_op jit(solution)/shard_map/partner_columns/pallas_call | solution.py:341
  24.8 15.5 %all_to_all.41.refs_0_ = f32[16,16,128]{2,1,0:T(8,128)S(1)} all-to-all(f32[16,16,128]{2,1,0:T(8,128)S(1)} %partner_columns.1), channel_id=1, replica_groups=mesh['z'=8,'p'=2,'q'=2,'core'=2,'x'=4] {'q','z'}, dimensions={0} | all-to-all | bytes 262144 | tf_op jit(solution)/shard_map/all_to_all | solution.py:350
  40.3 4.4 %later_rows.3 = f32[8,8,128]{2,1,0:T(8,128)S(1)} custom-call(f32[16,16,128]{2,1,0:T(8,128)S(1)} %all_to_all.41.refs_0_, bf16[2048,256]{1,0:T(8,128)(2,1)S(1)} %get-tuple-element.20.refs_1_.refs_2_, f32[512,2048]{1,0:T(8,128)S(1)} %get-tuple-element.32.refs_2_, f32[4,128]{1,0:T(4,128)S(1)} %get-tuple-element.33.refs_3_, ...), custom_call_target="tpu_custom_call" | custom-call | tf_op jit(solution)/shard_map/later_rows/pallas_call | solution.py:353
  44.8 10.2 %all_to_all.42.refs_0_ = f32[8,8,128]{2,1,0:T(8,128)S(1)} all-to-all(f32[8,8,128]{2,1,0:T(8,128)S(1)} %later_rows.3), channel_id=1, replica_groups=mesh['z'=8,'p'=2,'q'=2,'core'=2,'x'=4] {'core','x'}, dimensions={0} | all-to-all | bytes 65536 | tf_op jit(solution)/shard_map/all_to_all | solution.py:362
  55.0 3.6 %later_columns.3 = f32[16,16,128]{2,1,0:T(8,128)S(1)} custom-call(f32[8,8,128]{2,1,0:T(8,128)S(1)} %all_to_all.42.refs_0_, bf16[2048,256]{1,0:T(8,128)(2,1)S(1)} %get-tuple-element.20.refs_1_.refs_2_, f32[512,2048]{1,0:T(8,128)S(1)} %get-tuple-element.32.refs_2_, f32[4,128]{1,0:T(4,128)S(1)} %get-tuple-element.33.refs_3_, ...), custom_call_target="tpu_custom_call" | custom-call | tf_op jit(solution)/shard_map/later_columns/pallas_call | solution.py:363
  58.6 10.2 %all_to_all.43.refs_0_ = f32[16,16,128]{2,1,0:T(8,128)S(1)} all-to-all(f32[16,16,128]{2,1,0:T(8,128)S(1)} %later_columns.3), channel_id=1, replica_groups=mesh['z'=8,'p'=2,'q'=2,'core'=2,'x'=4] {'q','z'}, dimensions={0} | all-to-all | bytes 262144 | tf_op jit(solution)/shard_map/all_to_all | solution.py:372
  68.8 4.4 %later_rows.4 = f32[8,8,128]{2,1,0:T(8,128)S(1)} custom-call(f32[16,16,128]{2,1,0:T(8,128)S(1)} %all_to_all.43.refs_0_, bf16[2048,256]{1,0:T(8,128)(2,1)S(1)} %get-tuple-element.20.refs_1_.refs_2_, f32[512,2048]{1,0:T(8,128)S(1)} %get-tuple-element.32.refs_2_, f32[4,128]{1,0:T(4,128)S(1)} %get-tuple-element.33.refs_3_, ...), custom_call_target="tpu_custom_call" | custom-call | tf_op jit(solution)/shard_map/later_rows/pallas_call | solution.py:353
  73.3 9.3 %all_to_all.44.refs_0_ = f32[8,8,128]{2,1,0:T(8,128)S(1)} all-to-all(f32[8,8,128]{2,1,0:T(8,128)S(1)} %later_rows.4), channel_id=1, replica_groups=mesh['z'=8,'p'=2,'q'=2,'core'=2,'x'=4] {'core','x'}, dimensions={0} | all-to-all | bytes 65536 | tf_op jit(solution)/shard_map/all_to_all | solution.py:362
  82.6 3.6 %later_columns.4 = f32[16,16,128]{2,1,0:T(8,128)S(1)} custom-call(f32[8,8,128]{2,1,0:T(8,128)S(1)} %all_to_all.44.refs_0_, bf16[2048,256]{1,0:T(8,128)(2,1)S(1)} %get-tuple-element.20.refs_1_.refs_2_, f32[512,2048]{1,0:T(8,128)S(1)} %get-tuple-element.32.refs_2_, f32[4,128]{1,0:T(4,128)S(1)} %get-tuple-element.33.refs_3_, ...), custom_call_target="tpu_custom_call" | custom-call | tf_op jit(solution)/shard_map/later_columns/pallas_call | solution.py:363
  86.2 10.3 %all_to_all.45.refs_0_ = f32[16,16,128]{2,1,0:T(8,128)S(1)} all-to-all(f32[16,16,128]{2,1,0:T(8,128)S(1)} %later_columns.4), channel_id=1, replica_groups=mesh['z'=8,'p'=2,'q'=2,'core'=2,'x'=4] {'q','z'}, dimensions={0} | all-to-all | bytes 262144 | tf_op jit(solution)/shard_map/all_to_all | solution.py:372
  96.5 4.6 %later_rows.5 = f32[8,8,128]{2,1,0:T(8,128)S(1)} custom-call(f32[16,16,128]{2,1,0:T(8,128)S(1)} %all_to_all.45.refs_0_, bf16[2048,256]{1,0:T(8,128)(2,1)S(1)} %get-tuple-element.20.refs_1_.refs_2_, f32[512,2048]{1,0:T(8,128)S(1)} %get-tuple-element.32.refs_2_, f32[4,128]{1,0:T(4,128)S(1)} %get-tuple-element.33.refs_3_, ...), custom_call_target="tpu_custom_call" | custom-call | tf_op jit(solution)/shard_map/later_rows/pallas_call | solution.py:353
  101.1 9.3 %all_to_all.46.refs_0_ = f32[8,8,128]{2,1,0:T(8,128)S(1)} all-to-all(f32[8,8,128]{2,1,0:T(8,128)S(1)} %later_rows.5), channel_id=1, replica_groups=mesh['z'=8,'p'=2,'q'=2,'core'=2,'x'=4] {'core','x'}, dimensions={0} | all-to-all | bytes 65536 | tf_op jit(solution)/shard_map/all_to_all | solution.py:362
  110.4 3.6 %later_columns.5 = f32[16,16,128]{2,1,0:T(8,128)S(1)} custom-call(f32[8,8,128]{2,1,0:T(8,128)S(1)} %all_to_all.46.refs_0_, bf16[2048,256]{1,0:T(8,128)(2,1)S(1)} %get-tuple-element.20.refs_1_.refs_2_, f32[512,2048]{1,0:T(8,128)S(1)} %get-tuple-element.32.refs_2_, f32[4,128]{1,0:T(4,128)S(1)} %get-tuple-element.33.refs_3_, ...), custom_call_target="tpu_custom_call" | custom-call | tf_op jit(solution)/shard_map/later_columns/pallas_call | solution.py:363
  114.1 10.3 %all_to_all.47.refs_1_ = f32[16,16,128]{2,1,0:T(8,128)S(1)} all-to-all(f32[16,16,128]{2,1,0:T(8,128)S(1)} %later_columns.5), channel_id=1, replica_groups=mesh['z'=8,'p'=2,'q'=2,'core'=2,'x'=4] {'q','z'}, dimensions={0} | all-to-all | bytes 262144 | tf_op jit(solution)/shard_map/all_to_all | solution.py:372
  124.4 2.1 %collective-permute-start.4 = (f32[2048]{0:T(1024)S(1)}, f32[2048]{0:T(1024)S(1)}, u32[]{:S(2)}, u32[]{:S(2)}) collective-permute-start(f32[2048]{0:T(1024)S(1)} %bitcast.2), channel_id=1, source_target_pairs={{0,4},{4,0},{1,5},{5,1},{2,6},{6,2},{3,7},{7,3},{8,12},{12,8},{9,1... | collective-permute-start | bytes 24584 | tf_op jit(solution)/shard_map/ppermute | solution.py:383
  126.5 0.6 dynamic_slice.3
  127.1 0.2 collective-permute-done.4
  127.3 0.6 maximum_select_fusion
  (1 shorter events, 0.0 us)
Async XLA Ops:
  2.2 0.9 copy-start
  4.7 13.5 %collective-permute-start = (f32[256,256]{1,0:T(8,128)S(1)}, f32[256,256]{1,0:T(8,128)S(1)}, u32[]{:S(2)}, u32[]{:S(2)}) collective-permute-start(f32[256,256]{1,0:T(8,128)S(1)} %get-tuple-element.23.refs_1_), channel_id=1, source_target_pairs={{0,24},{24,0},{8,16},{16,8},{1,25},{25,1},{9,17},{17,9},{2,26},{26... | collective-permute-start | bytes 786440 | tf_op jit(solution)/shard_map/ppermute | solution.py:310
  18.3 1.6 %collective-permute-start.3 = (f32[256,256]{1,0:T(8,128)S(1)}, f32[256,256]{1,0:T(8,128)S(1)}, u32[]{:S(2)}, u32[]{:S(2)}) collective-permute-start(f32[256,256]{1,0:T(8,128)S(1)} %get-tuple-element.27.refs_0_), channel_id=1, source_target_pairs={{0,4},{4,0},{1,5},{5,1},{2,6},{6,2},{3,7},{7,3},{8,12},{12,8},{9,1... | collective-permute-start | bytes 786440 | tf_op jit(solution)/shard_map/ppermute | solution.py:338
  18.8 2.5 %collective-permute-start.1 = (f32[256,256]{1,0:T(8,128)S(1)}, f32[256,256]{1,0:T(8,128)S(1)}, u32[]{:S(2)}, u32[]{:S(2)}) collective-permute-start(f32[256,256]{1,0:T(8,128)S(1)} %get-tuple-element.24.refs_0_), channel_id=1, source_target_pairs={{0,4},{4,0},{1,5},{5,1},{2,6},{6,2},{3,7},{7,3},{8,12},{12,8},{9,1... | collective-permute-start | bytes 786440 | tf_op jit(solution)/shard_map/ppermute | solution.py:320
  18.9 3.9 %collective-permute-start.2 = (f32[4,128]{1,0:T(4,128)S(1)}, f32[4,128]{1,0:T(4,128)S(1)}, u32[]{:S(2)}, u32[]{:S(2)}) collective-permute-start(f32[4,128]{1,0:T(4,128)S(1)} %get-tuple-element.25.refs_3_), channel_id=1, source_target_pairs={{0,24},{24,0},{8,16},{16,8},{1,25},{25,1},{9,17},{17,9},{2,26},{26... | collective-permute-start | bytes 6152 | tf_op jit(solution)/shard_map/ppermute | solution.py:321
  124.4 2.9 %collective-permute-start.4 = (f32[2048]{0:T(1024)S(1)}, f32[2048]{0:T(1024)S(1)}, u32[]{:S(2)}, u32[]{:S(2)}) collective-permute-start(f32[2048]{0:T(1024)S(1)} %bitcast.2), channel_id=1, source_target_pairs={{0,4},{4,0},{1,5},{5,1},{2,6},{6,2},{3,7},{7,3},{8,12},{12,8},{9,1... | collective-permute-start | bytes 24584 | tf_op jit(solution)/shard_map/ppermute | solution.py:383

commit v9 on v8

--- a/solution.py
+++ b/solution.py
@@ -12,6 +12,7 @@
 TILE = 256
 LANES = 128
 SUBLANES = 8
+CHUNKS = 4
 SAFE = 2.0**-80
 
 FIRST_PLANE = ("z", "p", "q")
@@ -58,23 +59,25 @@
     )
 
 
-def fetch(target_ref, half_ref, rest_ref, arrived):
+def first_rows(scale, source_ref, target_ref, out_ref, wide_ref, half_ref, rest_ref, scores, peaks, line, arrived):
     core = lax.axis_index("core")
-    half = half_ref.shape[0]
+    rows, half = source_ref.shape[0], half_ref.shape[0]
+    chunk = half // CHUNKS
     copies = [
-        pltpu.make_async_copy(target_ref.at[pl.ds(pl.multiple_of(side * half, half), half)], place, arrived.at[k])
-        for k, (side, place) in enumerate(((core, half_ref), (1 - core, rest_ref)))
+        pltpu.make_async_copy(
+            target_ref.at[pl.ds(pl.multiple_of(side * half + k * chunk, chunk), chunk)],
+            place.at[pl.ds(k * chunk, chunk)],
+            arrived.at[index * CHUNKS + k],
+        )
+        for index, (side, place) in enumerate(((core, half_ref), (1 - core, rest_ref)))
+        for k in range(CHUNKS)
     ]
     for copy in copies:
         copy.start()
-    for copy in copies:
-        copy.wait()
-
-
-def first_rows(scale, source_ref, half_ref, rest_ref, out_ref, wide_ref, scores, peaks, line):
-    rows, half = source_ref.shape[0], half_ref.shape[0]
     wide_ref[...] = source_ref[...].astype(jnp.float32)
     for start in range(0, 2 * half, TILE):
+        if start % chunk == 0:
+            copies[start // chunk].wait()
         place = half_ref if start < half else rest_ref
         tile = slice(start, start + TILE)
         part = score(source_ref[...], place[start % half : start % half + TILE, :], scale)
@@ -282,31 +285,25 @@
         jax.ShapeDtypeStruct((rows, width), source.dtype),
     ]
 
-    half, rest = pl.pallas_call(
-        fetch,
-        in_specs=[hbm],
-        out_specs=[vmem] * 2,
-        out_shape=[jax.ShapeDtypeStruct((cols, width), target.dtype)] * 2,
-        scratch_shapes=[pltpu.SemaphoreType.DMA((2,))],
-        compiler_params=pltpu.CompilerParams(vmem_limit_bytes=51 * 2**20),
-        name="fetch",
-    )(target)
-    parts, mine = pl.pallas_call(
+    parts, mine, half = pl.pallas_call(
         lambda *refs: first_rows(scale, *refs),
-        in_specs=[vmem] * 3,
-        out_specs=[vmem] * 2,
+        in_specs=[vmem, hbm],
+        out_specs=[vmem] * 3,
         out_shape=[
             jax.ShapeDtypeStruct((line, own // LANES, LANES), f32),
             jax.ShapeDtypeStruct((own, width), f32),
+            jax.ShapeDtypeStruct((cols, width), target.dtype),
         ],
         scratch_shapes=[
+            pltpu.VMEM((cols, width), target.dtype),
             pltpu.VMEM((own, target.shape[0]), f32),
             pltpu.VMEM((own, LANES), f32),
             pltpu.VMEM((own // LANES, LANES), f32),
+            pltpu.SemaphoreType.DMA((2 * CHUNKS,)),
         ],
-        compiler_params=limit,
+        compiler_params=pltpu.CompilerParams(vmem_limit_bytes=52 * 2**20),
         name="first_rows",
-    )(source, half, rest)
+    )(source, target)
     away = lax.ppermute(mine, ("p", "q"), partner)
     gathered = lax.all_to_all(parts, LINE, 0, 0)
     potential, mine, away = pl.pallas_call(

time: 128 us -> 130 us (1.016)
  Pallas kernels: 32.5 us -> 34.3 us
    pallas_call x2 -> x1, Pallas kernels: 3.14 us -> 3.86 us  [local(): pl.pallas_call(lambda *refs: first_rows(scale, *refs), in_specs=[vmem, hb...]
where the time goes in v9:
time: 130 us
  blocking collectives  84.9 us (65%)
  Pallas kernels  34.3 us (26%)
  starting transfers between devices  6.33 us (5%)
  local copies, waits for them, and re-layouts  1.53 us (1%)
    all_to_all x4, blocking collectives, local(): columns = lax.all_to_all(parts, PLANE, 0, 0)  46.4 us
    all_to_all x4, blocking collectives, local(): gathered = lax.all_to_all(parts, LINE, 0, 0)  38.5 us
    pallas_call x3, Pallas kernels, local(): pl.pallas_call(lambda *refs: later_rows(scale, row_bits, *refs), in_specs...  14.2 us
    pallas_call x3, Pallas kernels, local(): pl.pallas_call(lambda *refs: later_columns(scale, col_bits, *refs), in_sp...  11.2 us
    pallas_call x1, Pallas kernels, local(): pl.pallas_call(lambda *refs: first_rows(scale, *refs), in_specs=[vmem, hb...  3.86 us
    ppermute x1, starting transfers between devices, local(): away = lax.ppermute(mine, ('p', 'q'), partner)  3.66 us
  transfers between devices with their start and end apart: 5, of which 2 were waited for; matrix products, arithmetic and copies ran while one was open for 0% of the time, Pallas kernels for 2%

profile of v9, /device:TPU:1, one launch (start us, length us, event | category | flops | bytes accessed | tf_op | source)
XLA Modules:
  0.0 129.6 jit_solution(14601278246461764190)
XLA Ops:
  0.6 0.0 copy-start
  0.6 0.9 copy-done
  1.5 3.9 %first_rows.1 = (f32[8,2,128]{2,1,0:T(2,128)S(1)}, f32[256,256]{1,0:T(8,128)S(1)}, bf16[2048,256]{1,0:T(8,128)(2,1)S(1)}) custom-call(bf16[256,256]{1,0:T(8,128)(2,1)S(1)} %copy-done, bf16[4096,256]{1,0:T(8,128)(2,1)} %refs_1_.1), custom_call_target="tpu_custom_call" | custom-call | tf_op jit(solution)/shard_map/first_rows/pallas_call | solution.py:288
  5.4 3.7 %collective-permute-start = (f32[256,256]{1,0:T(8,128)S(1)}, f32[256,256]{1,0:T(8,128)S(1)}, u32[]{:S(2)}, u32[]{:S(2)}) collective-permute-start(f32[256,256]{1,0:T(8,128)S(1)} %get-tuple-element.20.refs_1_), channel_id=1, source_target_pairs={{0,24},{24,0},{8,16},{16,8},{1,25},{25,1},{9,17},{17,9},{2,26},{26... | collective-permute-start | bytes 786440 | tf_op jit(solution)/shard_map/ppermute | solution.py:307
  9.1 9.9 %all_to_all.40.refs_0_ = f32[8,2,128]{2,1,0:T(2,128)S(1)} all-to-all(f32[8,2,128]{2,1,0:T(2,128)S(1)} %get-tuple-element.19), channel_id=1, replica_groups=mesh['z'=8,'p'=2,'q'=2,'core'=2,'x'=4] {'core','x'}, dimensions={0} | all-to-all | bytes 16384 | tf_op jit(solution)/shard_map/all_to_all | solution.py:308
  19.0 0.0 collective-permute-done.refs_2_
  19.0 0.1 first_potential.1
  19.1 0.5 collective-permute-start.1
  19.5 0.1 collective-permute-start.3
  19.7 0.0 collective-permute-start.2
  19.7 1.0 collective-permute-done.1.refs_1_
  20.7 1.5 %first_columns.1 = (f32[16,128]{1,0:T(8,128)S(1)}, f32[512,2048]{1,0:T(8,128)S(1)}, f32[4,128]{1,0:T(4,128)S(1)}, f32[16,128]{1,0:T(8,128)S(1)}, bf16[512,256]{1,0:T(8,128)(2,1)S(1)}) custom-call(f32[256,256]{1,0:T(8,128)S(1)} %get-tuple-element.21.refs_0_, f32[256,256]{1,0:T(8,128)S(1)} %collective-permute-done.1.refs_1_, ...), custom_call_target="tpu_custom_call" | custom-call | tf_op jit(solution)/shard_map/first_columns/pallas_call | solution.py:319
  22.2 0.0 collective-permute-done.3.refs_1_
  22.2 1.3 %partner_rows.1 = (f32[512,2048]{1,0:T(8,128)S(1)}, f32[4,128]{1,0:T(4,128)S(1)}, f32[16,128]{1,0:T(8,128)S(1)}, bf16[512,256]{1,0:T(8,128)(2,1)S(1)}) custom-call(f32[256,256]{1,0:T(8,128)S(1)} %get-tuple-element.25.refs_0_, f32[256,256]{1,0:T(8,128)S(1)} %collective-permute-done.3.refs_1_, bf16[2048,256]{1,0:T(8,128)(2,1)S(1)} %get-tuple-element.22.refs_2_.refs_1_), custom_call_target="tpu_custom_call" | custom-call | tf_op jit(solution)/shard_map/partner_rows/pallas_call | solution.py:328
  23.5 0.0 collective-permute-done.2.refs_1_
  23.5 2.1 %partner_columns.1 = f32[16,16,128]{2,1,0:T(8,128)S(1)} custom-call(f32[16,128]{1,0:T(8,128)S(1)} %get-tuple-element.24.refs_0_, f32[4,128]{1,0:T(4,128)S(1)} %collective-permute-done.2.refs_1_, bf16[2048,256]{1,0:T(8,128)(2,1)S(1)} %get-tuple-element.22.refs_2_.refs_1_, f32[512,2048]{1,0:T(8,128)S(1)} %get-tuple-element.26.refs_3_.refs_6_, ...), custom_call_target="tpu_custom_call" | custom-call | tf_op jit(solution)/shard_map/partner_columns/pallas_call | solution.py:338
  25.6 15.5 %all_to_all.41.refs_0_ = f32[16,16,128]{2,1,0:T(8,128)S(1)} all-to-all(f32[16,16,128]{2,1,0:T(8,128)S(1)} %partner_columns.1), channel_id=1, replica_groups=mesh['z'=8,'p'=2,'q'=2,'core'=2,'x'=4] {'q','z'}, dimensions={0} | all-to-all | bytes 262144 | tf_op jit(solution)/shard_map/all_to_all | solution.py:347
  41.1 4.8 %later_rows.3 = f32[8,8,128]{2,1,0:T(8,128)S(1)} custom-call(f32[16,16,128]{2,1,0:T(8,128)S(1)} %all_to_all.41.refs_0_, bf16[2048,256]{1,0:T(8,128)(2,1)S(1)} %get-tuple-element.22.refs_2_.refs_1_, f32[512,2048]{1,0:T(8,128)S(1)} %get-tuple-element.30.refs_2_, f32[4,128]{1,0:T(4,128)S(1)} %get-tuple-element.31.refs_3_, ...), custom_call_target="tpu_custom_call" | custom-call | tf_op jit(solution)/shard_map/later_rows/pallas_call | solution.py:350
  46.0 10.0 %all_to_all.42.refs_0_ = f32[8,8,128]{2,1,0:T(8,128)S(1)} all-to-all(f32[8,8,128]{2,1,0:T(8,128)S(1)} %later_rows.3), channel_id=1, replica_groups=mesh['z'=8,'p'=2,'q'=2,'core'=2,'x'=4] {'core','x'}, dimensions={0} | all-to-all | bytes 65536 | tf_op jit(solution)/shard_map/all_to_all | solution.py:359
  56.0 3.7 %later_columns.3 = f32[16,16,128]{2,1,0:T(8,128)S(1)} custom-call(f32[8,8,128]{2,1,0:T(8,128)S(1)} %all_to_all.42.refs_0_, bf16[2048,256]{1,0:T(8,128)(2,1)S(1)} %get-tuple-element.22.refs_2_.refs_1_, f32[512,2048]{1,0:T(8,128)S(1)} %get-tuple-element.30.refs_2_, f32[4,128]{1,0:T(4,128)S(1)} %get-tuple-element.31.refs_3_, ...), custom_call_target="tpu_custom_call" | custom-call | tf_op jit(solution)/shard_map/later_columns/pallas_call | solution.py:360
  59.7 10.2 %all_to_all.43.refs_0_ = f32[16,16,128]{2,1,0:T(8,128)S(1)} all-to-all(f32[16,16,128]{2,1,0:T(8,128)S(1)} %later_columns.3), channel_id=1, replica_groups=mesh['z'=8,'p'=2,'q'=2,'core'=2,'x'=4] {'q','z'}, dimensions={0} | all-to-all | bytes 262144 | tf_op jit(solution)/shard_map/all_to_all | solution.py:369
  69.9 4.7 %later_rows.4 = f32[8,8,128]{2,1,0:T(8,128)S(1)} custom-call(f32[16,16,128]{2,1,0:T(8,128)S(1)} %all_to_all.43.refs_0_, bf16[2048,256]{1,0:T(8,128)(2,1)S(1)} %get-tuple-element.22.refs_2_.refs_1_, f32[512,2048]{1,0:T(8,128)S(1)} %get-tuple-element.30.refs_2_, f32[4,128]{1,0:T(4,128)S(1)} %get-tuple-element.31.refs_3_, ...), custom_call_target="tpu_custom_call" | custom-call | tf_op jit(solution)/shard_map/later_rows/pallas_call | solution.py:350
  74.6 9.3 %all_to_all.44.refs_0_ = f32[8,8,128]{2,1,0:T(8,128)S(1)} all-to-all(f32[8,8,128]{2,1,0:T(8,128)S(1)} %later_rows.4), channel_id=1, replica_groups=mesh['z'=8,'p'=2,'q'=2,'core'=2,'x'=4] {'core','x'}, dimensions={0} | all-to-all | bytes 65536 | tf_op jit(solution)/shard_map/all_to_all | solution.py:359
  83.8 3.9 %later_columns.4 = f32[16,16,128]{2,1,0:T(8,128)S(1)} custom-call(f32[8,8,128]{2,1,0:T(8,128)S(1)} %all_to_all.44.refs_0_, bf16[2048,256]{1,0:T(8,128)(2,1)S(1)} %get-tuple-element.22.refs_2_.refs_1_, f32[512,2048]{1,0:T(8,128)S(1)} %get-tuple-element.30.refs_2_, f32[4,128]{1,0:T(4,128)S(1)} %get-tuple-element.31.refs_3_, ...), custom_call_target="tpu_custom_call" | custom-call | tf_op jit(solution)/shard_map/later_columns/pallas_call | solution.py:360
  87.8 10.3 %all_to_all.45.refs_0_ = f32[16,16,128]{2,1,0:T(8,128)S(1)} all-to-all(f32[16,16,128]{2,1,0:T(8,128)S(1)} %later_columns.4), channel_id=1, replica_groups=mesh['z'=8,'p'=2,'q'=2,'core'=2,'x'=4] {'q','z'}, dimensions={0} | all-to-all | bytes 262144 | tf_op jit(solution)/shard_map/all_to_all | solution.py:369
  98.1 4.7 %later_rows.5 = f32[8,8,128]{2,1,0:T(8,128)S(1)} custom-call(f32[16,16,128]{2,1,0:T(8,128)S(1)} %all_to_all.45.refs_0_, bf16[2048,256]{1,0:T(8,128)(2,1)S(1)} %get-tuple-element.22.refs_2_.refs_1_, f32[512,2048]{1,0:T(8,128)S(1)} %get-tuple-element.30.refs_2_, f32[4,128]{1,0:T(4,128)S(1)} %get-tuple-element.31.refs_3_, ...), custom_call_target="tpu_custom_call" | custom-call | tf_op jit(solution)/shard_map/later_rows/pallas_call | solution.py:350
  102.7 9.3 %all_to_all.46.refs_0_ = f32[8,8,128]{2,1,0:T(8,128)S(1)} all-to-all(f32[8,8,128]{2,1,0:T(8,128)S(1)} %later_rows.5), channel_id=1, replica_groups=mesh['z'=8,'p'=2,'q'=2,'core'=2,'x'=4] {'core','x'}, dimensions={0} | all-to-all | bytes 65536 | tf_op jit(solution)/shard_map/all_to_all | solution.py:359
  112.0 3.7 %later_columns.5 = f32[16,16,128]{2,1,0:T(8,128)S(1)} custom-call(f32[8,8,128]{2,1,0:T(8,128)S(1)} %all_to_all.46.refs_0_, bf16[2048,256]{1,0:T(8,128)(2,1)S(1)} %get-tuple-element.22.refs_2_.refs_1_, f32[512,2048]{1,0:T(8,128)S(1)} %get-tuple-element.30.refs_2_, f32[4,128]{1,0:T(4,128)S(1)} %get-tuple-element.31.refs_3_, ...), custom_call_target="tpu_custom_call" | custom-call | tf_op jit(solution)/shard_map/later_columns/pallas_call | solution.py:360
  115.7 10.3 %all_to_all.47.refs_1_ = f32[16,16,128]{2,1,0:T(8,128)S(1)} all-to-all(f32[16,16,128]{2,1,0:T(8,128)S(1)} %later_columns.5), channel_id=1, replica_groups=mesh['z'=8,'p'=2,'q'=2,'core'=2,'x'=4] {'q','z'}, dimensions={0} | all-to-all | bytes 262144 | tf_op jit(solution)/shard_map/all_to_all | solution.py:369
  126.1 2.1 %collective-permute-start.4 = (f32[2048]{0:T(1024)S(1)}, f32[2048]{0:T(1024)S(1)}, u32[]{:S(2)}, u32[]{:S(2)}) collective-permute-start(f32[2048]{0:T(1024)S(1)} %bitcast.2), channel_id=1, source_target_pairs={{0,4},{4,0},{1,5},{5,1},{2,6},{6,2},{3,7},{7,3},{8,12},{12,8},{9,1... | collective-permute-start | bytes 24584 | tf_op jit(solution)/shard_map/ppermute | solution.py:380
  128.1 0.6 dynamic_slice.3
  128.8 0.2 collective-permute-done.4
  129.0 0.6 maximum_select_fusion
  (1 shorter events, 0.0 us)
Async XLA Ops:
  0.6 0.9 copy-start
  5.4 13.6 %collective-permute-start = (f32[256,256]{1,0:T(8,128)S(1)}, f32[256,256]{1,0:T(8,128)S(1)}, u32[]{:S(2)}, u32[]{:S(2)}) collective-permute-start(f32[256,256]{1,0:T(8,128)S(1)} %get-tuple-element.20.refs_1_), channel_id=1, source_target_pairs={{0,24},{24,0},{8,16},{16,8},{1,25},{25,1},{9,17},{17,9},{2,26},{26... | collective-permute-start | bytes 786440 | tf_op jit(solution)/shard_map/ppermute | solution.py:307
  19.1 1.6 %collective-permute-start.1 = (f32[256,256]{1,0:T(8,128)S(1)}, f32[256,256]{1,0:T(8,128)S(1)}, u32[]{:S(2)}, u32[]{:S(2)}) collective-permute-start(f32[256,256]{1,0:T(8,128)S(1)} %get-tuple-element.21.refs_0_), channel_id=1, source_target_pairs={{0,4},{4,0},{1,5},{5,1},{2,6},{6,2},{3,7},{7,3},{8,12},{12,8},{9,1... | collective-permute-start | bytes 786440 | tf_op jit(solution)/shard_map/ppermute | solution.py:317
  19.5 2.6 %collective-permute-start.3 = (f32[256,256]{1,0:T(8,128)S(1)}, f32[256,256]{1,0:T(8,128)S(1)}, u32[]{:S(2)}, u32[]{:S(2)}) collective-permute-start(f32[256,256]{1,0:T(8,128)S(1)} %get-tuple-element.25.refs_0_), channel_id=1, source_target_pairs={{0,4},{4,0},{1,5},{5,1},{2,6},{6,2},{3,7},{7,3},{8,12},{12,8},{9,1... | collective-permute-start | bytes 786440 | tf_op jit(solution)/shard_map/ppermute | solution.py:335
  19.7 3.9 %collective-permute-start.2 = (f32[4,128]{1,0:T(4,128)S(1)}, f32[4,128]{1,0:T(4,128)S(1)}, u32[]{:S(2)}, u32[]{:S(2)}) collective-permute-start(f32[4,128]{1,0:T(4,128)S(1)} %get-tuple-element.23.refs_3_), channel_id=1, source_target_pairs={{0,24},{24,0},{8,16},{16,8},{1,25},{25,1},{9,17},{17,9},{2,26},{26... | collective-permute-start | bytes 6152 | tf_op jit(solution)/shard_map/ppermute | solution.py:318
  126.1 2.9 %collective-permute-start.4 = (f32[2048]{0:T(1024)S(1)}, f32[2048]{0:T(1024)S(1)}, u32[]{:S(2)}, u32[]{:S(2)}) collective-permute-start(f32[2048]{0:T(1024)S(1)} %bitcast.2), channel_id=1, source_target_pairs={{0,4},{4,0},{1,5},{5,1},{2,6},{6,2},{3,7},{7,3},{8,12},{12,8},{9,1... | collective-permute-start | bytes 24584 | tf_op jit(solution)/shard_map/ppermute | solution.py:380

commit v10 on v8

--- a/solution.py
+++ b/solution.py
@@ -111,23 +111,24 @@
 
 def exponentials(scale, source_ref, half_ref, plan_ref, standing):
     rows, cols = plan_ref.shape
-    highs = []
+    peaks, totals = [], []
     for start in range(0, cols, TILE):
         tile = slice(start, start + TILE)
         part = score(source_ref[...], half_ref[tile, :], scale)
         if standing is not None:
             part = part + spread(standing[...], TILE // LANES)
         plan_ref[:, tile] = part
-        highs.append(jnp.max(part, axis=0, keepdims=True))
-    peak = jnp.concatenate(highs, axis=1)
-    shift = jnp.broadcast_to(peak, (SUBLANES, cols))
-
-    def term(block):
-        value = jnp.exp2(plan_ref[block, :] - shift)
-        plan_ref[block, :] = value
-        return value
-
-    return peak, column_sums(rows, cols, term)
+        peak = jnp.max(part, axis=0, keepdims=True)
+        shift = jnp.broadcast_to(peak, (SUBLANES, TILE))
+        total = jnp.zeros((SUBLANES, TILE), jnp.float32)
+        for row in range(0, rows, SUBLANES):
+            block = slice(row, row + SUBLANES)
+            value = jnp.exp2(plan_ref[block, tile] - shift)
+            plan_ref[block, tile] = value
+            total = total + value
+        peaks.append(peak)
+        totals.append(jnp.sum(total, axis=0, keepdims=True))
+    return jnp.concatenate(peaks, axis=1), jnp.concatenate(totals, axis=1)
 
 
 def first_potential(bits, gathered_ref, mine_ref, away_ref, potential_ref, mine_out, away_out):

time: 128 us -> 128 us (level)
  no operation moved by 1% of the time
where the time goes in v10:
time: 128 us
  blocking collectives  85.1 us (66%)
  Pallas kernels  32.5 us (25%)
  starting transfers between devices  6.29 us (5%)
  local copies, waits for them, and re-layouts  1.53 us (1%)
    all_to_all x4, blocking collectives, local(): columns = lax.all_to_all(parts, PLANE, 0, 0)  46.4 us
    all_to_all x4, blocking collectives, local(): gathered = lax.all_to_all(parts, LINE, 0, 0)  38.7 us
    pallas_call x3, Pallas kernels, local(): pl.pallas_call(lambda *refs: later_rows(scale, row_bits, *refs), in_specs...  13.5 us
    pallas_call x3, Pallas kernels, local(): pl.pallas_call(lambda *refs: later_columns(scale, col_bits, *refs), in_sp...  10.9 us
    ppermute x1, starting transfers between devices, local(): away = lax.ppermute(mine, ('p', 'q'), partner)  3.62 us
  transfers between devices with their start and end apart: 5, of which 2 were waited for; matrix products, arithmetic and copies ran while one was open for 0% of the time, Pallas kernels for 2%

profile of v10, /device:TPU:1, one launch (start us, length us, event | category | flops | bytes accessed | tf_op | source)
XLA Modules:
  0.0 127.9 jit_solution(7620858270229739671)
XLA Ops:
  0.6 1.6 %fetch.1 = (bf16[2048,256]{1,0:T(8,128)(2,1)S(1)}, bf16[2048,256]{1,0:T(8,128)(2,1)S(1)}) custom-call(bf16[4096,256]{1,0:T(8,128)(2,1)} %target_ref.1), custom_call_target="tpu_custom_call" | custom-call | tf_op jit(solution)/shard_map/fetch/pallas_call | solution.py:286
  2.2 0.0 copy-start
  2.2 0.9 copy-done
  3.1 1.6 %first_rows.1 = (f32[8,2,128]{2,1,0:T(2,128)S(1)}, f32[256,256]{1,0:T(8,128)S(1)}) custom-call(bf16[256,256]{1,0:T(8,128)(2,1)S(1)} %copy-done, bf16[2048,256]{1,0:T(8,128)(2,1)S(1)} %get-tuple-element.20.refs_1_.refs_2_, bf16[2048,256]{1,0:T(8,128)(2,1)S(1)} %get-tuple-element.21.refs_2_), custom_call_target="tpu_custom_call" | custom-call | tf_op jit(solution)/shard_map/first_rows/pallas_call | solution.py:295
  4.7 3.6 %collective-permute-start = (f32[256,256]{1,0:T(8,128)S(1)}, f32[256,256]{1,0:T(8,128)S(1)}, u32[]{:S(2)}, u32[]{:S(2)}) collective-permute-start(f32[256,256]{1,0:T(8,128)S(1)} %get-tuple-element.23.refs_1_), channel_id=1, source_target_pairs={{0,24},{24,0},{8,16},{16,8},{1,25},{25,1},{9,17},{17,9},{2,26},{26... | collective-permute-start | bytes 786440 | tf_op jit(solution)/shard_map/ppermute | solution.py:311
  8.3 9.9 %all_to_all.40.refs_0_ = f32[8,2,128]{2,1,0:T(2,128)S(1)} all-to-all(f32[8,2,128]{2,1,0:T(2,128)S(1)} %get-tuple-element.22), channel_id=1, replica_groups=mesh['z'=8,'p'=2,'q'=2,'core'=2,'x'=4] {'core','x'}, dimensions={0} | all-to-all | bytes 16384 | tf_op jit(solution)/shard_map/all_to_all | solution.py:312
  18.2 0.0 collective-permute-done.refs_2_
  18.2 0.1 first_potential.1
  18.3 0.5 collective-permute-start.3
  18.8 0.1 collective-permute-start.1
  18.9 0.0 collective-permute-start.2
  18.9 1.0 collective-permute-done.3.refs_1_
  19.9 1.3 %partner_rows.1 = (f32[512,2048]{1,0:T(8,128)S(1)}, f32[4,128]{1,0:T(4,128)S(1)}, f32[16,128]{1,0:T(8,128)S(1)}, bf16[512,256]{1,0:T(8,128)(2,1)S(1)}) custom-call(f32[256,256]{1,0:T(8,128)S(1)} %get-tuple-element.27.refs_0_, f32[256,256]{1,0:T(8,128)S(1)} %collective-permute-done.3.refs_1_, bf16[2048,256]{1,0:T(8,128)(2,1)S(1)} %get-tuple-element.20.refs_1_.refs_2_), custom_call_target="tpu_custom_call" | custom-call | tf_op jit(solution)/shard_map/partner_rows/pallas_call | solution.py:332
  21.3 0.0 collective-permute-done.1.refs_1_
  21.3 1.5 %first_columns.1 = (f32[16,128]{1,0:T(8,128)S(1)}, f32[512,2048]{1,0:T(8,128)S(1)}, f32[4,128]{1,0:T(4,128)S(1)}, f32[16,128]{1,0:T(8,128)S(1)}, bf16[512,256]{1,0:T(8,128)(2,1)S(1)}) custom-call(f32[256,256]{1,0:T(8,128)S(1)} %get-tuple-element.24.refs_0_, f32[256,256]{1,0:T(8,128)S(1)} %collective-permute-done.1.refs_1_, ...), custom_call_target="tpu_custom_call" | custom-call | tf_op jit(solution)/shard_map/first_columns/pallas_call | solution.py:323
  22.8 0.0 collective-permute-done.2.refs_1_
  22.8 2.1 %partner_columns.1 = f32[16,16,128]{2,1,0:T(8,128)S(1)} custom-call(f32[16,128]{1,0:T(8,128)S(1)} %get-tuple-element.26.refs_0_, f32[4,128]{1,0:T(4,128)S(1)} %collective-permute-done.2.refs_1_, bf16[2048,256]{1,0:T(8,128)(2,1)S(1)} %get-tuple-element.20.refs_1_.refs_2_, f32[512,2048]{1,0:T(8,128)S(1)} %get-tuple-element.28.refs_3_.refs_6_, ...), custom_call_target="tpu_custom_call" | custom-call | tf_op jit(solution)/shard_map/partner_columns/pallas_call | solution.py:342
  24.8 15.5 %all_to_all.41.refs_0_ = f32[16,16,128]{2,1,0:T(8,128)S(1)} all-to-all(f32[16,16,128]{2,1,0:T(8,128)S(1)} %partner_columns.1), channel_id=1, replica_groups=mesh['z'=8,'p'=2,'q'=2,'core'=2,'x'=4] {'q','z'}, dimensions={0} | all-to-all | bytes 262144 | tf_op jit(solution)/shard_map/all_to_all | solution.py:351
  40.3 4.4 %later_rows.3 = f32[8,8,128]{2,1,0:T(8,128)S(1)} custom-call(f32[16,16,128]{2,1,0:T(8,128)S(1)} %all_to_all.41.refs_0_, bf16[2048,256]{1,0:T(8,128)(2,1)S(1)} %get-tuple-element.20.refs_1_.refs_2_, f32[512,2048]{1,0:T(8,128)S(1)} %get-tuple-element.32.refs_2_, f32[4,128]{1,0:T(4,128)S(1)} %get-tuple-element.33.refs_3_, ...), custom_call_target="tpu_custom_call" | custom-call | tf_op jit(solution)/shard_map/later_rows/pallas_call | solution.py:354
  44.8 10.2 %all_to_all.42.refs_0_ = f32[8,8,128]{2,1,0:T(8,128)S(1)} all-to-all(f32[8,8,128]{2,1,0:T(8,128)S(1)} %later_rows.3), channel_id=1, replica_groups=mesh['z'=8,'p'=2,'q'=2,'core'=2,'x'=4] {'core','x'}, dimensions={0} | all-to-all | bytes 65536 | tf_op jit(solution)/shard_map/all_to_all | solution.py:363
  55.0 3.6 %later_columns.3 = f32[16,16,128]{2,1,0:T(8,128)S(1)} custom-call(f32[8,8,128]{2,1,0:T(8,128)S(1)} %all_to_all.42.refs_0_, bf16[2048,256]{1,0:T(8,128)(2,1)S(1)} %get-tuple-element.20.refs_1_.refs_2_, f32[512,2048]{1,0:T(8,128)S(1)} %get-tuple-element.32.refs_2_, f32[4,128]{1,0:T(4,128)S(1)} %get-tuple-element.33.refs_3_, ...), custom_call_target="tpu_custom_call" | custom-call | tf_op jit(solution)/shard_map/later_columns/pallas_call | solution.py:364
  58.6 10.2 %all_to_all.43.refs_0_ = f32[16,16,128]{2,1,0:T(8,128)S(1)} all-to-all(f32[16,16,128]{2,1,0:T(8,128)S(1)} %later_columns.3), channel_id=1, replica_groups=mesh['z'=8,'p'=2,'q'=2,'core'=2,'x'=4] {'q','z'}, dimensions={0} | all-to-all | bytes 262144 | tf_op jit(solution)/shard_map/all_to_all | solution.py:373
  68.8 4.4 %later_rows.4 = f32[8,8,128]{2,1,0:T(8,128)S(1)} custom-call(f32[16,16,128]{2,1,0:T(8,128)S(1)} %all_to_all.43.refs_0_, bf16[2048,256]{1,0:T(8,128)(2,1)S(1)} %get-tuple-element.20.refs_1_.refs_2_, f32[512,2048]{1,0:T(8,128)S(1)} %get-tuple-element.32.refs_2_, f32[4,128]{1,0:T(4,128)S(1)} %get-tuple-element.33.refs_3_, ...), custom_call_target="tpu_custom_call" | custom-call | tf_op jit(solution)/shard_map/later_rows/pallas_call | solution.py:354
  73.3 9.3 %all_to_all.44.refs_0_ = f32[8,8,128]{2,1,0:T(8,128)S(1)} all-to-all(f32[8,8,128]{2,1,0:T(8,128)S(1)} %later_rows.4), channel_id=1, replica_groups=mesh['z'=8,'p'=2,'q'=2,'core'=2,'x'=4] {'core','x'}, dimensions={0} | all-to-all | bytes 65536 | tf_op jit(solution)/shard_map/all_to_all | solution.py:363
  82.6 3.6 %later_columns.4 = f32[16,16,128]{2,1,0:T(8,128)S(1)} custom-call(f32[8,8,128]{2,1,0:T(8,128)S(1)} %all_to_all.44.refs_0_, bf16[2048,256]{1,0:T(8,128)(2,1)S(1)} %get-tuple-element.20.refs_1_.refs_2_, f32[512,2048]{1,0:T(8,128)S(1)} %get-tuple-element.32.refs_2_, f32[4,128]{1,0:T(4,128)S(1)} %get-tuple-element.33.refs_3_, ...), custom_call_target="tpu_custom_call" | custom-call | tf_op jit(solution)/shard_map/later_columns/pallas_call | solution.py:364
  86.2 10.3 %all_to_all.45.refs_0_ = f32[16,16,128]{2,1,0:T(8,128)S(1)} all-to-all(f32[16,16,128]{2,1,0:T(8,128)S(1)} %later_columns.4), channel_id=1, replica_groups=mesh['z'=8,'p'=2,'q'=2,'core'=2,'x'=4] {'q','z'}, dimensions={0} | all-to-all | bytes 262144 | tf_op jit(solution)/shard_map/all_to_all | solution.py:373
  96.5 4.6 %later_rows.5 = f32[8,8,128]{2,1,0:T(8,128)S(1)} custom-call(f32[16,16,128]{2,1,0:T(8,128)S(1)} %all_to_all.45.refs_0_, bf16[2048,256]{1,0:T(8,128)(2,1)S(1)} %get-tuple-element.20.refs_1_.refs_2_, f32[512,2048]{1,0:T(8,128)S(1)} %get-tuple-element.32.refs_2_, f32[4,128]{1,0:T(4,128)S(1)} %get-tuple-element.33.refs_3_, ...), custom_call_target="tpu_custom_call" | custom-call | tf_op jit(solution)/shard_map/later_rows/pallas_call | solution.py:354
  101.2 9.3 %all_to_all.46.refs_0_ = f32[8,8,128]{2,1,0:T(8,128)S(1)} all-to-all(f32[8,8,128]{2,1,0:T(8,128)S(1)} %later_rows.5), channel_id=1, replica_groups=mesh['z'=8,'p'=2,'q'=2,'core'=2,'x'=4] {'core','x'}, dimensions={0} | all-to-all | bytes 65536 | tf_op jit(solution)/shard_map/all_to_all | solution.py:363
  110.4 3.6 %later_columns.5 = f32[16,16,128]{2,1,0:T(8,128)S(1)} custom-call(f32[8,8,128]{2,1,0:T(8,128)S(1)} %all_to_all.46.refs_0_, bf16[2048,256]{1,0:T(8,128)(2,1)S(1)} %get-tuple-element.20.refs_1_.refs_2_, f32[512,2048]{1,0:T(8,128)S(1)} %get-tuple-element.32.refs_2_, f32[4,128]{1,0:T(4,128)S(1)} %get-tuple-element.33.refs_3_, ...), custom_call_target="tpu_custom_call" | custom-call | tf_op jit(solution)/shard_map/later_columns/pallas_call | solution.py:364
  114.1 10.3 %all_to_all.47.refs_1_ = f32[16,16,128]{2,1,0:T(8,128)S(1)} all-to-all(f32[16,16,128]{2,1,0:T(8,128)S(1)} %later_columns.5), channel_id=1, replica_groups=mesh['z'=8,'p'=2,'q'=2,'core'=2,'x'=4] {'q','z'}, dimensions={0} | all-to-all | bytes 262144 | tf_op jit(solution)/shard_map/all_to_all | solution.py:373
  124.4 2.1 %collective-permute-start.4 = (f32[2048]{0:T(1024)S(1)}, f32[2048]{0:T(1024)S(1)}, u32[]{:S(2)}, u32[]{:S(2)}) collective-permute-start(f32[2048]{0:T(1024)S(1)} %bitcast.2), channel_id=1, source_target_pairs={{0,4},{4,0},{1,5},{5,1},{2,6},{6,2},{3,7},{7,3},{8,12},{12,8},{9,1... | collective-permute-start | bytes 24584 | tf_op jit(solution)/shard_map/ppermute | solution.py:384
  126.5 0.6 dynamic_slice.3
  127.1 0.2 collective-permute-done.4
  127.3 0.6 maximum_select_fusion
  (1 shorter events, 0.0 us)
Async XLA Ops:
  2.2 0.9 copy-start
  4.7 13.5 %collective-permute-start = (f32[256,256]{1,0:T(8,128)S(1)}, f32[256,256]{1,0:T(8,128)S(1)}, u32[]{:S(2)}, u32[]{:S(2)}) collective-permute-start(f32[256,256]{1,0:T(8,128)S(1)} %get-tuple-element.23.refs_1_), channel_id=1, source_target_pairs={{0,24},{24,0},{8,16},{16,8},{1,25},{25,1},{9,17},{17,9},{2,26},{26... | collective-permute-start | bytes 786440 | tf_op jit(solution)/shard_map/ppermute | solution.py:311
  18.3 1.6 %collective-permute-start.3 = (f32[256,256]{1,0:T(8,128)S(1)}, f32[256,256]{1,0:T(8,128)S(1)}, u32[]{:S(2)}, u32[]{:S(2)}) collective-permute-start(f32[256,256]{1,0:T(8,128)S(1)} %get-tuple-element.27.refs_0_), channel_id=1, source_target_pairs={{0,4},{4,0},{1,5},{5,1},{2,6},{6,2},{3,7},{7,3},{8,12},{12,8},{9,1... | collective-permute-start | bytes 786440 | tf_op jit(solution)/shard_map/ppermute | solution.py:339
  18.8 2.5 %collective-permute-start.1 = (f32[256,256]{1,0:T(8,128)S(1)}, f32[256,256]{1,0:T(8,128)S(1)}, u32[]{:S(2)}, u32[]{:S(2)}) collective-permute-start(f32[256,256]{1,0:T(8,128)S(1)} %get-tuple-element.24.refs_0_), channel_id=1, source_target_pairs={{0,4},{4,0},{1,5},{5,1},{2,6},{6,2},{3,7},{7,3},{8,12},{12,8},{9,1... | collective-permute-start | bytes 786440 | tf_op jit(solution)/shard_map/ppermute | solution.py:321
  18.9 3.9 %collective-permute-start.2 = (f32[4,128]{1,0:T(4,128)S(1)}, f32[4,128]{1,0:T(4,128)S(1)}, u32[]{:S(2)}, u32[]{:S(2)}) collective-permute-start(f32[4,128]{1,0:T(4,128)S(1)} %get-tuple-element.25.refs_3_), channel_id=1, source_target_pairs={{0,24},{24,0},{8,16},{16,8},{1,25},{25,1},{9,17},{17,9},{2,26},{26... | collective-permute-start | bytes 6152 | tf_op jit(solution)/shard_map/ppermute | solution.py:322
  124.4 2.9 %collective-permute-start.4 = (f32[2048]{0:T(1024)S(1)}, f32[2048]{0:T(1024)S(1)}, u32[]{:S(2)}, u32[]{:S(2)}) collective-permute-start(f32[2048]{0:T(1024)S(1)} %bitcast.2), channel_id=1, source_target_pairs={{0,4},{4,0},{1,5},{5,1},{2,6},{6,2},{3,7},{7,3},{8,12},{12,8},{9,1... | collective-permute-start | bytes 24584 | tf_op jit(solution)/shard_map/ppermute | solution.py:384
